TPU v7x, 32 devices: a whole 2x2x4 slice. The times are simulated.
32 devices in a mesh: batch: 8 (over y, x, core), head: 4 (over z).
Axes of the slice: x: 2, y: 2, z: 4, core: 2. Of those that a mesh axis runs over, the one named last changes fastest.
Arguments:
- hidden_in: bfloat16 [16384, 2048], P(('batch', 'head')), may hold values from -6 to 6
- out_grad: bfloat16 [16384, 2048], P(('batch', 'head')), may hold values from -6 to 6
- norm_gain: float32 [2048], replicated, may hold values from 0.1 to 1.9
- w_z: bfloat16 [2048, 4096], P(None, 'head'), may hold values from -0.125 to 0.125
- w_x: bfloat16 [2048, 4096], P(None, 'head'), may hold values from -0.125 to 0.125
- w_dt: bfloat16 [2048, 64], P(None, 'head'), may hold values from -0.125 to 0.125
- w_bc: bfloat16 [2048, 256], replicated, may hold values from -0.046875 to 0.046875
- conv_x: float32 [4, 4096], P(None, 'head'), may hold values from -3 to 3
- conv_x_bias: float32 [4096], P('head'), may hold values from -3 to 3
- conv_bc: float32 [4, 256], replicated, may hold values from -3 to 3
- conv_bc_bias: float32 [256], replicated, may hold values from -0.6 to 0.6
- dt_bias: float32 [64], P('head'), may hold values from -4 to -1
- a_log: float32 [64], P('head'), may hold values from -6.2 to -1.2
- d_skip: float32 [64], P('head'), may hold values from 0.5 to 1.5
- gate_gain: float32 [4096], P('head'), may hold values from 0.1 to 1.9
- w_out: bfloat16 [4096, 2048], P('head'), may hold values from -0.1875 to 0.1875
- doc_lengths: int32 [16, 4], P('batch'), may hold values from 1 to 512, 1024 in all within a row
- widths: int32 [16], P('batch'), may hold values from 8 to 64, as said below
Outputs:
- mixed: bfloat16 [16384, 2048], P(('batch', 'head'))
- in_grad: bfloat16 [16384, 2048], P(('batch', 'head'))
- g_norm_gain: float32 [2048], replicated
- g_w_z: float32 [2048, 4096], P(None, 'head')
- g_w_x: float32 [2048, 4096], P(None, 'head')
- g_w_dt: float32 [2048, 64], P(None, 'head')
- g_w_bc: float32 [2048, 256], replicated
- g_conv_x: float32 [4, 4096], P(None, 'head')
- g_conv_x_bias: float32 [4096], P('head')
- g_conv_bc: float32 [4, 256], replicated
- g_conv_bc_bias: float32 [256], replicated
- g_dt_bias: float32 [64], P('head')
- g_a_log: float32 [64], P('head')
- g_d_skip: float32 [64], P('head')
- g_gate_gain: float32 [4096], P('head')
- g_w_out: float32 [4096, 2048], P('head')
Inputs may be any that keep to these rules, and one draw needn't show every extreme that they name: `doc_lengths`: each row sums to 1024. `widths`: each entry is 64, 32, 16 or 8; every draw has a sequence of 64 and one of 8.
All inputs are finite; a program needn't handle non-finite values.
Results may differ from a plain program's by a relative error of at most 0.018.
Values may be sent and summed in bfloat16 or wider, within the bound.
No kernel may reach another device: no remote copies, remote signals or barrier semaphores. Data moves between devices by JAX's collectives and lax.ppermute only.
A program may use at most 256 MiB of HBM per device.

v0:
```python
import jax
import jax.numpy as jnp
from jax import lax
from jax.sharding import PartitionSpec as P

HEADS = 64
HEAD_DIM = 64
STATE = 128
CONV = 4
SPAN = 256
SEQ_LEN = 1024
DOCS = 4


EPSILON = 1e-05
HIGHEST = lax.Precision.HIGHEST


def rounded_copy(values):
    return lax.optimization_barrier(values.astype(jnp.bfloat16)).astype(jnp.float32)


def shifted(values, lag_rows, fill):
    padding = jnp.full((lag_rows,) + values.shape[1:], fill, values.dtype)
    return jnp.concatenate([padding, values[: values.shape[0] - lag_rows]], axis=0)


def convolve(values, taps, offset_bias, doc_ids):
    result = offset_bias + taps[0] * values
    for lag_rows in range(1, CONV):
        same = (shifted(doc_ids, lag_rows, -1) == doc_ids).astype(jnp.float32)[:, None]
        result = result + taps[lag_rows] * shifted(values, lag_rows, 0.0) * same
    return result


def block_step(carry_pair, inputs):
    state_now, last_doc = carry_pair
    x_block, b_block, c_block, d_block, s_block, doc_block = inputs
    cum_decay = jnp.cumsum(d_block, axis=0)
    head_cum = cum_decay.T
    offsets = jnp.arange(SPAN)
    inside = (doc_block[:, None] == doc_block[None, :]) & (offsets[:, None] >= offsets[None, :])
    gap_decay = head_cum[:, :, None] - head_cum[:, None, :]
    decays = jnp.exp(jnp.where(inside[None, :, :], gap_decay, -1e30))
    scores = jnp.dot(
        c_block.astype(jnp.bfloat16),
        b_block.astype(jnp.bfloat16).T,
        preferred_element_type=jnp.float32,
    )
    mixing = decays * scores[None, :, :] * s_block.T[:, None, :]
    local_out = jnp.einsum("hij,jhp->ihp", mixing, x_block, precision=HIGHEST)
    entry_decay = jnp.exp(cum_decay) * (doc_block == last_doc).astype(jnp.float32)[:, None]
    carried = (
        jnp.einsum("in,hpn->ihp", c_block, state_now, precision=HIGHEST) * entry_decay[:, :, None]
    )
    tail_weight = (
        jnp.exp(cum_decay[-1][None, :] - cum_decay)
        * (doc_block == doc_block[-1]).astype(jnp.float32)[:, None]
        * s_block
    )
    weighted = x_block * tail_weight[:, :, None]
    fresh_state = jnp.einsum("jhp,jn->hpn", weighted, b_block, precision=HIGHEST)
    keep_decay = jnp.exp(cum_decay[-1]) * (doc_block[-1] == last_doc).astype(jnp.float32)
    state_now = state_now * keep_decay[:, None, None] + fresh_state
    return ((state_now, doc_block[-1]), local_out + carried)


def ssd_scan(values, b_rows, c_rows, decay, step_sizes, doc_ids):
    row_total, head_count, channels = values.shape
    blocks = row_total // SPAN
    inputs = (
        values.reshape(blocks, SPAN, head_count, channels),
        b_rows.reshape(blocks, SPAN, STATE),
        c_rows.reshape(blocks, SPAN, STATE),
        decay.reshape(blocks, SPAN, head_count),
        step_sizes.reshape(blocks, SPAN, head_count),
        doc_ids.reshape(blocks, SPAN),
    )
    start = (jnp.zeros((head_count, channels, STATE), jnp.float32), jnp.int32(-1))
    ending, outputs = lax.scan(jax.checkpoint(block_step), start, inputs)
    return outputs.reshape(row_total, head_count, channels)


def rows_product(left, right):
    return lax.dot_general(
        left, right, (((0,), (0,)), ((), ())), preferred_element_type=jnp.float32
    )


def cols_product(left, right):
    return lax.dot_general(
        left, right, (((1,), (1,)), ((), ())), preferred_element_type=jnp.float32
    )


def body(
    hidden_in,
    out_grad,
    norm_gain,
    w_z,
    w_x,
    w_dt,
    w_bc,
    conv_x,
    conv_x_bias,
    conv_bc,
    conv_bc_bias,
    dt_bias,
    a_log,
    d_skip,
    gate_gain,
    w_out,
    doc_lengths,
    widths,
):
    shard_rows = hidden_in.shape[0]
    heads_here = dt_bias.shape[0]
    seqs_here = widths.shape[0]
    residual = hidden_in.astype(jnp.float32)
    inverse = lax.rsqrt(jnp.mean(residual * residual, axis=-1, keepdims=True) + EPSILON)
    unit_rows = residual * inverse
    normed = (unit_rows * norm_gain).astype(jnp.bfloat16)
    gathered = lax.all_gather(normed, "head", axis=0, tiled=True)
    gate_cols = jnp.dot(gathered, w_z, preferred_element_type=jnp.float32)
    inner_cols = jnp.dot(gathered, w_x, preferred_element_type=jnp.float32)
    pair_cols = jnp.dot(gathered, w_bc, preferred_element_type=jnp.float32)
    rate_cols = jnp.dot(gathered, w_dt, preferred_element_type=jnp.float32)
    positions = jnp.arange(SEQ_LEN)
    doc_ends = jnp.cumsum(doc_lengths, axis=1)
    doc_local = jnp.sum(
        (positions[None, :, None] >= doc_ends[:, None, :]).astype(jnp.int32), axis=2
    )
    doc_ids = (doc_local + DOCS * jnp.arange(seqs_here)[:, None]).reshape(-1)

    def conv_part(inner_in, pair_in, taps_x, bias_x, taps_bc, bias_bc):
        return (
            jax.nn.silu(convolve(inner_in, taps_x, bias_x, doc_ids)),
            jax.nn.silu(convolve(pair_in, taps_bc, bias_bc, doc_ids)),
        )

    def scan_part(mixed_x, mixed_bc, rate_in, step_bias, log_rates, skip_weight):
        step_sizes = jax.nn.softplus(rate_in + step_bias)
        decay = -step_sizes * jnp.exp(log_rates)
        values = mixed_x.reshape(mixed_x.shape[0], heads_here, HEAD_DIM)
        scanned_out = ssd_scan(
            values, mixed_bc[:, :STATE], mixed_bc[:, STATE:], decay, step_sizes, doc_ids
        )
        return scanned_out + skip_weight[None, :, None] * values

    conv_outs, pull_conv = jax.vjp(
        conv_part, inner_cols, pair_cols, conv_x, conv_x_bias, conv_bc, conv_bc_bias
    )
    mixed_x_low = rounded_copy(conv_outs[0])
    mixed_bc_low = rounded_copy(conv_outs[1])
    scanned, pull_scan = jax.vjp(
        scan_part, mixed_x_low, mixed_bc_low, rate_cols, dt_bias, a_log, d_skip
    )
    active = (jnp.arange(heads_here)[None, :] < (widths * heads_here // HEADS)[:, None]).astype(
        jnp.float32
    )
    row_active = jnp.broadcast_to(active[:, None, :], (seqs_here, SEQ_LEN, heads_here)).reshape(
        -1, heads_here
    )
    row_count = jnp.broadcast_to(
        (widths * HEAD_DIM).astype(jnp.float32)[:, None], (seqs_here, SEQ_LEN)
    ).reshape(-1, 1)
    masked = (scanned * row_active[:, :, None]).reshape(scanned.shape[0], -1)
    switch = jax.nn.silu(gate_cols)
    gated = masked * switch
    square_sum = lax.psum(jnp.sum(gated * gated, axis=-1, keepdims=True), "head")
    scale_rows = lax.rsqrt(square_sum / row_count + EPSILON)
    scaled = gated * scale_rows
    normed_y = (scaled * gate_gain).astype(jnp.bfloat16)
    branch = lax.psum_scatter(
        jnp.dot(normed_y, w_out, preferred_element_type=jnp.float32).astype(jnp.bfloat16),
        "head",
        scatter_dimension=0,
        tiled=True,
    ).astype(jnp.float32)
    mixed = (residual + branch).astype(jnp.bfloat16)
    upstream = lax.all_gather(out_grad, "head", axis=0, tiled=True)
    g_w_out = rows_product(normed_y, upstream)
    d_normed = cols_product(upstream, w_out)
    g_gate_gain = jnp.sum(d_normed * scaled, axis=0)
    d_scaled = d_normed * gate_gain
    inner_sum = lax.psum(jnp.sum(d_scaled * gated, axis=-1, keepdims=True), "head")
    d_gated = (
        d_scaled * scale_rows
        - gated * (scale_rows * scale_rows * scale_rows) * inner_sum / row_count
    )
    sigma_gate = jax.nn.sigmoid(gate_cols)
    d_gate = (d_gated * masked * sigma_gate * (1.0 + gate_cols * (1.0 - sigma_gate))).astype(
        jnp.bfloat16
    )
    d_masked = (d_gated * switch).reshape(scanned.shape) * row_active[:, :, None]
    scan_grads = pull_scan(d_masked)
    conv_grads = pull_conv((scan_grads[0], scan_grads[1]))
    core_grads = (
        conv_grads[0],
        conv_grads[1],
        scan_grads[2],
        conv_grads[2],
        conv_grads[3],
        conv_grads[4],
        conv_grads[5],
        scan_grads[3],
        scan_grads[4],
        scan_grads[5],
    )
    d_inner = core_grads[0].astype(jnp.bfloat16)
    d_rates = core_grads[2].astype(jnp.bfloat16)
    pair_sum, g_conv_bc, g_conv_bc_bias = (
        lax.psum(core_grads[1].astype(jnp.bfloat16), "head").astype(jnp.float32),
        lax.psum(core_grads[5].astype(jnp.bfloat16), "head").astype(jnp.float32),
        lax.psum(core_grads[6].astype(jnp.bfloat16), "head").astype(jnp.float32),
    )
    d_pairs = pair_sum.astype(jnp.bfloat16)
    g_w_z = rows_product(gathered, d_gate)
    g_w_x = rows_product(gathered, d_inner)
    g_w_dt = rows_product(gathered, d_rates)
    d_normed_in = lax.psum_scatter(
        (
            cols_product(d_gate, w_z) + cols_product(d_inner, w_x) + cols_product(d_rates, w_dt)
        ).astype(jnp.bfloat16),
        "head",
        scatter_dimension=0,
        tiled=True,
    ).astype(jnp.float32)
    own_start = lax.axis_index("head") * shard_rows
    own_pairs = lax.dynamic_slice_in_dim(d_pairs, own_start, shard_rows, 0)
    d_normed_in = d_normed_in + cols_product(own_pairs, w_bc)
    g_norm_gain = jnp.sum(d_normed_in * unit_rows, axis=0)
    d_unit = d_normed_in * norm_gain
    d_residual = inverse * (
        d_unit - unit_rows * jnp.mean(d_unit * unit_rows, axis=-1, keepdims=True)
    )
    in_grad = (out_grad.astype(jnp.float32) + d_residual).astype(jnp.bfloat16)
    g_w_bc_local = rows_product(gathered, d_pairs)
    summed = (
        lax.psum(g_w_z.astype(jnp.bfloat16), "batch").astype(jnp.float32),
        lax.psum(g_w_x.astype(jnp.bfloat16), "batch").astype(jnp.float32),
        lax.psum(g_w_dt.astype(jnp.bfloat16), "batch").astype(jnp.float32),
        lax.psum(g_w_bc_local.astype(jnp.bfloat16), "batch").astype(jnp.float32),
        lax.psum(core_grads[3].astype(jnp.bfloat16), "batch").astype(jnp.float32),
        lax.psum(core_grads[4].astype(jnp.bfloat16), "batch").astype(jnp.float32),
        lax.psum(g_conv_bc.astype(jnp.bfloat16), "batch").astype(jnp.float32),
        lax.psum(g_conv_bc_bias.astype(jnp.bfloat16), "batch").astype(jnp.float32),
        lax.psum(core_grads[7].astype(jnp.bfloat16), "batch").astype(jnp.float32),
        lax.psum(core_grads[8].astype(jnp.bfloat16), "batch").astype(jnp.float32),
        lax.psum(core_grads[9].astype(jnp.bfloat16), "batch").astype(jnp.float32),
        lax.psum(g_gate_gain.astype(jnp.bfloat16), "batch").astype(jnp.float32),
        lax.psum(g_w_out.astype(jnp.bfloat16), "batch").astype(jnp.float32),
    )
    gain_total = lax.psum((g_norm_gain,), ("batch", "head"))
    g_norm_total = gain_total[0]
    g_w_bc = summed[3]
    rest = (
        summed[0],
        summed[1],
        summed[2],
        summed[4],
        summed[5],
        summed[6],
        summed[7],
        summed[8],
        summed[9],
        summed[10],
        summed[11],
        summed[12],
    )
    return (
        mixed,
        in_grad,
        g_norm_total,
        rest[0],
        rest[1],
        rest[2],
        g_w_bc,
        rest[3],
        rest[4],
        rest[5],
        rest[6],
        rest[7],
        rest[8],
        rest[9],
        rest[10],
        rest[11],
    )


def solution(mesh):
    return jax.shard_map(
        body,
        mesh=mesh,
        in_specs=(
            P(("batch", "head"), None),
            P(("batch", "head"), None),
            P(),
            P(None, "head"),
            P(None, "head"),
            P(None, "head"),
            P(),
            P(None, "head"),
            P("head"),
            P(),
            P(),
            P("head"),
            P("head"),
            P("head"),
            P("head"),
            P("head", None),
            P("batch", None),
            P("batch"),
        ),
        out_specs=(
            P(("batch", "head"), None),
            P(("batch", "head"), None),
            P(),
            P(None, "head"),
            P(None, "head"),
            P(None, "head"),
            P(),
            P(None, "head"),
            P("head"),
            P(),
            P(),
            P("head"),
            P("head"),
            P("head"),
            P("head"),
            P("head", None),
        ),
        check_vma=False,
    )
```

profile of v0, /device:TPU:0, one launch (start us, length us, event | category | flops | bytes accessed | tf_op | source)
XLA Modules:
  0.0 1693.8 jit_solution(5550940634796316247)
XLA Ops:
  31.0 135.0 %all-gather.3.cloned.1.call-done = bf16[2048,2048]{1,0:T(8,128)(2,1)} async-done(((bf16[512,2048]{1,0:T(8,128)(2,1)}), bf16[2048,2048]{1,0:T(8,128)(2,1)}) %all-gather.3.cloned.1.call-update) | async-done | bytes 8388624 | tf_op jit(solution)/shard_map/all_gather | solution.py:123
  201.3 14.0 copy.121
  234.7 170.1 %while.45 = (s32[]{:T(128)}, f32[16,64,128]{2,1,0:T(8,128)S(1)}, s32[]{:T(128)}, f32[8,256,16,64]{1,3,2,0:T(8,128)}, f32[8,16,64,128]{3,2,1,0:T(8,128)}, /*index...) while((s32[]{:T(128)}, f32[16,64,128]{2,1,0:T(8,128)S(1)}, ...), condition=%wide.region_6.7_spmd.clone, body=%wide.region_3.6_spmd.clone.sunk | while | flops 1633768448 | bytes 9221823 | solution.py:80
  404.8 14.5 copy.138
  419.3 14.5 reshape.583
  433.8 22.5 %multiply_reduce_fusion.11 = (f32[2048]{0:T(1024)S(1)}, f32[2048,1024]{1,0:T(8,128)}, f32[2048,1024]{1,0:T(8,128)}) fusion(f32[2048,1024]{1,0:T(8,128)} %copy.126, f32[2048,1024]{1,0:T(8,128)} %reshape.583, bf16[2048,1024]{1,0:T(8,128)(2,1)} %get-tuple-element.784, f32[1024]{0:T(1024)S(1)} %mul.1002, bf16[2048,2048]{1,0:T(8,128)(2,1)} %all-gather.3.cloned.1.call-done, ...), kind=kOutput, calls=%fused_computation.169 | convolution fusion | flops 8613001216 | bytes 50343936 | tf_op jit(solution)/shard_map/dot_general | solution.py:124
  465.2 18.4 %multiply_reduce_fusion.4 = (bf16[1024]{0:T(1024)(128)(2,1)}, f32[2048]{0:T(1024)S(1)}, f32[2048,1024]{1,0:T(8,128)}) fusion(f32[2048,1024]{1,0:T(8,128)} %get-tuple-element.781, f32[2048]{0:T(1024)S(1)} %bitcast.495, f32[1024]{0:T(1024)S(1)} %copy-done.78, bf16[2048,2048]{1,0:T(8,128)(2,1)} %all-gather.5.cloned.1.call-done, bf16[1024,2048]{1,0:T(8,128)(2,1)} %param.37), kind=kOutput, calls=%fused_computation.158 | convolution fusion | flops 8602514432 | bytes 29382656 | tf_op jit(solution)/shard_map/dot_general | solution.py:91
  493.9 21.7 %multiply_reduce_fusion.5 = (f32[1024]{0:T(1024)}, f32[2048,1024]{1,0:T(8,128)}, bf16[2048,1024]{1,0:T(8,128)(2,1)}) fusion(bf16[2048,1024]{1,0:T(8,128)(2,1)} %get-tuple-element.784, f32[2048,1024]{1,0:T(8,128)} %copy.126, f32[2048,1024]{1,0:T(8,128)} %get-tuple-element.841, f32[2048]{0:T(1024)S(1)} %bitcast.494, f32[2048]{0:T(1024)S(1)} %psum.134, ...), kind=kLoop, calls=%fused_computation.159 | loop fusion | flops 52427776 | bytes 58765312 | tf_op jit(solution)/shard_map/transpose(jvp())/reduce_sum | solution.py:148
  544.2 494.1 %while.46 = (s32[]{:T(128)}, f32[16,64,128]{2,1,0:T(8,128)}, f32[8,256,16,64]{1,3,2,0:T(8,128)}, f32[8,256,128]{2,1,0:T(8,128)}, f32[8,256,128]{2,1,0:T(8,128)},...) while((s32[]{:T(128)}, f32[16,64,128]{2,1,0:T(8,128)}, ...), condition=%wide.region_25.26_spmd.clone, body=%wide.region_12.25_spmd.clone.sunk | while | flops 3696575488 | bytes 31303708 | solution.py:80
  1048.8 14.5 copy.139
  1063.3 14.5 reshape.584
  1077.8 19.8 %multiply_reduce_fusion.9 = (f32[1024]{0:T(1024)}, f32[2048,1024]{1,0:T(8,128)}, f32[2048,1024]{1,0:T(8,128)S(1)}) fusion(f32[2045,1024]{1,0:T(8,128)} %bitcast.446, f32[2048]{0:T(1024)S(1)} %copy-done.37, f32[2048,1024]{1,0:T(8,128)} %get-tuple-element.785, f32[2048,1024]{1,0:T(8,128)} %reshape.584, f32[2048,1024]{1,0:T(8,128)} %get-tuple-element.761, ...), kind=kLoop, calls=%fused_computation.163 | loop fusion | flops 31456256 | bytes 58724352 | tf_op jit(solution)/shard_map/transpose(jvp())/reduce_sum | solution.py:32
  1097.6 14.7 multiply_reduce_fusion.8
  1134.1 16.3 fusion.133
  1150.4 17.2 %convolution_convert_fusion.3 = bf16[1024,2048]{1,0:T(8,128)(2,1)} fusion(bf16[2048,2048]{1,0:T(8,128)(2,1)} %all-gather.5.cloned.1.call-done, f32[2048,1024]{1,0:T(8,128)} %get-tuple-element.781, f32[1024]{0:T(1024)S(1)} %copy-done.79, f32[2048]{0:T(1024)S(1)} %bitcast.497), kind=kOutput, calls=%fused_computation.199 | convolution fusion | flops 8598323200 | bytes 20983808 | tf_op jit(solution)/shard_map/dot_general | solution.py:85
  1167.6 13.0 convolution_convert_fusion.4
  1200.9 15.9 fusion.147
  1228.5 17.3 %add_convert_fusion = bf16[2048,2048]{1,0:T(8,128)(2,1)} fusion(f32[2048,2048]{1,0:T(8,128)} %fusion.146, f32[2048,2048]{1,0:T(8,128)} %fusion.147, bf16[2048,16]{0,1:T(8,128)(2,1)S(1)} %copy-done.34, bf16[2048,16]{0,1:T(8,128)(2,1)S(1)} %get-tuple-element.763), kind=kOutput, calls=%fused_computation.151 | convolution fusion | flops 146800640 | bytes 42074112 | tf_op jit(solution)/shard_map/dot_general | solution.py:91
  1245.9 14.7 convolution_convert_fusion.2
  1270.0 23.3 %all-reduce.26 = (bf16[4,1024]{1,0:T(4,128)(2,1)S(1)}, bf16[1024]{0:T(1024)(128)(2,1)S(1)}, bf16[4,256]{1,0:T(4,128)(2,1)S(1)}, bf16[256]{0:T(256)(128)(2,1)S(1)...) all-reduce(bf16[4,1024]{1,0:T(4,128)(2,1)S(1)} %add_convert_fusion., ...), channel_id=1, replica_groups=mesh['batch'=8,'head'=4] {'batch'}, use_global_device_ids=true, to_apply=%region_39.40 | all-reduce | flops 7472 | bytes 29888 | tf_op jit(solution)/shard_map/psum | solution.py:244
  1297.8 88.0 %all-reduce.34.cloned.1.call-done = (bf16[2048,1024]{1,0:T(8,128)(2,1)}, bf16[2048,1024]{1,0:T(8,128)(2,1)}, bf16[2048,16]{0,1:T(8,128)(2,1)}, bf16[2048,256]{1,0:T(8,128)(2,1)}, bf16[1024,2048]{1,0:T(8,128)(2,1)}) async-done(((bf16[2048,1024]{1,0:T(8,128)(2,1)}, bf16[2048,1024]{1,0:T(8,128)(2,1)}, bf16[2048,16]{0,1:T(8,128)(2,1)}, bf16[2048,256]{1,0:T(8,128)(2,1)}, bf16[1024,2048]{1,0:T(8,128)(2,1)}), ...) | async-done | bytes 13697040 | tf_op jit(solution)/shard_map/psum | solution.py:240
  1403.8 128.8 %reduce-scatter.5.cloned.1.call-done = bf16[512,2048]{1,0:T(8,128)(2,1)} async-done(((bf16[2048,2048]{1,0:T(8,128)(2,1)}), bf16[512,2048]{1,0:T(8,128)(2,1)}) %reduce-scatter.5.cloned.1.call-update) | async-done | bytes 2097168 | tf_op jit(solution)/shard_map/reduce_scatter | solution.py:221
  1537.7 44.9 %psum.136 = f32[2048]{0:T(1024)} all-reduce(f32[2048]{0:T(1024)S(1)} %get-tuple-element.685), channel_id=1, replica_groups=mesh['batch'=8,'head'=4] {'batch','head'}, use_global_device_ids=true, to_apply=%region_30.31 | all-reduce | flops 2048 | bytes 16384 | tf_op jit(solution)/shard_map/psum | solution.py:254
  1582.6 98.4 %reduce-scatter.3.cloned.1.call-done = bf16[512,2048]{1,0:T(8,128)(2,1)} async-done(((bf16[2048,2048]{1,0:T(8,128)(2,1)}), bf16[512,2048]{1,0:T(8,128)(2,1)}) %reduce-scatter.3.cloned.1.call-update) | async-done | bytes 2097168 | tf_op jit(solution)/shard_map/reduce_scatter | solution.py:174
  (1035 shorter events, 873.3 us)
Async XLA Ops:
  7.2 208.1 %copy-start = (bf16[2048,256]{1,0:T(8,128)(2,1)S(1)}, bf16[2048,256]{1,0:T(8,128)(2,1)}, u32[]{:S(2)}) copy-start(bf16[2048,256]{1,0:T(8,128)(2,1)} %param.28) | copy-start | bytes 3145732
  7.2 158.8 %all-gather.3.cloned.1.call-start = ((), (), s32[]{:S(2)}) async-start(), calls=%async_computation.2 | async-start | bytes 10485760 | tf_op jit(solution)/shard_map/all_gather | solution.py:123
  13.5 451.7 %all-gather.5.cloned.1.call-start = ((), (), s32[]{:S(2)}) async-start(), calls=%async_computation.4 | async-start | bytes 10485760 | tf_op jit(solution)/shard_map/all_gather | solution.py:181
  14.3 1179.4 %all-reduce.32.cloned.1.call-start = ((), (), s32[]{:S(2)}) async-start(), calls=%async_computation.6 | async-start | bytes 2097152 | tf_op jit(solution)/shard_map/psum | solution.py:213
  14.8 163.8 %copy-start.47 = (f32[1,1024]{1,0:T(1,128)}, f32[1,1024]{1,0:T(1,128)S(1)}, u32[]{:S(2)}) copy-start(f32[1,1024]{1,0:T(1,128)S(1)} %get-tuple-element.825) | copy-start | bytes 12292
  14.8 163.8 %copy-start.49 = (f32[1,1024]{1,0:T(1,128)}, f32[1,1024]{1,0:T(1,128)S(1)}, u32[]{:S(2)}) copy-start(f32[1,1024]{1,0:T(1,128)S(1)} %get-tuple-element.827) | copy-start | bytes 12292
  14.8 163.8 %copy-start.51 = (f32[1,1024]{1,0:T(1,128)}, f32[1,1024]{1,0:T(1,128)S(1)}, u32[]{:S(2)}) copy-start(f32[1,1024]{1,0:T(1,128)S(1)} %get-tuple-element.826) | copy-start | bytes 12292
  14.8 163.8 %copy-start.53 = (f32[1,1024]{1,0:T(1,128)}, f32[1,1024]{1,0:T(1,128)S(1)}, u32[]{:S(2)}) copy-start(f32[1,1024]{1,0:T(1,128)S(1)} %get-tuple-element.828) | copy-start | bytes 12292
  14.9 206.4 %copy-start.66 = (f32[1,256]{1,0:T(1,128)}, f32[1,256]{1,0:T(1,128)S(1)}, u32[]{:S(2)}) copy-start(f32[1,256]{1,0:T(1,128)S(1)} %get-tuple-element.832) | copy-start | bytes 3076
  14.9 206.4 %copy-start.68 = (f32[1,256]{1,0:T(1,128)}, f32[1,256]{1,0:T(1,128)S(1)}, u32[]{:S(2)}) copy-start(f32[1,256]{1,0:T(1,128)S(1)} %get-tuple-element.834) | copy-start | bytes 3076
  14.9 206.4 %copy-start.70 = (f32[1,256]{1,0:T(1,128)}, f32[1,256]{1,0:T(1,128)S(1)}, u32[]{:S(2)}) copy-start(f32[1,256]{1,0:T(1,128)S(1)} %get-tuple-element.833) | copy-start | bytes 3076
  14.9 206.4 %copy-start.72 = (f32[1,256]{1,0:T(1,128)}, f32[1,256]{1,0:T(1,128)S(1)}, u32[]{:S(2)}) copy-start(f32[1,256]{1,0:T(1,128)S(1)} %get-tuple-element.835) | copy-start | bytes 3076
  14.9 211.6 %copy-start.74 = (f32[16]{0:T(128)}, f32[16]{0:T(128)S(1)}, u32[]{:S(2)}) copy-start(f32[16]{0:T(128)S(1)} %exp.98) | copy-start | bytes 196
  29.5 464.4 %copy-start.45 = (f32[1024]{0:T(1024)}, f32[1024]{0:T(1024)S(1)}, u32[]{:S(2)}) copy-start(f32[1024]{0:T(1024)S(1)} %mul.1002) | copy-start | bytes 12292
  31.0 190.3 %copy-start.36 = (f32[2048]{0:T(1024)}, f32[2048]{0:T(1024)S(1)}, u32[]{:S(2)}) copy-start(f32[2048]{0:T(1024)S(1)} %get-tuple-element.831) | copy-start | bytes 24580
  31.0 190.3 %copy-start.38 = (f32[2048]{0:T(1024)}, f32[2048]{0:T(1024)S(1)}, u32[]{:S(2)}) copy-start(f32[2048]{0:T(1024)S(1)} %get-tuple-element.829) | copy-start | bytes 24580
  31.0 190.3 %copy-start.40 = (f32[2048]{0:T(1024)}, f32[2048]{0:T(1024)S(1)}, u32[]{:S(2)}) copy-start(f32[2048]{0:T(1024)S(1)} %get-tuple-element.830) | copy-start | bytes 24580
  31.0 147.6 %copy-start.77 = (f32[1024]{0:T(1024)S(1)}, f32[1024]{0:T(1024)}, u32[]{:S(2)}) copy-start(f32[1024]{0:T(1024)} %param.30) | copy-start | bytes 12292
  1134.0 251.8 %all-reduce.34.cloned.1.call-start = ((), (), s32[]{:S(2)}) async-start(), calls=%async_computation.7 | async-start | bytes 27394048 | tf_op jit(solution)/shard_map/psum | solution.py:240
  1200.8 331.8 %reduce-scatter.5.cloned.1.call-start = ((), (), s32[]{:S(2)}) async-start(), calls=%async_computation.5 | async-start | bytes 10485760 | tf_op jit(solution)/shard_map/reduce_scatter | solution.py:221
  1245.9 435.1 %reduce-scatter.3.cloned.1.call-start = ((), (), s32[]{:S(2)}) async-start(), calls=%async_computation.3 | async-start | bytes 10485760 | tf_op jit(solution)/shard_map/reduce_scatter | solution.py:174
  1397.2 135.4 %copy-start.8 = (bf16[512,2048]{1,0:T(8,128)(2,1)S(1)}, bf16[512,2048]{1,0:T(8,128)(2,1)}, u32[]{:S(2)}) copy-start(bf16[512,2048]{1,0:T(8,128)(2,1)} %param.22) | copy-start | bytes 6291460
  1397.2 135.4 %copy-start.55 = (f32[2048]{0:T(1024)S(1)}, f32[2048]{0:T(1024)}, u32[]{:S(2)}) copy-start(f32[2048]{0:T(1024)} %param.24) | copy-start | bytes 24580
  1397.2 135.4 %copy-start.60 = (f32[512]{0:T(512)S(1)}, f32[512]{0:T(512)}, u32[]{:S(2)}) copy-start(f32[512]{0:T(512)} %copy-done.59) | copy-start | bytes 6148
  (185 other events, 1582.7 us)
Sparse Core Ops, SparseCore 0:
  13.6 152.3 all-gather.2
  167.6 147.8 all-gather.4
  1134.1 49.9 all-reduce.31
  1200.9 184.8 all-reduce.33
  1388.1 144.4 reduce-scatter.4
  1534.8 146.1 reduce-scatter.2
where the time goes:
time: 1710 us; the launch traced here: 1690 us
  matrix products  506 us (30%)
  waiting for transfers between devices  451 us (26%)
  local copies, waits for them, and re-layouts  323 us (19%)
  other arithmetic  280 us (16%)
  blocking collectives  95.6 us (6%)
  loops' own time  23.3 us (1%)
    dot_general x24, matrix products, block_step(): local_out = jnp.einsum('hij,jhp->ihp', mixing, x_block, precision=HIGHEST)  163 us
    all_gather x1, waiting for transfers between devices, body(): gathered = lax.all_gather(normed, 'head', axis=0, tiled=True)  135 us
    reduce_scatter x1, waiting for transfers between devices, body(): lax.psum_scatter((cols_product(d_gate, w_z) + cols_product(d_inner, w_x)...  129 us
    reduce_scatter x1, waiting for transfers between devices, body(): lax.psum_scatter(jnp.dot(normed_y, w_out, preferred_element_type=jnp.floa...  98.4 us
    psum x1, waiting for transfers between devices, body(): lax.psum(g_w_z.astype(jnp.bfloat16), 'batch').astype(jnp.float32)  88 us
    dot_general x24, matrix products, block_step(): jnp.einsum('jhp,jn->hpn', weighted, b_block, precision=HIGHEST)  74.7 us
    dot_general x32, matrix products, block_step(): jnp.einsum('in,hpn->ihp', c_block, state_now, precision=HIGHEST)  72.2 us
    dot_general x5, matrix products, cols_product(): lax.dot_general(left, right, (((1,), (1,)), ((), ())), preferred_element_...  68.5 us
  transfers between devices with their start and end apart: 6, of which 4 were waited for; matrix products, arithmetic and copies ran while one was open for 26% of the time, Pallas kernels for 0%

commit v1 on v0

v1 whole, which is shorter than its diff:
```python
import functools

import jax
import jax.numpy as jnp
from jax import lax
from jax.experimental import pallas as pl
from jax.experimental.pallas import tpu as pltpu
from jax.sharding import PartitionSpec as P

HEAD_DIM = 64
STATE = 128
CONV = 4
SPAN = 256
SEQ_LEN = 1024
DOCS = 4
CHUNKS = SEQ_LEN // SPAN
WIDE = 256
GROUP = WIDE // HEAD_DIM
EPSILON = 1e-05
F32 = jnp.float32
BF16 = jnp.bfloat16
VMEM_LIMIT = 48 * 1024 * 1024


def dot_nn(a, b):
    return lax.dot_general(a, b, (((1,), (0,)), ((), ())), preferred_element_type=F32)


def dot_nt(a, b):
    return lax.dot_general(a, b, (((1,), (1,)), ((), ())), preferred_element_type=F32)


def dot_tn(a, b):
    return lax.dot_general(a, b, (((0,), (0,)), ((), ())), preferred_element_type=F32)


def sigmoid(v):
    return 0.5 * (1.0 + jnp.tanh(0.5 * v))


def chunk_start(info, c, per_block):
    block = (c // per_block) ^ info[DOCS]
    return pl.multiple_of((block * per_block + c % per_block) * SPAN, SPAN)


def doc_place(info, pos):
    first = jnp.zeros_like(pos)
    last = jnp.full_like(pos, SEQ_LEN)
    for k in range(DOCS):
        first = jnp.where(pos >= info[k], info[k], first)
    for k in reversed(range(DOCS)):
        last = jnp.where(pos < info[k], info[k], last)
    return pos - first, last - 1 - pos


def chunk_masks(info, c):
    local = lax.broadcasted_iota(jnp.int32, (SPAN, 128), 0)
    since, until = doc_place(info, local + c * SPAN)
    return local, since, until


def wide2(v):
    return jnp.concatenate([v, v], axis=1)


def expand(cols):
    rows = cols.shape[0]
    low = lax.broadcasted_iota(jnp.int32, (rows, 128), 1) < HEAD_DIM
    tiles = [
        jnp.where(low, cols[:, 2 * p : 2 * p + 1], cols[:, 2 * p + 1 : 2 * p + 2]) for p in range(WIDE // 128)
    ]
    return jnp.concatenate(tiles, axis=1)


def conv_inputs(src, info, c, per_block, r0):
    now = src[pl.ds(r0, SPAN), :].astype(F32)
    if c == 0:
        before = jnp.zeros((8, now.shape[1]), F32)
    else:
        p0 = chunk_start(info, c - 1, per_block)
        before = src[pl.ds(pl.multiple_of(p0 + SPAN - 16, 16), 16), :].astype(F32)[8:]
    ext = jnp.concatenate([before, now], axis=0)
    return now, [now] + [pltpu.roll(ext, k, 0)[8:] for k in range(1, CONV)]


def conv_apply(lags, taps, bias, masks):
    u = bias + taps[0] * lags[0]
    for k in range(1, CONV):
        u = u + taps[k] * (lags[k] * masks[k])
    return u


def conv_back(du, after, taps, masks_after):
    ext = jnp.concatenate([du, after], axis=0)
    total = taps[0] * du
    for k in range(1, CONV):
        total = total + taps[k] * (pltpu.roll(ext, SPAN + 8 - k, 0)[:SPAN] * masks_after[k])
    return total


def prep_kernel(per_block, info, pairs, par, bc_out, bct_out):
    taps = [par[k : k + 1, :] for k in range(CONV)]
    for c in range(CHUNKS):
        r0 = chunk_start(info, c, per_block)
        _, since, _ = chunk_masks(info, c)
        masks = [wide2((since >= k).astype(F32)) for k in range(CONV)]
        _, lags = conv_inputs(pairs, info, c, per_block, r0)
        u = conv_apply(lags, taps, par[4:5, :], masks)
        low = (u * sigmoid(u)).astype(BF16)
        bc_out[pl.ds(r0, SPAN), :] = low
        bct_out[:, pl.ds(r0, SPAN)] = low.T


def fwd_kernel(
    per_block, info, inner, gate, bc, bct, hs, par, y_out, yg_out, st_out, ss_out, score_scr, state_scr
):
    taps = [par[k : k + 1, :] for k in range(CONV)]
    bias, skip, gain, act = par[4:5, :], par[5:6, :], par[6:7, :], par[7:8, :]
    lane = lax.broadcasted_iota(jnp.int32, (1, 128), 1)
    sides = [(lane < HEAD_DIM).astype(BF16), (lane >= HEAD_DIM).astype(BF16)]

    @pl.when(pl.program_id(0) == 0)
    def _():
        ss_out[...] = jnp.zeros_like(ss_out)
        for c in range(CHUNKS):
            r0 = chunk_start(info, c, per_block)
            _, since, _ = chunk_masks(info, c)
            bcv = bc[pl.ds(r0, SPAN), :]
            score = dot_nt(bcv[:, STATE:], bcv[:, :STATE])
            gap = lax.broadcasted_iota(jnp.int32, (SPAN, SPAN), 0) - lax.broadcasted_iota(
                jnp.int32, (SPAN, SPAN), 1
            )
            score_scr[c] = jnp.where((gap >= 0) & (gap <= wide2(since)), score, 0.0)

    state_scr[...] = jnp.zeros_like(state_scr)
    for c in range(CHUNKS):
        r0 = chunk_start(info, c, per_block)
        local, since, until = chunk_masks(info, c)
        masks = [wide2((since >= k).astype(F32)) for k in range(CONV)]
        _, lags = conv_inputs(inner, info, c, per_block, r0)
        u = conv_apply(lags, taps, bias, masks)
        xf = (u * sigmoid(u)).astype(BF16).astype(F32)
        head_rows = hs[:, pl.ds(r0, SPAN)]
        cum_rows = head_rows[:8]
        cum = cum_rows.T
        step = head_rows[8:].T
        local8, since8, until8 = local[:, :8], since[:, :8], until[:, :8]
        cum_end = cum[SPAN - 1 : SPAN, :]
        entry = jnp.where(since8 > local8, jnp.exp(cum), 0.0)
        tail = jnp.where(until8 >= SPAN - 1 - local8, jnp.exp(cum_end - cum), 0.0)
        keep = entry[SPAN - 1 : SPAN, :]
        xs = (xf * expand(step)).astype(BF16)
        xw = (xf * expand(tail * step)).astype(BF16)
        state = state_scr[...]
        state_low = state.astype(BF16)
        st_out[pl.ds(c * STATE, STATE), :] = state_low
        carried = dot_nn(bc[pl.ds(r0, SPAN), STATE:], state_low) * expand(entry)
        state_scr[...] = state * expand(keep) + dot_nn(bct[:STATE, pl.ds(r0, SPAN)], xw)
        tiles = []
        for p in range(WIDE // 128):
            tile = carried[:, p * 128 : (p + 1) * 128]
            for s in range(2):
                h = 2 * p + s
                decays = jnp.exp(jnp.minimum(cum[:, h : h + 1] - cum_rows[h : h + 1, :], 0.0))
                mixing = (decays * score_scr[c]).astype(BF16)
                tile = tile + dot_nn(mixing, xs[:, p * 128 : (p + 1) * 128] * sides[s])
            tiles.append(tile)
        y = jnp.concatenate(tiles, axis=1)
        y_out[pl.ds(r0, SPAN), :] = y.astype(BF16)
        g = gate[pl.ds(r0, SPAN), :].astype(F32)
        gated = (y + skip * xf) * act * (g * sigmoid(g))
        yg_out[pl.ds(r0, SPAN), :] = (gated * gain).astype(BF16)
        square = gated * gated
        ss_out[pl.ds(r0, SPAN), :] += square[:, :128] + square[:, 128:]


def split_low(v):
    high = v.astype(BF16)
    return high, (v - high.astype(F32)).astype(BF16)


def bwd_kernel(
    per_block,
    blocks,
    info,
    inner,
    gate,
    y_in,
    dn_in,
    bc,
    bct,
    hs,
    sk,
    st,
    par,
    dgate_out,
    dinner_out,
    dbc_out,
    gp_out,
    hr_out,
    score_scr,
    pair_scr,
    mask_scr,
    adj_scr,
):
    taps = [par[k : k + 1, :] for k in range(CONV)]
    bias, skip, gain, act = par[4:5, :], par[5:6, :], par[6:7, :], par[7:8, :]
    lane = lax.broadcasted_iota(jnp.int32, (1, 128), 1)
    sides = [(lane < HEAD_DIM).astype(BF16), (lane >= HEAD_DIM).astype(BF16)]
    head_of = lax.broadcasted_iota(jnp.int32, (8, WIDE), 1) // HEAD_DIM
    row8 = lax.broadcasted_iota(jnp.int32, (8, WIDE), 0)
    pick = (head_of == row8).astype(BF16)
    pick_up = (head_of + 4 == row8).astype(BF16)

    @pl.when(pl.program_id(0) == 0)
    def _():
        dbc_out[...] = jnp.zeros_like(dbc_out)
        pair_scr[...] = jnp.zeros_like(pair_scr)
        for c in range(CHUNKS):
            r0 = chunk_start(info, c, per_block)
            _, since, until = chunk_masks(info, c)
            bcv = bc[pl.ds(r0, SPAN), :]
            score = dot_nt(bcv[:, :STATE], bcv[:, STATE:])
            gap = lax.broadcasted_iota(jnp.int32, (SPAN, SPAN), 1) - lax.broadcasted_iota(
                jnp.int32, (SPAN, SPAN), 0
            )
            score_scr[c] = jnp.where((gap >= 0) & (gap <= wide2(until)), score, 0.0)
            mask_scr[c] = jnp.where((gap <= 0) & (-gap <= wide2(since)), 1.0, 0.0).astype(BF16)

    adj_scr[...] = jnp.zeros_like(adj_scr)
    after = jnp.zeros((8, WIDE), F32)
    gp = jnp.zeros((8, WIDE), F32)
    for c in reversed(range(CHUNKS)):
        r0 = chunk_start(info, c, per_block)
        local, since, until = chunk_masks(info, c)
        masks = [wide2((since >= k).astype(F32)) for k in range(CONV)]
        masks_after = [wide2((until >= k).astype(F32)) for k in range(CONV)]
        _, lags = conv_inputs(inner, info, c, per_block, r0)
        u = conv_apply(lags, taps, bias, masks)
        su = sigmoid(u)
        xf = (u * su).astype(BF16).astype(F32)
        head_rows = hs[:, pl.ds(r0, SPAN)]
        cum_rows, step_rows = head_rows[:8], head_rows[8:]
        cum = cum_rows.T
        step = step_rows.T
        local8, since8, until8 = local[:, :8], since[:, :8], until[:, :8]
        cum_end = cum[SPAN - 1 : SPAN, :]
        entry = jnp.where(since8 > local8, jnp.exp(cum), 0.0)
        tail = jnp.where(until8 >= SPAN - 1 - local8, jnp.exp(cum_end - cum), 0.0)
        keep = entry[SPAN - 1 : SPAN, :]
        step_wide = expand(step)
        xs = (xf * step_wide).astype(BF16)
        xw = (xf * expand(tail * step)).astype(BF16)
        row_cols = sk[:, pl.ds(r0, SPAN)].T
        scale, fix = row_cols[:, 0:1], row_cols[:, 1:2]

        g = gate[pl.ds(r0, SPAN), :].astype(F32)
        sg = sigmoid(g)
        sw = g * sg
        y = y_in[pl.ds(r0, SPAN), :].astype(F32)
        dn = dn_in[pl.ds(r0, SPAN), :].astype(F32)
        masked = (y + skip * xf) * act
        gated = masked * sw
        d_scale = dn * scale
        d_gated = d_scale * gain - gated * fix
        dgate_out[pl.ds(r0, SPAN), :] = (d_gated * masked * sg * (1.0 + g * (1.0 - sg))).astype(BF16)
        dy_low = (d_gated * sw * act).astype(BF16)
        dy = dy_low.astype(F32)
        dy_entry = (dy * expand(entry)).astype(BF16)
        g_gain = jnp.sum(d_scale * gated, axis=0, keepdims=True)

        adj = adj_scr[...]
        adj_low = adj.astype(BF16)
        bcv = bc[pl.ds(r0, SPAN), :]
        d_c = dot_nt(dy_entry, st[pl.ds(c * STATE, STATE), :])
        d_b = dot_nt(xw, adj_low)
        dbc_out[pl.ds(r0, SPAN), :] += jnp.concatenate([d_b, d_c], axis=1)
        carried = dot_nn(bcv[:, :STATE], adj_low) * expand(tail)
        adj_scr[...] = adj * expand(keep) + dot_nn(bct[STATE:, pl.ds(r0, SPAN)], dy_entry)

        pair_sum = pair_scr[c]
        tiles = []
        for p in range(WIDE // 128):
            tile = carried[:, p * 128 : (p + 1) * 128]
            dy_tile = dy_low[:, p * 128 : (p + 1) * 128]
            xs_tile = xs[:, p * 128 : (p + 1) * 128]
            for s in range(2):
                h = 2 * p + s
                decays = jnp.exp(jnp.minimum(cum_rows[h : h + 1, :] - cum[:, h : h + 1], 0.0))
                mixing = (decays * score_scr[c]).astype(BF16)
                tile = tile + dot_nn(mixing, dy_tile * sides[s])
                pair_sum = pair_sum + decays * dot_nt(xs_tile * sides[s], dy_tile)
            tiles.append(tile)
        pair_scr[c] = pair_sum
        dxu = jnp.concatenate(tiles, axis=1)

        du = (step_wide * dxu + skip * dy) * (su * (1.0 + u * (1.0 - su)))
        dinner_out[pl.ds(r0, SPAN), :] = conv_back(du, after, taps, masks_after).astype(BF16)
        after = du[:8]
        sums = [jnp.sum(du * lags[k] * masks[k], axis=0, keepdims=True) for k in range(CONV)]
        sums += [jnp.sum(du, axis=0, keepdims=True), jnp.zeros((1, WIDE), F32), g_gain, jnp.zeros((1, WIDE), F32)]
        gp = gp + jnp.concatenate(sums, axis=0)

        q1h, q1l = split_low(dy * y)
        q2h, q2l = split_low(xf * dxu)
        q3h, q3l = split_low(xf * dy)
        row_term = dot_nt(pick, q1h) + dot_nt(pick, q1l)
        steps = dot_nt(pick, q2h) + dot_nt(pick, q2l) + dot_nt(pick_up, q3h) + dot_nt(pick_up, q3l)
        vh, vl = split_low(row_term - step_rows * jnp.where(row8 < GROUP, steps, 0.0))
        d_decay = dot_nn(vh, mask_scr[c]) + dot_nn(vl, mask_scr[c])
        row_local = lax.broadcasted_iota(jnp.int32, (8, SPAN), 1)
        row_since, row_until = doc_place(info, row_local + c * SPAN)
        if c < CHUNKS - 1:
            ph, plow = split_low(st[pl.ds((c + 1) * STATE, STATE), :].astype(F32) * adj)
            cross = jnp.sum(dot_nt(pick, ph) + dot_nt(pick, plow), axis=1, keepdims=True)
            d_decay = d_decay + jnp.where(row_until >= SPAN - 1 - row_local, cross, 0.0)
        d_decay = jnp.where(row_since > 0, d_decay, 0.0)
        hr_out[:, pl.ds(r0, SPAN)] = jnp.concatenate([steps, d_decay], axis=0)
    gp_out[...] = gp

    @pl.when(pl.program_id(0) == blocks - 1)
    def _():
        for c in range(CHUNKS):
            r0 = chunk_start(info, c, per_block)
            _, _, until = chunk_masks(info, c)
            gap = lax.broadcasted_iota(jnp.int32, (SPAN, SPAN), 1) - lax.broadcasted_iota(
                jnp.int32, (SPAN, SPAN), 0
            )
            pair_low = jnp.where((gap >= 0) & (gap <= wide2(until)), pair_scr[c], 0.0).astype(BF16)
            bcv = bc[pl.ds(r0, SPAN), :]
            dbc_out[pl.ds(r0, SPAN), :] += jnp.concatenate(
                [dot_nn(pair_low, bcv[:, STATE:]), dot_tn(pair_low, bcv[:, :STATE])], axis=1
            )


def pair_kernel(per_block, info, pairs, dbc_a, dbc_b, par, dp_out, gp_out):
    taps = [par[k : k + 1, :] for k in range(CONV)]
    after = jnp.zeros((8, WIDE), F32)
    gp = jnp.zeros((8, WIDE), F32)
    for c in reversed(range(CHUNKS)):
        r0 = chunk_start(info, c, per_block)
        _, since, until = chunk_masks(info, c)
        masks = [wide2((since >= k).astype(F32)) for k in range(CONV)]
        masks_after = [wide2((until >= k).astype(F32)) for k in range(CONV)]
        _, lags = conv_inputs(pairs, info, c, per_block, r0)
        u = conv_apply(lags, taps, par[4:5, :], masks)
        su = sigmoid(u)
        rows = pl.ds(r0, SPAN)
        du = (dbc_a[rows, :] + dbc_b[rows, :]) * (su * (1.0 + u * (1.0 - su)))
        dp_out[rows, :] = conv_back(du, after, taps, masks_after).astype(BF16)
        after = du[:8]
        sums = [jnp.sum(du * lags[k] * masks[k], axis=0, keepdims=True) for k in range(CONV)]
        sums += [jnp.sum(du, axis=0, keepdims=True), jnp.zeros((3, WIDE), F32)]
        gp = gp + jnp.concatenate(sums, axis=0)
    gp_out[...] = gp


def whole(shape):
    return pl.BlockSpec(shape, lambda i, info: (0,) * len(shape))


def cols(rows):
    return pl.BlockSpec((rows, WIDE), lambda i, info: (0, i))


def call(kernel, grid, in_specs, out_specs, out_shape, scratch, flops, moved, info, *operands):
    return pl.pallas_call(
        kernel,
        grid_spec=pltpu.PrefetchScalarGridSpec(
            num_scalar_prefetch=1,
            grid=(grid,),
            in_specs=in_specs,
            out_specs=out_specs,
            scratch_shapes=scratch,
        ),
        out_shape=out_shape,
        compiler_params=pltpu.CompilerParams(vmem_limit_bytes=VMEM_LIMIT),
        cost_estimate=pl.CostEstimate(flops=flops, bytes_accessed=moved, transcendentals=0),
    )(info, *operands)


def shape(dims, kind):
    return jax.ShapeDtypeStruct(dims, kind)


def prep(per_block, info, pairs, par):
    t = SEQ_LEN
    return call(
        functools.partial(prep_kernel, per_block),
        1,
        [whole((t, WIDE)), whole((8, WIDE))],
        [whole((t, WIDE)), whole((WIDE, t))],
        [shape((t, WIDE), BF16), shape((WIDE, t), BF16)],
        [],
        10**9,
        3 * 10**6,
        info,
        pairs,
        par,
    )


def scan_forward(per_block, info, inner, gate, bc, bct, hs, par):
    t, channels = inner.shape
    blocks = channels // WIDE
    return call(
        functools.partial(fwd_kernel, per_block),
        blocks,
        [
            cols(t),
            cols(t),
            whole((t, WIDE)),
            whole((WIDE, t)),
            pl.BlockSpec((16, t), lambda i, info: (i, 0)),
            cols(8),
        ],
        [cols(t), cols(t), cols(CHUNKS * STATE), whole((t, 128))],
        [
            shape((t, channels), BF16),
            shape((t, channels), BF16),
            shape((CHUNKS * STATE, channels), BF16),
            shape((t, 128), F32),
        ],
        [pltpu.VMEM((CHUNKS, SPAN, SPAN), F32), pltpu.VMEM((STATE, WIDE), F32)],
        blocks * 2 * 10**9,
        10 * t * channels,
        info,
        inner,
        gate,
        bc,
        bct,
        hs,
        par,
    )


def scan_backward(per_block, info, inner, gate, y, dn, bc, bct, hs, sk, st, par):
    t, channels = inner.shape
    blocks = channels // WIDE
    return call(
        functools.partial(bwd_kernel, per_block, blocks),
        blocks,
        [
            cols(t),
            cols(t),
            cols(t),
            cols(t),
            whole((t, WIDE)),
            whole((WIDE, t)),
            pl.BlockSpec((16, t), lambda i, info: (i, 0)),
            whole((8, t)),
            cols(CHUNKS * STATE),
            cols(8),
        ],
        [
            cols(t),
            cols(t),
            whole((t, WIDE)),
            cols(8),
            pl.BlockSpec((16, t), lambda i, info: (i, 0)),
        ],
        [
            shape((t, channels), BF16),
            shape((t, channels), BF16),
            shape((t, WIDE), F32),
            shape((8, channels), F32),
            shape((blocks * 16, t), F32),
        ],
        [
            pltpu.VMEM((CHUNKS, SPAN, SPAN), F32),
            pltpu.VMEM((CHUNKS, SPAN, SPAN), F32),
            pltpu.VMEM((CHUNKS, SPAN, SPAN), BF16),
            pltpu.VMEM((STATE, WIDE), F32),
        ],
        blocks * 5 * 10**9,
        16 * t * channels,
        info,
        inner,
        gate,
        y,
        dn,
        bc,
        bct,
        hs,
        sk,
        st,
        par,
    )


def pair_backward(per_block, info, pairs, dbc_a, dbc_b, par):
    t = SEQ_LEN
    return call(
        functools.partial(pair_kernel, per_block),
        1,
        [whole((t, WIDE)), whole((t, WIDE)), whole((t, WIDE)), whole((8, WIDE))],
        [whole((t, WIDE)), whole((8, WIDE))],
        [shape((t, WIDE), BF16), shape((8, WIDE), F32)],
        [],
        10**9,
        4 * 10**6,
        info,
        pairs,
        dbc_a,
        dbc_b,
        par,
    )


def body(
    axis_sizes,
    hidden_in,
    out_grad,
    norm_gain,
    w_z,
    w_x,
    w_dt,
    w_bc,
    conv_x,
    conv_x_bias,
    conv_bc,
    conv_bc_bias,
    dt_bias,
    a_log,
    d_skip,
    gate_gain,
    w_out,
    doc_lengths,
    widths,
):
    batches, stacks = axis_sizes
    rows, width_in = hidden_in.shape
    heads_here = dt_bias.shape[0]
    channels = w_x.shape[1]
    members = stacks // widths.shape[0]
    far_bit = members
    per_block = rows // SPAN
    place = lax.axis_index("head")
    lot = lax.axis_index("batch")
    own_seq = place // members
    ends = jnp.cumsum(lax.dynamic_index_in_dim(doc_lengths, own_seq, 0, keepdims=False))
    width = lax.dynamic_index_in_dim(widths, own_seq, 0, keepdims=False)
    info = jnp.concatenate([ends.astype(jnp.int32), (place % members).astype(jnp.int32)[None]])

    def across(v, bit):
        return lax.ppermute(v, "head", [(i, i ^ bit) for i in range(stacks)])

    def gather_rows(v):
        bit = 1
        while bit < members:
            v = jnp.concatenate([v, across(v, bit)], axis=0)
            bit *= 2
        return v

    def scatter_rows(v):
        bit = members // 2
        while bit >= 1:
            half = v.shape[0] // 2
            v = v[:half] + across(v[half:], bit)
            bit //= 2
        return v

    def sum_rows(v):
        bit = 1
        while bit < members:
            got = across(v, bit)
            flipped = got.reshape(v.shape[0], -1, 2, bit * rows)[:, :, ::-1, :].reshape(v.shape)
            v = v + flipped
            bit *= 2
        return v

    def fetch_far(w):
        piece = w.shape[0] // batches
        mine = lax.dynamic_slice_in_dim(w, lot * piece, piece, 0)
        return lax.all_gather(across(mine, far_bit), "batch", axis=0, tiled=True)

    hidden_all = gather_rows(hidden_in)
    upstream = gather_rows(out_grad)
    w_x2 = (w_x, fetch_far(w_x))
    w_z2 = (w_z, fetch_far(w_z))
    w_out2 = (w_out, fetch_far(w_out))
    w_dt_own = w_dt.T
    w_dt_far = across(w_dt_own, far_bit)
    head_row = jnp.concatenate([dt_bias, a_log])
    par_own = jnp.concatenate(
        [
            conv_x,
            conv_x_bias[None],
            jnp.repeat(d_skip, HEAD_DIM)[None],
            gate_gain[None],
            jnp.pad(head_row, (0, channels - head_row.shape[0]))[None],
        ],
        axis=0,
    )
    par_far = across(par_own, far_bit)
    active = (jnp.arange(channels) // HEAD_DIM < width * heads_here // (heads_here * stacks)).astype(F32)
    rate_par = [(v[7, :heads_here], v[7, heads_here : 2 * heads_here]) for v in (par_own, par_far)]
    par2 = [jnp.concatenate([v[:7], active[None]], axis=0) for v in (par_own, par_far)]
    step_bias = jnp.concatenate([rate_par[0][0], rate_par[1][0]])[:, None]
    speed = jnp.exp(jnp.concatenate([rate_par[0][1], rate_par[1][1]]))[:, None]
    par_bc = jnp.concatenate([conv_bc, conv_bc_bias[None], jnp.zeros((3, 2 * STATE), F32)], axis=0)

    residual_all = hidden_all.astype(F32)
    inverse_all = lax.rsqrt(jnp.mean(residual_all * residual_all, axis=-1, keepdims=True) + EPSILON)
    normed = (residual_all * inverse_all * norm_gain).astype(BF16)
    w_small = jnp.concatenate([w_bc, w_dt_own.T, w_dt_far.T], axis=1)
    small_cols = dot_nn(normed, w_small)
    pairs = small_cols[:, : 2 * STATE]
    rates = small_cols[:, 2 * STATE :].T
    step = jax.nn.softplus(rates + step_bias)
    decay = -step * speed
    upper = (jnp.arange(SPAN)[:, None] <= jnp.arange(SPAN)[None, :]).astype(F32)
    cum = lax.dot_general(
        decay.reshape(-1, SPAN), upper, (((1,), (0,)), ((), ())), precision=lax.Precision.HIGHEST
    ).reshape(decay.shape)

    def grouped(v):
        v = v.reshape(-1, GROUP, SEQ_LEN)
        return jnp.pad(v, ((0, 0), (0, 8 - GROUP), (0, 0)))

    hs = jnp.concatenate([grouped(cum), grouped(step)], axis=1).reshape(-1, SEQ_LEN)
    half = hs.shape[0] // 2
    hs2 = (hs[:half], hs[half:])
    bc, bct = prep(per_block, info, pairs, par_bc)

    inner2 = [dot_nn(normed, w).astype(BF16) for w in w_x2]
    gate2 = [dot_nn(normed, w).astype(BF16) for w in w_z2]
    forward = [
        scan_forward(per_block, info, inner2[i], gate2[i], bc, bct, hs2[i], par2[i]) for i in range(2)
    ]
    y2 = [f[0] for f in forward]
    yg2 = [f[1] for f in forward]
    branch = scatter_rows((dot_nn(yg2[0], w_out2[0]) + dot_nn(yg2[1], w_out2[1])).astype(BF16))
    dn2, inner_sums = [], []
    for i in range(2):
        dn = dot_nt(upstream, w_out2[i])
        inner_sums.append(jnp.sum(dn * yg2[i].astype(F32), axis=1))
        dn2.append(dn.astype(BF16))
    square = jnp.sum(forward[0][3] + forward[1][3], axis=1)
    sums = sum_rows(jnp.stack([square, inner_sums[0] + inner_sums[1]]))
    count = (width * HEAD_DIM).astype(F32)
    scale = lax.rsqrt(sums[0] / count + EPSILON)
    fix = scale * scale * scale * sums[1] / count
    sk = jnp.concatenate([scale[None], fix[None], jnp.zeros((6, SEQ_LEN), F32)], axis=0)

    scaled_up = (upstream.astype(F32) * scale[:, None]).astype(BF16)
    mixed = (hidden_in.astype(F32) + branch.astype(F32) * scale[:rows, None]).astype(BF16)

    back = [None, None]
    for i in (1, 0):
        back[i] = scan_backward(
            per_block, info, inner2[i], gate2[i], y2[i], dn2[i], bc, bct, hs2[i], sk, forward[i][2], par2[i]
        )
    d_pairs, g_bc = pair_backward(per_block, info, pairs, back[0][2], back[1][2], par_bc)

    heads_out = [b[4].reshape(-1, 16, SEQ_LEN) for b in back]
    d_step = jnp.concatenate([h[:, :GROUP].reshape(-1, SEQ_LEN) for h in heads_out], axis=0)
    skip_rows = jnp.concatenate([h[:, GROUP : 2 * GROUP].reshape(-1, SEQ_LEN) for h in heads_out], axis=0)
    d_decay = jnp.concatenate([h[:, 8 : 8 + GROUP].reshape(-1, SEQ_LEN) for h in heads_out], axis=0)
    d_rates_pre = (d_step - d_decay * speed) * jax.nn.sigmoid(rates + step_bias)
    head_grads = jnp.stack(
        [jnp.sum(d_rates_pre, axis=1), jnp.sum(d_decay * decay, axis=1), jnp.sum(skip_rows, axis=1)]
    )
    d_rates = d_rates_pre.astype(BF16)
    d_small = jnp.concatenate([d_pairs, d_rates.T], axis=1)

    d_normed_part = dot_nt(d_small, w_small)
    for i in range(2):
        d_normed_part = d_normed_part + dot_nt(back[i][0], w_z2[i]) + dot_nt(back[i][1], w_x2[i])
    d_normed_in = scatter_rows(d_normed_part.astype(BF16)).astype(F32)

    def reduce_pair(own, far):
        far_piece = lax.psum_scatter(far, "batch", scatter_dimension=0, tiled=True)
        own_piece = lax.psum_scatter(own, "batch", scatter_dimension=0, tiled=True)
        total = own_piece + across(far_piece, far_bit)
        return lax.all_gather(total, "batch", axis=0, tiled=True).astype(F32)

    g_w_out = reduce_pair(*[dot_tn(yg2[i], scaled_up).astype(BF16) for i in range(2)])
    g_w_z = reduce_pair(*[dot_tn(normed, back[i][0]).astype(BF16) for i in range(2)])
    g_w_x = reduce_pair(*[dot_tn(normed, back[i][1]).astype(BF16) for i in range(2)])
    g_small = dot_tn(d_small, normed)
    g_w_bc = lax.psum(g_small[: 2 * STATE].astype(BF16), ("batch", "head")).astype(F32).T
    g_bc_total = lax.psum(g_bc, ("batch", "head"))

    def pack(i):
        gp = back[i][3]
        heads = head_grads[:, i * heads_here : (i + 1) * heads_here].reshape(-1)
        heads = jnp.pad(heads, (0, channels - heads.shape[0]))[None]
        start = 2 * STATE + i * heads_here
        return jnp.concatenate(
            [gp[:5], heads, gp[6:7], jnp.zeros((1, channels), F32), g_small[start : start + heads_here].reshape(-1, channels)],
            axis=0,
        )

    packed = lax.psum(pack(0) + across(pack(1), far_bit), "batch")
    heads_total = packed[5]
    g_w_dt = packed[8:].reshape(heads_here, width_in).T

    residual = hidden_in.astype(F32)
    inverse = inverse_all[:rows]
    unit_rows = residual * inverse
    g_norm = lax.psum(jnp.sum(d_normed_in * unit_rows, axis=0), ("batch", "head"))
    d_unit = d_normed_in * norm_gain
    d_residual = inverse * (d_unit - unit_rows * jnp.mean(d_unit * unit_rows, axis=-1, keepdims=True))
    in_grad = (out_grad.astype(F32) + d_residual).astype(BF16)
    return (
        mixed,
        in_grad,
        g_norm,
        g_w_z,
        g_w_x,
        g_w_dt,
        g_w_bc,
        packed[:4],
        packed[4],
        g_bc_total[:4],
        g_bc_total[4],
        heads_total[:heads_here],
        heads_total[heads_here : 2 * heads_here],
        heads_total[2 * heads_here : 3 * heads_here],
        packed[6],
        g_w_out,
    )


def solution(mesh):
    split = P(("batch", "head"), None)
    by_col, by_head, by_row = P(None, "head"), P("head"), P("head", None)
    return jax.shard_map(
        functools.partial(body, (mesh.shape["batch"], mesh.shape["head"])),
        mesh=mesh,
        in_specs=(
            split,
            split,
            P(),
            by_col,
            by_col,
            by_col,
            P(),
            by_col,
            by_head,
            P(),
            P(),
            by_head,
            by_head,
            by_head,
            by_head,
            by_row,
            P("batch", None),
            P("batch"),
        ),
        out_specs=(
            split,
            split,
            P(),
            by_col,
            by_col,
            by_col,
            P(),
            by_col,
            by_head,
            P(),
            P(),
            by_head,
            by_head,
            by_head,
            by_head,
            by_row,
        ),
        check_vma=False,
    )
```

time: 1710 us -> 1010 us (0.59)
  matrix products: 506 us -> 187 us
  local copies, waits for them, and re-layouts: 323 us -> 58.4 us
  other arithmetic: 280 us -> 43.7 us
  Pallas kernels: 0 us -> 128 us
  blocking collectives: 95.6 us -> 39.4 us
  waiting for transfers between devices: 451 us -> 502 us
  loops' own time: 23.3 us -> 0 us
  starting transfers between devices: 0.24 us -> 22.4 us
    dot_general x127 -> x22, matrix products: 506 us -> 187 us  [the longest x7 68.2 us: dot_nt(): lax.dot_general(a, b, (((1,), (1,)), ((), ())), preferred_element_type=F32)]
    ppermute x0 -> x14, waiting for transfers between devices: none -> 172 us  [across(): return lax.ppermute(v, 'head', [(i, i ^ bit) for i in range(stacks)])]
    pallas_call x0 -> x6, Pallas kernels: none -> 128 us  [call(): pl.pallas_call(kernel, grid_spec=pltpu.PrefetchScalarGridSpec(num_scalar_...]
    all_gather x2 -> x6, waiting for transfers between devices: 135 us -> 47.7 us  [the longest x3 47.7 us: reduce_pair(): return lax.all_gather(total, 'batch', axis=0, tiled=True).astype(F32)]
    reduce_scatter x2 -> x6, waiting for transfers between devices: 227 us -> 141 us  [the longest x3 88.6 us: reduce_pair(): own_piece = lax.psum_scatter(own, 'batch', scatter_dimension=0, tiled=True)]
    reduce_sum x19 -> x5, other arithmetic: 84.4 us -> 7.75 us  [the longest x1 3.76 us: body(): jnp.sum(d_normed_in * unit_rows, axis=0)]
    reshape x13 -> x14, local copies, waits for them, and re-layouts: 70.9 us -> 1.16 us  [the longest x1 0.7 us: body(): g_w_dt = packed[8:].reshape(heads_here, width_in).T]
    psum x5 -> x1, blocking collectives: 95.6 us -> 39.4 us  [body(): lax.psum(jnp.sum(d_normed_in * unit_rows, axis=0), ('batch', 'head'))]
  transfers between devices with their start and end apart: 6 -> 28, of which waited for: 4 -> 15; matrix products, arithmetic and copies ran while one was open for 26% -> 24% of each run, Pallas kernels for 0% -> 9%
where the time goes in v1:
time: 1010 us; the launch traced here: 997 us
  waiting for transfers between devices  502 us (50%)
  matrix products  187 us (19%)
  Pallas kernels  128 us (13%)
  local copies, waits for them, and re-layouts  58.4 us (6%)
  other arithmetic  43.7 us (4%)
  blocking collectives  39.4 us (4%)
  starting transfers between devices  22.4 us (2%)
  between operations  16.3 us (2%)
    ppermute x14, waiting for transfers between devices, across(): return lax.ppermute(v, 'head', [(i, i ^ bit) for i in range(stacks)])  172 us
    psum x1, waiting for transfers between devices, body(): lax.psum(g_small[:2 * STATE].astype(BF16), ('batch', 'head')).astype(F32)  133 us
    pallas_call x6, Pallas kernels, call(): pl.pallas_call(kernel, grid_spec=pltpu.PrefetchScalarGridSpec(num_scalar_...  128 us
    reduce_scatter x3, waiting for transfers between devices, reduce_pair(): own_piece = lax.psum_scatter(own, 'batch', scatter_dimension=0, tiled=True)  88.6 us
    dot_general x7, matrix products, dot_nt(): lax.dot_general(a, b, (((1,), (1,)), ((), ())), preferred_element_type=F32)  68.2 us
    dot_general x7, matrix products, dot_tn(): lax.dot_general(a, b, (((0,), (0,)), ((), ())), preferred_element_type=F32)  61.3 us
    dot_general x7, matrix products, dot_nn(): lax.dot_general(a, b, (((1,), (0,)), ((), ())), preferred_element_type=F32)  56.8 us
    reduce_scatter x3, waiting for transfers between devices, reduce_pair(): far_piece = lax.psum_scatter(far, 'batch', scatter_dimension=0, tiled=True)  52.1 us
  transfers between devices with their start and end apart: 28, of which 15 were waited for; matrix products, arithmetic and copies ran while one was open for 24% of the time, Pallas kernels for 9%

profile of v1, /device:TPU:0, one launch (start us, length us, event | category | flops | bytes accessed | tf_op | source)
XLA Modules:
  0.0 997.4 jit_solution(2538298439556861752)
XLA Ops:
  12.5 23.2 %collective-permute-done.3 = bf16[256,1024]{1,0:T(8,128)(2,1)S(1)} collective-permute-done((bf16[256,1024]{1,0:T(8,128)(2,1)S(1)}, bf16[256,1024]{1,0:T(8,128)(2,1)S(1)}, u32[]{:S(2)}, u32[]{:S(2)}) %collective-permute-start.3) | collective-permute-done | bytes 524320 | tf_op jit(solution)/shard_map/ppermute | solution.py:546
  37.8 25.2 %collective-permute-done.4 = bf16[256,1024]{1,0:T(8,128)(2,1)S(1)} collective-permute-done((bf16[256,1024]{1,0:T(8,128)(2,1)S(1)}, bf16[256,1024]{1,0:T(8,128)(2,1)S(1)}, u32[]{:S(2)}, u32[]{:S(2)}) %collective-permute-start.4) | collective-permute-done | bytes 524320 | tf_op jit(solution)/shard_map/ppermute | solution.py:546
  79.5 42.7 %collective-permute-done.2 = f32[8,1024]{1,0:T(8,128)S(1)} collective-permute-done((f32[8,1024]{1,0:T(8,128)S(1)}, f32[8,1024]{1,0:T(8,128)S(1)}, u32[]{:S(2)}, u32[]{:S(2)}) %collective-permute-start.2) | collective-permute-done | bytes 32800 | tf_op jit(solution)/shard_map/ppermute | solution.py:546
  122.4 53.7 %collective-permute-done.5 = bf16[128,2048]{1,0:T(8,128)(2,1)} collective-permute-done((bf16[128,2048]{1,0:T(8,128)(2,1)}, bf16[128,2048]{1,0:T(8,128)(2,1)}, u32[]{:S(2)}, u32[]{:S(2)}) %collective-permute-start.5) | collective-permute-done | bytes 524320 | tf_op jit(solution)/shard_map/ppermute | solution.py:546
  207.4 20.6 %shard_map.298 = (bf16[1024,1024]{1,0:T(8,128)(2,1)S(1)}, bf16[1024,1024]{1,0:T(8,128)(2,1)}, bf16[512,1024]{1,0:T(8,128)(2,1)S(1)}, f32[1024,128]{1,0:T(8,128)S(1)}) custom-call(s32[5]{0:T(128)S(1)} %pad_add_fusion.info, bf16[1024,1024]{1,0:T(8,128)(2,1)} %convolution_convert_fusion.9.inner, bf16[1024,1024]{1,0:T(8,128)(2,1)} %convolution_convert_fusion.8.gate, ...), custom_call_target="tpu_custom_call" | custom-call | flops 8000000000 | bytes 10485760 | tf_op jit(solution)/shard_map/pallas_call | solution.py:367
  256.5 20.0 %shard_map.299 = (bf16[1024,1024]{1,0:T(8,128)(2,1)S(1)}, bf16[1024,1024]{1,0:T(8,128)(2,1)}, bf16[512,1024]{1,0:T(8,128)(2,1)S(1)}, f32[1024,128]{1,0:T(8,128)S(1)}) custom-call(s32[5]{0:T(128)S(1)} %pad_add_fusion.info, bf16[1024,1024]{1,0:T(8,128)(2,1)} %convolution_convert_fusion.7.inner, bf16[1024,1024]{1,0:T(8,128)(2,1)} %convolution_convert_fusion.6.gate, ...), custom_call_target="tpu_custom_call" | custom-call | flops 8000000000 | bytes 10485760 | tf_op jit(solution)/shard_map/pallas_call | solution.py:367
  278.8 9.9 fusion.40
  297.0 41.3 %shard_map.301 = (bf16[1024,1024]{1,0:T(8,128)(2,1)S(1)}, bf16[1024,1024]{1,0:T(8,128)(2,1)}, f32[1024,256]{1,0:T(8,128)S(1)}, f32[8,1024]{1,0:T(8,128)S(1)}, f32[64,1024]{1,0:T(8,128)S(1)}) custom-call(s32[5]{0:T(128)S(1)} %pad_add_fusion.info, bf16[1024,1024]{1,0:T(8,128)(2,1)} %convolution_convert_fusion.7.inner, ...), custom_call_target="tpu_custom_call" | custom-call | flops 20000000000 | bytes 16777216 | tf_op jit(solution)/shard_map/pallas_call | solution.py:367
  351.6 41.2 %shard_map.300 = (bf16[1024,1024]{1,0:T(8,128)(2,1)S(1)}, bf16[1024,1024]{1,0:T(8,128)(2,1)}, f32[1024,256]{1,0:T(8,128)S(1)}, f32[8,1024]{1,0:T(8,128)S(1)}, f32[64,1024]{1,0:T(8,128)S(1)}) custom-call(s32[5]{0:T(128)S(1)} %pad_add_fusion.info, bf16[1024,1024]{1,0:T(8,128)(2,1)} %convolution_convert_fusion.9.inner, ...), custom_call_target="tpu_custom_call" | custom-call | flops 20000000000 | bytes 16777216 | tf_op jit(solution)/shard_map/pallas_call | solution.py:367
  414.3 10.4 %convolution_convert_fusion.3 = bf16[2048,1024]{1,0:T(8,128)(2,1)} fusion(bf16[1024,1024]{1,0:T(8,128)(2,1)} %get-tuple-element.54, f32[2048]{0:T(1024)S(1)} %copy-done.45, f32[1024]{0:T(1024)S(1)} %copy-done.50, bf16[512,2048]{1,0:T(8,128)(2,1)} %collective-permute-done, bf16[512,2048]{1,0:T(8,128)(2,1)} %param.18), kind=kOutput, calls=%fused_computation.27 | convolution fusion | flops 4311744512 | bytes 10498048 | tf_op jit(solution)/shard_map/dot_general | solution.py:34
  425.0 10.4 %convolution_convert_fusion = bf16[1024,2048]{1,0:T(8,128)(2,1)} fusion(bf16[1024,1024]{1,0:T(8,128)(2,1)} %get-tuple-element.41, bf16[1024,2048]{1,0:T(8,128)(2,1)} %constant_dynamic-update-slice_fusion, f32[1024]{0:T(1024)S(1)} %bitcast.111), kind=kOutput, calls=%fused_computation.24 | convolution fusion | flops 4303355904 | bytes 10489856 | tf_op jit(solution)/shard_map/dot_general | solution.py:34
  471.6 19.0 %collective-permute-done.10 = bf16[256,1024]{1,0:T(8,128)(2,1)S(1)} collective-permute-done((bf16[256,1024]{1,0:T(8,128)(2,1)}, bf16[256,1024]{1,0:T(8,128)(2,1)S(1)}, u32[]{:S(2)}, u32[]{:S(2)}) %collective-permute-start.10) | collective-permute-done | bytes 524320 | tf_op jit(solution)/shard_map/ppermute | solution.py:546
  492.7 17.7 %reduce-scatter.13.cloned.1.call-done = bf16[256,1024]{1,0:T(8,128)(2,1)} async-done(((bf16[2048,1024]{1,0:T(8,128)(2,1)}), bf16[256,1024]{1,0:T(8,128)(2,1)}) %reduce-scatter.13.cloned.1.call-update) | async-done | bytes 524304 | tf_op jit(solution)/shard_map/reduce_scatter | solution.py:673
  512.8 52.7 %reduce-scatter.11.cloned.1.call-done = bf16[256,1024]{1,0:T(8,128)(2,1)} async-done(((bf16[2048,1024]{1,0:T(8,128)(2,1)}), bf16[256,1024]{1,0:T(8,128)(2,1)}) %reduce-scatter.11.cloned.1.call-update) | async-done | bytes 524304 | tf_op jit(solution)/shard_map/reduce_scatter | solution.py:674
  567.6 11.2 %fusion.47 = f32[1024,2048]{1,0:T(8,128)} fusion(bf16[1024,1024]{1,0:T(8,128)(2,1)} %get-tuple-element.40, bf16[1024,2048]{1,0:T(8,128)(2,1)} %param.33), kind=kOutput, calls=%fused_computation.109 | convolution fusion | flops 4294967296 | bytes 14680064 | tf_op jit(solution)/shard_map/dot_general | solution.py:26
  585.7 34.4 %reduce-scatter.17.cloned.1.call-done = bf16[128,2048]{1,0:T(8,128)(2,1)} async-done(((bf16[1024,2048]{1,0:T(8,128)(2,1)}), bf16[128,2048]{1,0:T(8,128)(2,1)}) %reduce-scatter.17.cloned.1.call-update) | async-done | bytes 524304 | tf_op jit(solution)/shard_map/reduce_scatter | solution.py:673
  622.6 11.0 %fusion.48 = f32[1024,2048]{1,0:T(8,128)} fusion(bf16[1024,1024]{1,0:T(8,128)(2,1)} %copy-done.13, bf16[2048,1024]{1,0:T(8,128)(2,1)} %param.21), kind=kOutput, calls=%fused_computation.110 | convolution fusion | flops 4294967296 | bytes 14680064 | tf_op jit(solution)/shard_map/dot_general | solution.py:30
  639.4 35.9 %reduce-scatter.15.cloned.1.call-done = bf16[128,2048]{1,0:T(8,128)(2,1)} async-done(((bf16[1024,2048]{1,0:T(8,128)(2,1)}), bf16[128,2048]{1,0:T(8,128)(2,1)}) %reduce-scatter.15.cloned.1.call-update) | async-done | bytes 524304 | tf_op jit(solution)/shard_map/reduce_scatter | solution.py:674
  677.3 10.9 %fusion.50 = f32[1024,2048]{1,0:T(8,128)} fusion(bf16[1024,1024]{1,0:T(8,128)(2,1)} %copy-done.12, bf16[2048,1024]{1,0:T(8,128)(2,1)} %all-gather.9.cloned.1.call-done), kind=kOutput, calls=%fused_computation.112 | convolution fusion | flops 4294967296 | bytes 14680064 | tf_op jit(solution)/shard_map/dot_general | solution.py:30
  688.2 16.2 %add_convert_fusion = bf16[1024,2048]{1,0:T(8,128)(2,1)} fusion(f32[1024,2048]{1,0:T(8,128)} %fusion.50, f32[1024,2048]{1,0:T(8,128)} %fusion.49, f32[1024,2048]{1,0:T(8,128)} %fusion.15, f32[1024,2048]{1,0:T(8,128)} %fusion.48, bf16[1024,1024]{1,0:T(8,128)(2,1)S(1)} %copy-done.31, bf16[2048,1024]{1,0:T(8,128)(2,1)} %all-gather.7.cloned.1.call-done), kind=kOutput, calls=%fused_computation.6 | convolution fusion | flops 4305453056 | bytes 44040192 | tf_op jit(solution)/shard_map/dot_general | solution.py:30
  736.0 132.5 %all-reduce.11.cloned.1.call-done = bf16[2048,256]{0,1:T(8,128)(2,1)} async-done(((bf16[2048,256]{0,1:T(8,128)(2,1)}), bf16[2048,256]{0,1:T(8,128)(2,1)}) %all-reduce.11.cloned.1.call-update) | async-done | bytes 1048592 | tf_op jit(solution)/shard_map/psum | solution.py:682
  874.8 39.4 %all-reduce.5 = (f32[2048]{0:T(1024)}, f32[8,256]{1,0:T(8,128)S(1)}) all-reduce(f32[2048]{0:T(1024)S(1)} %get-tuple-element.124, f32[8,256]{1,0:T(8,128)S(1)} %get-tuple-element.59), channel_id=1, replica_groups=mesh['batch'=8,'head'=4] {'batch','head'}, use_global_device_ids=true, to_apply=%region_7.8 | all-reduce | flops 4096 | bytes 32768 | tf_op jit(solution)/shard_map/psum | solution.py:702
  929.6 15.7 %all-gather.15.cloned.1.call-done = bf16[2048,1024]{1,0:T(8,128)(2,1)} async-done(((bf16[256,1024]{1,0:T(8,128)(2,1)}), bf16[2048,1024]{1,0:T(8,128)(2,1)}) %all-gather.15.cloned.1.call-update) | async-done | bytes 4194320 | tf_op jit(solution)/shard_map/all_gather | solution.py:676
  952.0 32.0 %all-gather.17.cloned.1.call-done = bf16[1024,2048]{1,0:T(8,128)(2,1)} async-done(((bf16[128,2048]{1,0:T(8,128)(2,1)}), bf16[1024,2048]{1,0:T(8,128)(2,1)}) %all-gather.17.cloned.1.call-update) | async-done | bytes 4194320 | tf_op jit(solution)/shard_map/all_gather | solution.py:676
  (291 shorter events, 253.8 us)
Async XLA Ops:
  7.2 230.6 %all-gather.7.cloned.1.call-start = ((), (), s32[]{:S(2)}) async-start(), calls=%async_computation.6 | async-start | bytes 4718592 | tf_op jit(solution)/shard_map/all_gather | solution.py:575
  8.4 27.3 %collective-permute-start.3 = (bf16[256,1024]{1,0:T(8,128)(2,1)S(1)}, bf16[256,1024]{1,0:T(8,128)(2,1)S(1)}, u32[]{:S(2)}, u32[]{:S(2)}) collective-permute-start(bf16[256,1024]{1,0:T(8,128)(2,1)S(1)} %constant_dynamic-slice_fusion.2), channel_id=1, source_target_pairs={{0,2},{1,3},{2,0},{3,1},{4,6},{5,7},{6,4},{7,5},{8,10},{9,11},{10,... | collective-permute-start | bytes 1572872 | tf_op jit(solution)/shard_map/ppermute | solution.py:546
  36.5 210.6 %all-gather.9.cloned.1.call-start = ((), (), s32[]{:S(2)}) async-start(), calls=%async_computation.7 | async-start | bytes 4718592 | tf_op jit(solution)/shard_map/all_gather | solution.py:575
  63.9 214.9 %all-gather.11.cloned.1.call-start = ((), (), s32[]{:S(2)}) async-start(), calls=%async_computation.8 | async-start | bytes 4718592 | tf_op jit(solution)/shard_map/all_gather | solution.py:575
  63.9 112.3 %collective-permute-start = (bf16[512,2048]{1,0:T(8,128)(2,1)}, bf16[512,2048]{1,0:T(8,128)(2,1)}, u32[]{:S(2)}, u32[]{:S(2)}) collective-permute-start(bf16[512,2048]{1,0:T(8,128)(2,1)} %param.18), channel_id=1, source_target_pairs={{0,1},{1,0},{2,3},{3,2},{4,5},{5,4},{6,7},{7,6},{8,9},{9,8},{10,11... | collective-permute-start | bytes 6291464 | tf_op jit(solution)/shard_map/ppermute | solution.py:546
  65.2 113.4 %collective-permute-start.1 = (bf16[16,2048]{0,1:T(8,128)(2,1)S(1)}, bf16[16,2048]{0,1:T(8,128)(2,1)S(1)}, u32[]{:S(2)}, u32[]{:S(2)}) collective-permute-start(bf16[16,2048]{0,1:T(8,128)(2,1)S(1)} %bitcast.98), channel_id=1, source_target_pairs={{0,2},{1,3},{2,0},{3,1},{4,6},{5,7},{6,4},{7,5},{8,10},{9,11},{10,... | collective-permute-start | bytes 196616 | tf_op jit(solution)/shard_map/ppermute | solution.py:546
  69.3 53.0 %collective-permute-start.2 = (f32[8,1024]{1,0:T(8,128)S(1)}, f32[8,1024]{1,0:T(8,128)S(1)}, u32[]{:S(2)}, u32[]{:S(2)}) collective-permute-start(f32[8,1024]{1,0:T(8,128)S(1)} %concatenate.72), channel_id=1, source_target_pairs={{0,2},{1,3},{2,0},{3,1},{4,6},{5,7},{6,4},{7,5},{8,10},{9,11},{10,... | collective-permute-start | bytes 98312 | tf_op jit(solution)/shard_map/ppermute | solution.py:546
  70.5 118.4 %collective-permute-start.7 = (bf16[512,2048]{1,0:T(8,128)(2,1)}, bf16[512,2048]{1,0:T(8,128)(2,1)}, u32[]{:S(2)}, u32[]{:S(2)}) collective-permute-start(bf16[512,2048]{1,0:T(8,128)(2,1)} %param.19), channel_id=1, source_target_pairs={{0,1},{1,0},{2,3},{3,2},{4,5},{5,4},{6,7},{7,6},{8,9},{9,8},{10,11... | collective-permute-start | bytes 6291464 | tf_op jit(solution)/shard_map/ppermute | solution.py:546
  74.4 101.7 %collective-permute-start.5 = (bf16[128,2048]{1,0:T(8,128)(2,1)}, bf16[128,2048]{1,0:T(8,128)(2,1)}, u32[]{:S(2)}, u32[]{:S(2)}) collective-permute-start(bf16[128,2048]{1,0:T(8,128)(2,1)} %constant_dynamic-slice_fusion), channel_id=1, source_target_pairs={{0,2},{1,3},{2,0},{3,1},{4,6},{5,7},{6,4},{7,5},{8,10},{9,11},{10,... | collective-permute-start | bytes 1572872 | tf_op jit(solution)/shard_map/ppermute | solution.py:546
  176.2 292.3 %reduce-scatter.9.cloned.1.call-start = ((), (), s32[]{:S(2)}) async-start(), calls=%async_computation.10 | async-start | bytes 4718592 | tf_op jit(solution)/shard_map/reduce_scatter | solution.py:673
  349.4 122.3 %reduce-scatter.7.cloned.1.call-start = ((), (), s32[]{:S(2)}) async-start(), calls=%async_computation.9 | async-start | bytes 4718592 | tf_op jit(solution)/shard_map/reduce_scatter | solution.py:674
  403.8 106.6 %reduce-scatter.13.cloned.1.call-start = ((), (), s32[]{:S(2)}) async-start(), calls=%async_computation.13 | async-start | bytes 4718592 | tf_op jit(solution)/shard_map/reduce_scatter | solution.py:673
  414.2 151.2 %reduce-scatter.11.cloned.1.call-start = ((), (), s32[]{:S(2)}) async-start(), calls=%async_computation.12 | async-start | bytes 4718592 | tf_op jit(solution)/shard_map/reduce_scatter | solution.py:674
  424.8 195.4 %reduce-scatter.17.cloned.1.call-start = ((), (), s32[]{:S(2)}) async-start(), calls=%async_computation.18 | async-start | bytes 4718592 | tf_op jit(solution)/shard_map/reduce_scatter | solution.py:673
  435.5 239.8 %reduce-scatter.15.cloned.1.call-start = ((), (), s32[]{:S(2)}) async-start(), calls=%async_computation.17 | async-start | bytes 4718592 | tf_op jit(solution)/shard_map/reduce_scatter | solution.py:674
  445.2 285.0 %all-reduce.9.cloned.1.call-start = ((), (), s32[]{:S(2)}) async-start(), calls=%async_computation.15 | async-start | bytes 327680 | tf_op jit(solution)/shard_map/psum | solution.py:695
  468.4 400.1 %all-reduce.11.cloned.1.call-start = ((), (), s32[]{:S(2)}) async-start(), calls=%async_computation.16 | async-start | bytes 2097152 | tf_op jit(solution)/shard_map/psum | solution.py:682
  471.6 451.4 %all-gather.13.cloned.1.call-start = ((), (), s32[]{:S(2)}) async-start(), calls=%async_computation.11 | async-start | bytes 4718592 | tf_op jit(solution)/shard_map/all_gather | solution.py:676
  492.6 452.7 %all-gather.15.cloned.1.call-start = ((), (), s32[]{:S(2)}) async-start(), calls=%async_computation.14 | async-start | bytes 4718592 | tf_op jit(solution)/shard_map/all_gather | solution.py:676
  510.4 55.1 %collective-permute-start.11 = (bf16[256,1024]{1,0:T(8,128)(2,1)}, bf16[256,1024]{1,0:T(8,128)(2,1)S(1)}, u32[]{:S(2)}, u32[]{:S(2)}) collective-permute-start(bf16[256,1024]{1,0:T(8,128)(2,1)} %reduce-scatter.13.cloned.1.call-done), channel_id=1, source_target_pairs={{0,2},{1,3},{2,0},{3,1},{4,6},{5,7},{6,4},{7,5},{8,10},{9,11},{10,... | collective-permute-start | bytes 1572872 | tf_op jit(solution)/shard_map/ppermute | solution.py:546
  567.5 416.5 %all-gather.17.cloned.1.call-start = ((), (), s32[]{:S(2)}) async-start(), calls=%async_computation.19 | async-start | bytes 4718592 | tf_op jit(solution)/shard_map/all_gather | solution.py:676
  620.2 55.1 %collective-permute-start.13 = (bf16[128,2048]{1,0:T(8,128)(2,1)}, bf16[128,2048]{1,0:T(8,128)(2,1)S(1)}, u32[]{:S(2)}, u32[]{:S(2)}) collective-permute-start(bf16[128,2048]{1,0:T(8,128)(2,1)} %reduce-scatter.17.cloned.1.call-done), channel_id=1, source_target_pairs={{0,2},{1,3},{2,0},{3,1},{4,6},{5,7},{6,4},{7,5},{8,10},{9,11},{10,... | collective-permute-start | bytes 1572872 | tf_op jit(solution)/shard_map/ppermute | solution.py:546
  707.7 163.3 %collective-permute-start.9 = (bf16[512,2048]{1,0:T(8,128)(2,1)}, bf16[512,2048]{1,0:T(8,128)(2,1)}, u32[]{:S(2)}, u32[]{:S(2)}) collective-permute-start(bf16[512,2048]{1,0:T(8,128)(2,1)} %slice.215), channel_id=1, source_target_pairs={{0,1},{1,0},{2,3},{3,2},{4,5},{5,4},{6,7},{7,6},{8,9},{9,8},{10,11... | collective-permute-start | bytes 6291464 | tf_op jit(solution)/shard_map/ppermute | solution.py:546
  720.5 195.0 %collective-permute-start.6 = (bf16[512,2048]{1,0:T(8,128)(2,1)}, bf16[512,2048]{1,0:T(8,128)(2,1)}, u32[]{:S(2)}, u32[]{:S(2)}) collective-permute-start(bf16[512,2048]{1,0:T(8,128)(2,1)} %slice.206), channel_id=1, source_target_pairs={{0,1},{1,0},{2,3},{3,2},{4,5},{5,4},{6,7},{7,6},{8,9},{9,8},{10,11... | collective-permute-start | bytes 6291464 | tf_op jit(solution)/shard_map/ppermute | solution.py:546
  (64 other events, 1935.2 us)
Sparse Core Ops, SparseCore 0:
  36.6 37.8 all-gather.6
  77.0 36.7 all-gather.8
  176.3 37.9 all-gather.10
  349.5 50.7 reduce-scatter.8
  404.5 51.3 reduce-scatter.6
  459.1 51.2 reduce-scatter.12
  514.1 51.3 reduce-scatter.10
  568.8 51.2 reduce-scatter.16
  623.9 51.3 reduce-scatter.14
  678.2 51.8 all-reduce.8
  735.3 133.1 all-reduce.10
  870.4 36.1 all-gather.12
  908.6 36.7 all-gather.14
  947.3 36.7 all-gather.16

commit v2 on v1

--- a/solution.py
+++ b/solution.py
@@ -16,10 +16,20 @@
 CHUNKS = SEQ_LEN // SPAN
 WIDE = 256
 GROUP = WIDE // HEAD_DIM
+STRIP = 128
+BELOW = [(k * STRIP, -(-(k + 1) * STRIP // 128) * 128) for k in range(SPAN // STRIP)]
+ABOVE = [(k * STRIP, k * STRIP // 128 * 128) for k in range(SPAN // STRIP)]
 EPSILON = 1e-05
 F32 = jnp.float32
 BF16 = jnp.bfloat16
 VMEM_LIMIT = 48 * 1024 * 1024
+
+
+PACE = 0.01e9
+
+
+def lasting(us):
+    return pl.CostEstimate(flops=int(us * PACE), bytes_accessed=1000, transcendentals=0)
 
 
 def dot_nn(a, b):
@@ -112,7 +122,7 @@
 
 
 def fwd_kernel(
-    per_block, info, inner, gate, bc, bct, hs, par, y_out, yg_out, st_out, ss_out, score_scr, state_scr
+    per_block, info, inner, gate, bc, bct, hs, par, y_out, mk_out, yg_out, st_out, ss_out, score_scr, state_scr
 ):
     taps = [par[k : k + 1, :] for k in range(CONV)]
     bias, skip, gain, act = par[4:5, :], par[5:6, :], par[6:7, :], par[7:8, :]
@@ -161,14 +171,21 @@
             tile = carried[:, p * 128 : (p + 1) * 128]
             for s in range(2):
                 h = 2 * p + s
-                decays = jnp.exp(jnp.minimum(cum[:, h : h + 1] - cum_rows[h : h + 1, :], 0.0))
-                mixing = (decays * score_scr[c]).astype(BF16)
-                tile = tile + dot_nn(mixing, xs[:, p * 128 : (p + 1) * 128] * sides[s])
+                values = xs[:, p * 128 : (p + 1) * 128] * sides[s]
+                strips = []
+                for at, end in BELOW:
+                    gap = cum[at : at + STRIP, h : h + 1] - cum_rows[h : h + 1, :end]
+                    decays = jnp.exp(jnp.minimum(gap, 0.0))
+                    mixing = (decays * score_scr[c, at : at + STRIP, :end]).astype(BF16)
+                    strips.append(dot_nn(mixing, values[:end]))
+                tile = tile + jnp.concatenate(strips, axis=0)
             tiles.append(tile)
         y = jnp.concatenate(tiles, axis=1)
         y_out[pl.ds(r0, SPAN), :] = y.astype(BF16)
         g = gate[pl.ds(r0, SPAN), :].astype(F32)
-        gated = (y + skip * xf) * act * (g * sigmoid(g))
+        masked = (y + skip * xf) * act
+        mk_out[pl.ds(r0, SPAN), :] = masked.astype(BF16)
+        gated = masked * (g * sigmoid(g))
         yg_out[pl.ds(r0, SPAN), :] = (gated * gain).astype(BF16)
         square = gated * gated
         ss_out[pl.ds(r0, SPAN), :] += square[:, :128] + square[:, 128:]
@@ -177,6 +194,26 @@
 def split_low(v):
     high = v.astype(BF16)
     return high, (v - high.astype(F32)).astype(BF16)
+
+
+def gate_kernel(mk, gate, dn_in, sk, par, dgate_out, dy_out, gg_out):
+    gain, act = par[6:7, :], par[7:8, :]
+    total = jnp.zeros((1, WIDE), F32)
+    for c in range(CHUNKS):
+        rows = pl.ds(c * SPAN, SPAN)
+        row_cols = sk[:, c * SPAN : (c + 1) * SPAN].T
+        scale, fix = row_cols[:, 0:1], row_cols[:, 1:2]
+        g = gate[rows, :].astype(F32)
+        sg = sigmoid(g)
+        sw = g * sg
+        masked = mk[rows, :].astype(F32)
+        gated = masked * sw
+        d_scale = dn_in[rows, :].astype(F32) * scale
+        d_gated = d_scale * gain - gated * fix
+        dgate_out[rows, :] = (d_gated * masked * sg * (1.0 + g * (1.0 - sg))).astype(BF16)
+        dy_out[rows, :] = (d_gated * sw * act).astype(BF16)
+        total = total + jnp.sum(d_scale * gated, axis=0, keepdims=True)
+    gg_out[...] = total + jnp.zeros((8, WIDE), F32)
 
 
 def bwd_kernel(
@@ -184,16 +221,13 @@
     blocks,
     info,
     inner,
-    gate,
     y_in,
-    dn_in,
+    dy_in,
     bc,
     bct,
     hs,
-    sk,
     st,
     par,
-    dgate_out,
     dinner_out,
     dbc_out,
     gp_out,
@@ -204,7 +238,7 @@
     adj_scr,
 ):
     taps = [par[k : k + 1, :] for k in range(CONV)]
-    bias, skip, gain, act = par[4:5, :], par[5:6, :], par[6:7, :], par[7:8, :]
+    bias, skip = par[4:5, :], par[5:6, :]
     lane = lax.broadcasted_iota(jnp.int32, (1, 128), 1)
     sides = [(lane < HEAD_DIM).astype(BF16), (lane >= HEAD_DIM).astype(BF16)]
     head_of = lax.broadcasted_iota(jnp.int32, (8, WIDE), 1) // HEAD_DIM
@@ -251,23 +285,10 @@
         step_wide = expand(step)
         xs = (xf * step_wide).astype(BF16)
         xw = (xf * expand(tail * step)).astype(BF16)
-        row_cols = sk[:, pl.ds(r0, SPAN)].T
-        scale, fix = row_cols[:, 0:1], row_cols[:, 1:2]
-
-        g = gate[pl.ds(r0, SPAN), :].astype(F32)
-        sg = sigmoid(g)
-        sw = g * sg
         y = y_in[pl.ds(r0, SPAN), :].astype(F32)
-        dn = dn_in[pl.ds(r0, SPAN), :].astype(F32)
-        masked = (y + skip * xf) * act
-        gated = masked * sw
-        d_scale = dn * scale
-        d_gated = d_scale * gain - gated * fix
-        dgate_out[pl.ds(r0, SPAN), :] = (d_gated * masked * sg * (1.0 + g * (1.0 - sg))).astype(BF16)
-        dy_low = (d_gated * sw * act).astype(BF16)
+        dy_low = dy_in[pl.ds(r0, SPAN), :]
         dy = dy_low.astype(F32)
         dy_entry = (dy * expand(entry)).astype(BF16)
-        g_gain = jnp.sum(d_scale * gated, axis=0, keepdims=True)
 
         adj = adj_scr[...]
         adj_low = adj.astype(BF16)
@@ -278,7 +299,6 @@
         carried = dot_nn(bcv[:, :STATE], adj_low) * expand(tail)
         adj_scr[...] = adj * expand(keep) + dot_nn(bct[STATE:, pl.ds(r0, SPAN)], dy_entry)
 
-        pair_sum = pair_scr[c]
         tiles = []
         for p in range(WIDE // 128):
             tile = carried[:, p * 128 : (p + 1) * 128]
@@ -286,19 +306,25 @@
             xs_tile = xs[:, p * 128 : (p + 1) * 128]
             for s in range(2):
                 h = 2 * p + s
-                decays = jnp.exp(jnp.minimum(cum_rows[h : h + 1, :] - cum[:, h : h + 1], 0.0))
-                mixing = (decays * score_scr[c]).astype(BF16)
-                tile = tile + dot_nn(mixing, dy_tile * sides[s])
-                pair_sum = pair_sum + decays * dot_nt(xs_tile * sides[s], dy_tile)
+                dy_side = dy_tile * sides[s]
+                xs_side = xs_tile * sides[s]
+                strips = []
+                for at, begin in ABOVE:
+                    rows = slice(at, at + STRIP)
+                    gap = cum_rows[h : h + 1, begin:] - cum[rows, h : h + 1]
+                    decays = jnp.exp(jnp.minimum(gap, 0.0))
+                    mixing = (decays * score_scr[c, rows, begin:]).astype(BF16)
+                    strips.append(dot_nn(mixing, dy_side[begin:]))
+                    pair_scr[c, rows, begin:] += decays * dot_nt(xs_side[rows], dy_tile[begin:])
+                tile = tile + jnp.concatenate(strips, axis=0)
             tiles.append(tile)
-        pair_scr[c] = pair_sum
         dxu = jnp.concatenate(tiles, axis=1)
 
         du = (step_wide * dxu + skip * dy) * (su * (1.0 + u * (1.0 - su)))
         dinner_out[pl.ds(r0, SPAN), :] = conv_back(du, after, taps, masks_after).astype(BF16)
         after = du[:8]
         sums = [jnp.sum(du * lags[k] * masks[k], axis=0, keepdims=True) for k in range(CONV)]
-        sums += [jnp.sum(du, axis=0, keepdims=True), jnp.zeros((1, WIDE), F32), g_gain, jnp.zeros((1, WIDE), F32)]
+        sums += [jnp.sum(du, axis=0, keepdims=True), jnp.zeros((3, WIDE), F32)]
         gp = gp + jnp.concatenate(sums, axis=0)
 
         q1h, q1l = split_low(dy * y)
@@ -363,7 +389,20 @@
     return pl.BlockSpec((rows, WIDE), lambda i, info: (0, i))
 
 
-def call(kernel, grid, in_specs, out_specs, out_shape, scratch, flops, moved, info, *operands):
+def ignore(kernel, at, count):
+    if not count:
+        return kernel
+    return lambda *refs: kernel(*refs[:at], *refs[at + count :])
+
+
+def unread(later):
+    return [pl.BlockSpec(memory_space=pl.ANY) for _ in later]
+
+
+def call(kernel, grid, in_specs, out_specs, out_shape, scratch, us, info, *operands, later=()):
+    kernel = ignore(kernel, 1 + len(operands), len(later))
+    in_specs = [*in_specs, *unread(later)]
+    operands = [*operands, *later]
     return pl.pallas_call(
         kernel,
         grid_spec=pltpu.PrefetchScalarGridSpec(
@@ -375,12 +414,191 @@
         ),
         out_shape=out_shape,
         compiler_params=pltpu.CompilerParams(vmem_limit_bytes=VMEM_LIMIT),
-        cost_estimate=pl.CostEstimate(flops=flops, bytes_accessed=moved, transcendentals=0),
+        cost_estimate=lasting(us),
     )(info, *operands)
 
 
 def shape(dims, kind):
     return jax.ShapeDtypeStruct(dims, kind)
+
+
+def project(a, b, kind, later):
+    rows, depth = a.shape
+    b, number = b if isinstance(b, tuple) else (b, 0)
+    columns = b.shape[-1]
+    wide = min(columns, 512)
+    block = pl.BlockSpec((depth, wide), lambda j: (0, j))
+    if b.ndim == 4:
+        block = pl.BlockSpec((b.shape[0], 1, b.shape[2], wide), lambda j: (0, number, 0, j))
+
+    def kernel(x, w, out):
+        out[...] = dot_nn(x[...], w[...].reshape(depth, wide)).astype(kind)
+
+    return pl.pallas_call(
+        ignore(kernel, 2, len(later)),
+        grid=(columns // wide,),
+        in_specs=[
+            pl.BlockSpec((rows, depth), lambda j: (0, 0)),
+            block,
+            *unread(later),
+        ],
+        out_specs=pl.BlockSpec((rows, wide), lambda j: (0, j)),
+        out_shape=shape((rows, columns), kind),
+        compiler_params=pltpu.CompilerParams(vmem_limit_bytes=VMEM_LIMIT),
+        cost_estimate=lasting(6),
+    )(a, b, *later)
+
+
+def project_few(a, b, later):
+    rows, depth = a.shape
+    columns = b.shape[1]
+
+    def kernel(x, w, out):
+        out[...] = dot_nn(x[...], w[...])
+
+    return pl.pallas_call(
+        ignore(kernel, 2, len(later)),
+        grid=(rows // 256,),
+        in_specs=[
+            pl.BlockSpec((256, depth), lambda i: (i, 0)),
+            pl.BlockSpec((depth, columns), lambda i: (0, 0)),
+            *unread(later),
+        ],
+        out_specs=pl.BlockSpec((256, columns), lambda i: (i, 0)),
+        out_shape=shape((rows, columns), F32),
+        compiler_params=pltpu.CompilerParams(vmem_limit_bytes=VMEM_LIMIT),
+        cost_estimate=lasting(3),
+    )(a, b, *later)
+
+
+def project_back(up, w, yg, later):
+    rows, depth = up.shape
+    columns = w.shape[0]
+    wide = min(columns, 512)
+
+    def kernel(x, b, y, out, sums):
+        value = dot_nt(x[...], b[...])
+        out[...] = value.astype(BF16)
+        value = value * y[...].astype(F32)
+        total = value[:, :128]
+        for k in range(1, wide // 128):
+            total = total + value[:, k * 128 : (k + 1) * 128]
+
+        @pl.when(pl.program_id(0) == 0)
+        def _():
+            sums[...] = total
+
+        @pl.when(pl.program_id(0) > 0)
+        def _():
+            sums[...] += total
+
+    return pl.pallas_call(
+        ignore(kernel, 3, len(later)),
+        grid=(columns // wide,),
+        in_specs=[
+            pl.BlockSpec((rows, depth), lambda j: (0, 0)),
+            pl.BlockSpec((wide, depth), lambda j: (j, 0)),
+            pl.BlockSpec((rows, wide), lambda j: (0, j)),
+            *unread(later),
+        ],
+        out_specs=[pl.BlockSpec((rows, wide), lambda j: (0, j)), pl.BlockSpec((rows, 128), lambda j: (0, 0))],
+        out_shape=[shape((rows, columns), BF16), shape((rows, 128), F32)],
+        compiler_params=pltpu.CompilerParams(vmem_limit_bytes=VMEM_LIMIT),
+        cost_estimate=lasting(8),
+    )(up, w, yg, *later)
+
+
+def rows_forward(lefts, rights, first, rows, later=()):
+    columns = rights[0].shape[1]
+    wide = 512
+    count = len(lefts)
+    start = first // rows
+
+    def kernel(*refs):
+        total = dot_nn(refs[0][...], refs[count][...])
+        for n in range(1, count):
+            total = total + dot_nn(refs[n][...], refs[count + n][...])
+        refs[-1][...] = total.astype(BF16)
+
+    return pl.pallas_call(
+        ignore(kernel, 2 * count, len(later)),
+        grid=(columns // wide,),
+        in_specs=[pl.BlockSpec((rows, v.shape[1]), lambda j: (start, 0)) for v in lefts]
+        + [pl.BlockSpec((v.shape[0], wide), lambda j: (0, j)) for v in rights]
+        + unread(later),
+        out_specs=pl.BlockSpec((rows, wide), lambda j: (0, j)),
+        out_shape=shape((rows, columns), BF16),
+        compiler_params=pltpu.CompilerParams(vmem_limit_bytes=VMEM_LIMIT),
+        cost_estimate=lasting(5),
+    )(*lefts, *rights, *later)
+
+
+def delayed(v, later):
+    flat = v.reshape(-1, v.shape[-1])
+    rows, width = flat.shape
+    block = rows // 2 if rows % 32 == 0 else rows
+
+    def kernel(a, out):
+        out[...] = a[...]
+
+    return pl.pallas_call(
+        ignore(kernel, 1, len(later)),
+        grid=(rows // block,),
+        in_specs=[pl.BlockSpec((block, width), lambda i: (i, 0)), *unread(later)],
+        out_specs=pl.BlockSpec((block, width), lambda i: (i, 0)),
+        out_shape=shape((rows, width), v.dtype),
+        compiler_params=pltpu.CompilerParams(vmem_limit_bytes=VMEM_LIMIT),
+        cost_estimate=lasting(2),
+    )(flat, *later).reshape(v.shape)
+
+
+def added(a, b, later):
+    def kernel(x, y, out):
+        out[...] = (x[...].astype(F32) + y[...].astype(F32)).astype(BF16)
+
+    return pl.pallas_call(
+        ignore(kernel, 2, len(later)),
+        in_specs=[pl.BlockSpec(memory_space=pltpu.VMEM)] * 2 + unread(later),
+        out_specs=pl.BlockSpec(memory_space=pltpu.VMEM),
+        out_shape=shape(a.shape, BF16),
+        compiler_params=pltpu.CompilerParams(vmem_limit_bytes=VMEM_LIMIT),
+        cost_estimate=lasting(1),
+    )(a, b, *later)
+
+
+def norm_rows(own, got, gain, later):
+    rows, width = own.shape
+    block = min(rows, 256)
+    here = rows // block
+
+    def kernel(a, b, gain_row, out):
+        def write(v):
+            v = v.astype(F32)
+            inverse = lax.rsqrt(jnp.mean(v * v, axis=1, keepdims=True) + EPSILON)
+            out[...] = (v * inverse * gain_row[...]).astype(BF16)
+
+        @pl.when(pl.program_id(0) < here)
+        def _():
+            write(a[...])
+
+        @pl.when(pl.program_id(0) >= here)
+        def _():
+            write(b[...])
+
+    return pl.pallas_call(
+        ignore(kernel, 3, len(later)),
+        grid=(SEQ_LEN // block,),
+        in_specs=[
+            pl.BlockSpec((block, width), lambda i: (jnp.minimum(i, here - 1), 0)),
+            pl.BlockSpec((block, width), lambda i: (jnp.maximum(i - here, 0), 0)),
+            pl.BlockSpec((1, width), lambda i: (0, 0)),
+            *unread(later),
+        ],
+        out_specs=pl.BlockSpec((block, width), lambda i: (i, 0)),
+        out_shape=shape((SEQ_LEN, width), BF16),
+        compiler_params=pltpu.CompilerParams(vmem_limit_bytes=VMEM_LIMIT),
+        cost_estimate=lasting(4),
+    )(own, got, gain[None], *later)
 
 
 def prep(per_block, info, pairs, par):
@@ -392,15 +610,14 @@
         [whole((t, WIDE)), whole((WIDE, t))],
         [shape((t, WIDE), BF16), shape((WIDE, t), BF16)],
         [],
-        10**9,
-        3 * 10**6,
+        2,
         info,
         pairs,
         par,
     )
 
 
-def scan_forward(per_block, info, inner, gate, bc, bct, hs, par):
+def scan_forward(per_block, info, inner, gate, bc, bct, hs, par, later):
     t, channels = inner.shape
     blocks = channels // WIDE
     return call(
@@ -414,16 +631,16 @@
             pl.BlockSpec((16, t), lambda i, info: (i, 0)),
             cols(8),
         ],
-        [cols(t), cols(t), cols(CHUNKS * STATE), whole((t, 128))],
+        [cols(t), cols(t), cols(t), cols(CHUNKS * STATE), whole((t, 128))],
         [
+            shape((t, channels), BF16),
             shape((t, channels), BF16),
             shape((t, channels), BF16),
             shape((CHUNKS * STATE, channels), BF16),
             shape((t, 128), F32),
         ],
         [pltpu.VMEM((CHUNKS, SPAN, SPAN), F32), pltpu.VMEM((STATE, WIDE), F32)],
-        blocks * 2 * 10**9,
-        10 * t * channels,
+        20,
         info,
         inner,
         gate,
@@ -431,10 +648,11 @@
         bct,
         hs,
         par,
+        later=later,
     )
 
 
-def scan_backward(per_block, info, inner, gate, y, dn, bc, bct, hs, sk, st, par):
+def scan_backward(per_block, info, inner, y, dy, bc, bct, hs, st, par, later):
     t, channels = inner.shape
     blocks = channels // WIDE
     return call(
@@ -444,23 +662,19 @@
             cols(t),
             cols(t),
             cols(t),
-            cols(t),
             whole((t, WIDE)),
             whole((WIDE, t)),
             pl.BlockSpec((16, t), lambda i, info: (i, 0)),
-            whole((8, t)),
             cols(CHUNKS * STATE),
             cols(8),
         ],
         [
-            cols(t),
             cols(t),
             whole((t, WIDE)),
             cols(8),
             pl.BlockSpec((16, t), lambda i, info: (i, 0)),
         ],
         [
-            shape((t, channels), BF16),
             shape((t, channels), BF16),
             shape((t, WIDE), F32),
             shape((8, channels), F32),
@@ -472,20 +686,250 @@
             pltpu.VMEM((CHUNKS, SPAN, SPAN), BF16),
             pltpu.VMEM((STATE, WIDE), F32),
         ],
-        blocks * 5 * 10**9,
-        16 * t * channels,
+        36,
         info,
         inner,
-        gate,
         y,
-        dn,
+        dy,
         bc,
         bct,
         hs,
-        sk,
         st,
         par,
+        later=later,
     )
+
+
+def gate_backward(mk, gate, dn, sk, par, later):
+    t, channels = gate.shape
+    block = pl.BlockSpec((t, WIDE), lambda i: (0, i))
+    small = pl.BlockSpec((8, WIDE), lambda i: (0, i))
+    return pl.pallas_call(
+        ignore(gate_kernel, 5, len(later)),
+        grid=(channels // WIDE,),
+        in_specs=[block, block, block, pl.BlockSpec((8, t), lambda i: (0, 0)), small, *unread(later)],
+        out_specs=[block, block, small],
+        out_shape=[shape((t, channels), BF16)] * 2 + [shape((8, channels), F32)],
+        compiler_params=pltpu.CompilerParams(vmem_limit_bytes=VMEM_LIMIT),
+        cost_estimate=lasting(8),
+    )(mk, gate, dn, sk, par, *later)
+
+
+def turned(number, bits):
+    return sum(((number >> k) & 1) << (bits - 1 - k) for k in range(bits))
+
+
+def grad_half(lefts, rights, half, more=None, scale=None, later=(), pieces=1, bits=0):
+    t, width = lefts[0].shape
+    columns = rights[0].shape[1]
+    count = max(len(lefts), len(rights))
+    tall = width // 2 // pieces
+    high, wide = min(width // 2, 256 if bits else 512), min(columns, 1024)
+    down, along = width // 2 // high, columns // wide
+    group = max(high // tall, 1)
+    split = max(tall // high, 1)
+    if bits and group > 1:
+        high, group = tall, 1
+        high = max(high, 128)
+        group = high // tall
+        down = width // 2 // high
+    resident = bits > 0 and group > 1
+    if resident:
+        block = pl.BlockSpec((pieces, count, tall, wide), lambda j, i, info: (0, 0, 0, j))
+    else:
+        block = pl.BlockSpec(
+            (group, count, tall // split, wide),
+            lambda j, i, info: (turned(i // split, bits) if bits else i // split, 0, i % split, j),
+        )
+    operands = [*lefts, *rights] + ([] if more is None else [more]) + ([] if scale is None else [scale])
+
+    def kernel(info, *refs):
+        out = refs[-1]
+        for n in range(count):
+            left = refs[n % len(lefts)][...]
+            if scale is not None:
+                left = (left.astype(F32) * refs[-2][...].T[:, 0:1]).astype(BF16)
+            total = dot_tn(left, refs[len(lefts) + n % len(rights)][...])
+            for g in range(group):
+                rows = total if group == 1 else total[g * tall : (g + 1) * tall]
+                at = turned(pl.program_id(1) * group + g, bits) if resident else g
+                if more is not None:
+                    rows = rows + refs[len(lefts) + len(rights)][at, n].astype(F32)
+                out[at, n] = rows.astype(BF16)
+
+    return pl.pallas_call(
+        ignore(kernel, 1 + len(operands), len(later)),
+        grid_spec=pltpu.PrefetchScalarGridSpec(
+            num_scalar_prefetch=1,
+            grid=(along, down),
+            in_specs=[pl.BlockSpec((t, high), lambda j, i, info: (0, info[0] * down + i)) for _ in lefts]
+            + [pl.BlockSpec((t, wide), lambda j, i, info: (0, j)) for _ in rights]
+            + ([] if more is None else [block])
+            + ([] if scale is None else [pl.BlockSpec((8, t), lambda j, i, info: (0, 0))])
+            + unread(later),
+            out_specs=block,
+        ),
+        out_shape=shape((pieces, count, tall, columns), BF16),
+        compiler_params=pltpu.CompilerParams(vmem_limit_bytes=VMEM_LIMIT),
+        cost_estimate=lasting(7),
+    )(half[None], *operands, *later)
+
+
+def grad_pieces(left, right, shared, batches, bits):
+    t, width = left.shape
+    columns = right.shape[1]
+    chips = batches // 2
+    tall = width // batches // 2
+    high = 256
+    group = high // tall
+
+    extra = 0 if shared is None else shared.shape[1]
+
+    def kernel(a, b, *refs):
+        out = refs[-1]
+        total = dot_tn(a[...], b[...]).astype(BF16)
+        for g in range(group):
+            block = pl.program_id(0) * group + g
+            core, quarter, number = block // (2 * chips), (block // chips) % 2, block % chips
+            chip = jnp.where(quarter == 0, number, turned(number, bits))
+            rows = pl.ds(pl.multiple_of(quarter * tall, tall), tall)
+            out[chip * 2 + core, rows, :] = total[g * tall : (g + 1) * tall]
+
+        if extra:
+
+            @pl.when(pl.program_id(0) == width // high - 1)
+            def _():
+                out[:, 2 * tall :, :] = refs[0][...]
+
+    return pl.pallas_call(
+        kernel,
+        grid=(width // high,),
+        in_specs=[
+            pl.BlockSpec((t, high), lambda i: (0, i)),
+            pl.BlockSpec((t, columns), lambda i: (0, 0)),
+        ]
+        + ([pl.BlockSpec(shared.shape, lambda i: (0, 0, 0))] if extra else []),
+        out_specs=pl.BlockSpec((batches, 2 * tall + extra, columns), lambda i: (0, 0, 0)),
+        out_shape=shape((batches, 2 * tall + extra, columns), BF16),
+        compiler_params=pltpu.CompilerParams(vmem_limit_bytes=VMEM_LIMIT),
+        cost_estimate=lasting(10),
+    )(left, right, *([shared] if extra else []))
+
+
+def place_pieces(v, tall, bits, later):
+    batches, _, columns = v.shape
+    chips = batches // 2
+
+    half = chips * tall
+    wide = columns // 4
+
+    def kernel(a, out):
+        for core in range(2):
+            for chip in range(chips):
+                v = a[chip * 2 + core]
+                for quarter, number in ((0, chip), (1, turned(chip, bits))):
+                    at = (core * 2 + quarter) * half + number * tall
+                    out[at : at + tall, :] = v[quarter * tall : (quarter + 1) * tall].astype(F32)
+
+    return pl.pallas_call(
+        ignore(kernel, 1, len(later)),
+        grid=(4,),
+        in_specs=[pl.BlockSpec((batches, 2 * tall, wide), lambda i: (0, 0, i)), *unread(later)],
+        out_specs=pl.BlockSpec((4 * half, wide), lambda i: (0, i)),
+        out_shape=shape((4 * half, columns), F32),
+        compiler_params=pltpu.CompilerParams(vmem_limit_bytes=VMEM_LIMIT),
+        cost_estimate=lasting(7),
+    )(v, *later)
+
+
+def place_halves(mine, other, core):
+    rows, columns = mine.shape
+    high = min(rows, 256)
+    per = rows // high
+
+    def kernel(info, a, b, out):
+        here = pl.program_id(0) // per == info[0]
+
+        @pl.when(here)
+        def _():
+            out[...] = a[...].astype(F32)
+
+        @pl.when(jnp.logical_not(here))
+        def _():
+            out[...] = b[...].astype(F32)
+
+    return pl.pallas_call(
+        kernel,
+        grid_spec=pltpu.PrefetchScalarGridSpec(
+            num_scalar_prefetch=1,
+            grid=(2 * per,),
+            in_specs=[
+                pl.BlockSpec((high, columns), lambda i, info: (jnp.clip(i - info[0] * per, 0, per - 1), 0)),
+                pl.BlockSpec((high, columns), lambda i, info: (jnp.clip(i - (1 - info[0]) * per, 0, per - 1), 0)),
+            ],
+            out_specs=pl.BlockSpec((high, columns), lambda i, info: (i, 0)),
+        ),
+        out_shape=shape((2 * rows, columns), F32),
+        compiler_params=pltpu.CompilerParams(vmem_limit_bytes=VMEM_LIMIT),
+        cost_estimate=lasting(6),
+    )(core[None], mine, other)
+
+
+def small_grads(left, right, later):
+    t, columns = right.shape
+    wide = 512
+
+    def kernel(a, b, out):
+        out[...] = dot_tn(a[...], b[...])
+
+    return pl.pallas_call(
+        ignore(kernel, 2, len(later)),
+        grid=(columns // wide,),
+        in_specs=[
+            pl.BlockSpec(left.shape, lambda j: (0, 0)),
+            pl.BlockSpec((t, wide), lambda j: (0, j)),
+            *unread(later),
+        ],
+        out_specs=pl.BlockSpec((left.shape[1], wide), lambda j: (0, j)),
+        out_shape=shape((left.shape[1], columns), F32),
+        compiler_params=pltpu.CompilerParams(vmem_limit_bytes=VMEM_LIMIT),
+        cost_estimate=lasting(4),
+    )(left, right, *later)
+
+
+def rows_back(lefts, rights, first, rows, gain_rows, later=()):
+    columns = rights[0].shape[0]
+    wide = 512
+
+    def right_block(v):
+        if not isinstance(v, tuple):
+            return pl.BlockSpec((wide, v.shape[1]), lambda j: (j, 0))
+        v, number = v
+        return pl.BlockSpec((wide // v.shape[2], 1, v.shape[2], v.shape[3]), lambda j: (j, number, 0, 0))
+
+    count = len(lefts)
+    start = first // rows
+
+    def kernel(*refs):
+        total = dot_nt(refs[0][...], refs[count][...].reshape(wide, -1))
+        for n in range(1, count):
+            total = total + dot_nt(refs[n][...], refs[count + n][...].reshape(wide, -1))
+        unit, out, sums = refs[-3:]
+        out[...] = total.astype(BF16)
+        sums[...] = jnp.sum(total * unit[...].astype(F32), axis=0, keepdims=True) + jnp.zeros((8, wide), F32)
+
+    return pl.pallas_call(
+        ignore(kernel, 2 * count + 1, len(later)),
+        grid=(columns // wide,),
+        in_specs=[pl.BlockSpec((rows, v.shape[1]), lambda j: (start, 0)) for v in lefts]
+        + [right_block(v) for v in rights]
+        + [pl.BlockSpec((rows, wide), lambda j: (start, j))]
+        + unread(later),
+        out_specs=[pl.BlockSpec((rows, wide), lambda j: (0, j)), pl.BlockSpec((8, wide), lambda j: (0, j))],
+        out_shape=[shape((rows, columns), BF16), shape((8, columns), F32)],
+        compiler_params=pltpu.CompilerParams(vmem_limit_bytes=VMEM_LIMIT),
+        cost_estimate=lasting(15),
+    )(*lefts, *[v[0] if isinstance(v, tuple) else v for v in rights], gain_rows, *later)
 
 
 def pair_backward(per_block, info, pairs, dbc_a, dbc_b, par):
@@ -497,8 +941,7 @@
         [whole((t, WIDE)), whole((8, WIDE))],
         [shape((t, WIDE), BF16), shape((8, WIDE), F32)],
         [],
-        10**9,
-        4 * 10**6,
+        4,
         info,
         pairs,
         dbc_a,
@@ -545,21 +988,6 @@
     def across(v, bit):
         return lax.ppermute(v, "head", [(i, i ^ bit) for i in range(stacks)])
 
-    def gather_rows(v):
-        bit = 1
-        while bit < members:
-            v = jnp.concatenate([v, across(v, bit)], axis=0)
-            bit *= 2
-        return v
-
-    def scatter_rows(v):
-        bit = members // 2
-        while bit >= 1:
-            half = v.shape[0] // 2
-            v = v[:half] + across(v[half:], bit)
-            bit //= 2
-        return v
-
     def sum_rows(v):
         bit = 1
         while bit < members:
@@ -569,16 +997,44 @@
             bit *= 2
         return v
 
-    def fetch_far(w):
-        piece = w.shape[0] // batches
-        mine = lax.dynamic_slice_in_dim(w, lot * piece, piece, 0)
-        return lax.all_gather(across(mine, far_bit), "batch", axis=0, tiled=True)
-
-    hidden_all = gather_rows(hidden_in)
-    upstream = gather_rows(out_grad)
-    w_x2 = (w_x, fetch_far(w_x))
-    w_z2 = (w_z, fetch_far(w_z))
-    w_out2 = (w_out, fetch_far(w_out))
+    chip_bits = []
+    bit = 2
+    while bit < batches:
+        chip_bits.append(bit)
+        bit *= 2
+    chips = batches // 2
+    core = lot % 2
+    chip_groups = [[2 * i + c for i in range(chips)] for c in range(2)]
+    orders = (chip_bits, chip_bits[::-1])
+
+    def planar(v, bit):
+        return lax.ppermute(v, "batch", [(i, i ^ bit) for i in range(batches)])
+
+    def side(bit):
+        return (lot // bit) % 2
+
+    def join(v, got, bit, axis=0):
+        low, high = jnp.concatenate([v, got], axis=axis), jnp.concatenate([got, v], axis=axis)
+        return jnp.where(side(bit) == 0, low, high)
+
+    def add(a, b):
+        return (a.astype(F32) + b.astype(F32)).astype(BF16)
+
+    def nothing(v):
+        return (v[(0,) * v.ndim].astype(F32) * 0.0).astype(jnp.int32)
+
+    def others(v):
+        got, bit = across(v, 1), 2
+        while bit < members:
+            got = jnp.concatenate([got, across(jnp.concatenate([v, got], axis=0), bit)], axis=0)
+            bit *= 2
+        return got
+
+    hidden_got = others(hidden_in)
+    piece = width_in // batches
+    far_parts = across(
+        jnp.concatenate([lax.dynamic_slice_in_dim(w, lot * piece, piece, 0) for w in (w_x, w_z)], axis=0), far_bit
+    )
     w_dt_own = w_dt.T
     w_dt_far = across(w_dt_own, far_bit)
     head_row = jnp.concatenate([dt_bias, a_log])
@@ -593,6 +1049,17 @@
         axis=0,
     )
     par_far = across(par_own, far_bit)
+    up_sent = delayed(out_grad, (hidden_got,))
+    normed = norm_rows(hidden_in, hidden_got, norm_gain, (far_parts, w_dt_far, par_far, up_sent))
+    far_parts = delayed(far_parts, (hidden_got, w_dt_far, par_far))
+    far_parts = delayed(far_parts, (hidden_got, w_dt_far, par_far))
+    far_both = lax.all_gather(far_parts, "batch", axis=0, tiled=True).reshape(batches, 2, piece, channels)
+    out_piece = channels // batches
+    w_out_part = across(
+        lax.dynamic_slice_in_dim(w_out, lot * out_piece + nothing(normed), out_piece, 0), far_bit
+    )
+    up_got = others(up_sent)
+    upstream = jnp.concatenate([out_grad, up_got], axis=0)
     active = (jnp.arange(channels) // HEAD_DIM < width * heads_here // (heads_here * stacks)).astype(F32)
     rate_par = [(v[7, :heads_here], v[7, heads_here : 2 * heads_here]) for v in (par_own, par_far)]
     par2 = [jnp.concatenate([v[:7], active[None]], axis=0) for v in (par_own, par_far)]
@@ -600,11 +1067,8 @@
     speed = jnp.exp(jnp.concatenate([rate_par[0][1], rate_par[1][1]]))[:, None]
     par_bc = jnp.concatenate([conv_bc, conv_bc_bias[None], jnp.zeros((3, 2 * STATE), F32)], axis=0)
 
-    residual_all = hidden_all.astype(F32)
-    inverse_all = lax.rsqrt(jnp.mean(residual_all * residual_all, axis=-1, keepdims=True) + EPSILON)
-    normed = (residual_all * inverse_all * norm_gain).astype(BF16)
     w_small = jnp.concatenate([w_bc, w_dt_own.T, w_dt_far.T], axis=1)
-    small_cols = dot_nn(normed, w_small)
+    small_cols = project_few(normed, w_small, ())
     pairs = small_cols[:, : 2 * STATE]
     rates = small_cols[:, 2 * STATE :].T
     step = jax.nn.softplus(rates + step_bias)
@@ -623,37 +1087,94 @@
     hs2 = (hs[:half], hs[half:])
     bc, bct = prep(per_block, info, pairs, par_bc)
 
-    inner2 = [dot_nn(normed, w).astype(BF16) for w in w_x2]
-    gate2 = [dot_nn(normed, w).astype(BF16) for w in w_z2]
-    forward = [
-        scan_forward(per_block, info, inner2[i], gate2[i], bc, bct, hs2[i], par2[i]) for i in range(2)
-    ]
-    y2 = [f[0] for f in forward]
-    yg2 = [f[1] for f in forward]
-    branch = scatter_rows((dot_nn(yg2[0], w_out2[0]) + dot_nn(yg2[1], w_out2[1])).astype(BF16))
-    dn2, inner_sums = [], []
-    for i in range(2):
-        dn = dot_nt(upstream, w_out2[i])
-        inner_sums.append(jnp.sum(dn * yg2[i].astype(F32), axis=1))
-        dn2.append(dn.astype(BF16))
-    square = jnp.sum(forward[0][3] + forward[1][3], axis=1)
-    sums = sum_rows(jnp.stack([square, inner_sums[0] + inner_sums[1]]))
+    inner_own = project(normed, w_x, BF16, (bc,))
+    gate_own = project(normed, w_z, BF16, (inner_own,))
+    forward_own = scan_forward(per_block, info, inner_own, gate_own, bc, bct, hs2[0], par2[0], (up_got,))
+    dn_own = project_back(upstream, w_out, forward_own[2], ())
+    w_x_far, w_z_far = (far_both, 0), (far_both, 1)
+    w_out_far = lax.all_gather(delayed(w_out_part, (forward_own[0],)), "batch", axis=0, tiled=True)
+    w_x2 = (w_x, w_x_far)
+    w_z2 = (w_z, w_z_far)
+    w_out2 = (w_out, w_out_far)
+    inner2 = (inner_own, project(normed, w_x_far, BF16, (dn_own[0],)))
+    gate2 = (gate_own, project(normed, w_z_far, BF16, (inner2[1],)))
+    forward = (forward_own, scan_forward(per_block, info, inner2[1], gate2[1], bc, bct, hs2[1], par2[1], ()))
+    y2, mk2, yg2, st2 = [[f[k] for f in forward] for k in range(4)]
+    dn_far = project_back(upstream, w_out_far, yg2[1], ())
+    dn2 = (dn_own[0], dn_far[0])
+
+    def branch_rows(first, count):
+        return rows_forward(yg2, w_out2, first, count, (dn_far[0],) if first else (give_out,))
+
+    def scatter_rows(make):
+        if members == 2:
+            give = make(rows, rows)
+            got = across(give, 1)
+            return give, got, lambda: make(0, rows).astype(F32) + got.astype(F32)
+        v = make(0, SEQ_LEN)
+        bit = members // 2
+        while bit >= 1:
+            half = v.shape[0] // 2
+            v = add(v[:half], across(v[half:], bit))
+            bit //= 2
+        return v, v, lambda: v.astype(F32)
+
+    give_out = dn_far[0]
+    branch_given, branch_got, branch = scatter_rows(branch_rows)
+    square = jnp.sum(forward[0][4] + forward[1][4], axis=1)
+    sums = sum_rows(jnp.stack([square, jnp.sum(dn_own[1] + dn_far[1], axis=1)]))
     count = (width * HEAD_DIM).astype(F32)
     scale = lax.rsqrt(sums[0] / count + EPSILON)
     fix = scale * scale * scale * sums[1] / count
     sk = jnp.concatenate([scale[None], fix[None], jnp.zeros((6, SEQ_LEN), F32)], axis=0)
 
-    scaled_up = (upstream.astype(F32) * scale[:, None]).astype(BF16)
-    mixed = (hidden_in.astype(F32) + branch.astype(F32) * scale[:rows, None]).astype(BF16)
+    bits = len(chip_bits)
+
+    def swap_halves(lefts, rights, scale=None, later=(), pieces=1, bits=0):
+        give = grad_half(lefts, rights, 1 - core, None, scale, later, pieces, bits)
+        got = planar(give, 1)
+        return give, lambda later=(): grad_half(lefts, rights, core, got, scale, later, pieces, bits)
+
+    def scatter_offloaded(mine):
+        flat = mine.reshape(-1, mine.shape[-1])
+        part = lax.psum_scatter(flat, "batch", scatter_dimension=0, tiled=True, axis_index_groups=chip_groups)
+        return part.reshape(mine.shape[1:])
+
+    def send_far(part, earlier):
+        far = lax.dynamic_slice_in_dim(part, 1 + jnp.minimum(nothing(earlier), 0), 1, 0)[0]
+        return across(far, far_bit)
+
+    def gather_both(parts, seen):
+        for step in range(bits):
+            got = [planar(v, order[step]) for v, order in zip(parts, orders)]
+            parts = [join(v, g, order[step]) for v, g, order in zip(parts, got, orders)]
+            seen.append(parts)
+        return parts, [planar(v, 1) for v in parts]
+
+    give_out, keep_out = swap_halves(yg2, [upstream], sk, (branch_given,), pieces=chips)
+    gates = [gate_backward(mk2[i], gate2[i], dn2[i], sk, par2[i], (give_out,)) for i in range(2)]
+    d_gate2 = [v[0] for v in gates]
+    mine_out = keep_out(later=(d_gate2[0],))
+    part_out = scatter_offloaded(mine_out)
+    give_z, keep_z = swap_halves([normed], d_gate2, later=(mine_out,), pieces=chips, bits=bits)
+    give_out = give_z
+    branch_sum = branch()
+    mixed = (hidden_in.astype(F32) + branch_sum * scale[:rows, None]).astype(BF16)
+    mine_z = keep_z(later=(give_z,))
+    part_z = scatter_offloaded(mine_z)
+
+    def scan_back(i, later):
+        return scan_backward(per_block, info, inner2[i], y2[i], gates[i][1], bc, bct, hs2[i], st2[i], par2[i], later)
 
     back = [None, None]
-    for i in (1, 0):
-        back[i] = scan_backward(
-            per_block, info, inner2[i], gate2[i], y2[i], dn2[i], bc, bct, hs2[i], sk, forward[i][2], par2[i]
-        )
-    d_pairs, g_bc = pair_backward(per_block, info, pairs, back[0][2], back[1][2], par_bc)
-
-    heads_out = [b[4].reshape(-1, 16, SEQ_LEN) for b in back]
+    back[1] = scan_back(1, (mine_z,))
+    far_cut = grad_pieces(normed, back[1][0], None, batches, bits)
+    far_piece = lax.psum_scatter(far_cut.reshape(-1, channels), "batch", scatter_dimension=0, tiled=True)
+    far_out = send_far(part_out, back[1][0])
+    back[0] = scan_back(0, (far_cut,))
+    total_out = added(part_out[0], far_out, (back[0][0],))
+    d_pairs, g_bc = pair_backward(per_block, info, pairs, back[0][1], back[1][1], par_bc)
+    heads_out = [b[3].reshape(-1, 16, SEQ_LEN) for b in back]
     d_step = jnp.concatenate([h[:, :GROUP].reshape(-1, SEQ_LEN) for h in heads_out], axis=0)
     skip_rows = jnp.concatenate([h[:, GROUP : 2 * GROUP].reshape(-1, SEQ_LEN) for h in heads_out], axis=0)
     d_decay = jnp.concatenate([h[:, 8 : 8 + GROUP].reshape(-1, SEQ_LEN) for h in heads_out], axis=0)
@@ -664,45 +1185,76 @@
     d_rates = d_rates_pre.astype(BF16)
     d_small = jnp.concatenate([d_pairs, d_rates.T], axis=1)
 
-    d_normed_part = dot_nt(d_small, w_small)
-    for i in range(2):
-        d_normed_part = d_normed_part + dot_nt(back[i][0], w_z2[i]) + dot_nt(back[i][1], w_x2[i])
-    d_normed_in = scatter_rows(d_normed_part.astype(BF16)).astype(F32)
-
-    def reduce_pair(own, far):
-        far_piece = lax.psum_scatter(far, "batch", scatter_dimension=0, tiled=True)
-        own_piece = lax.psum_scatter(own, "batch", scatter_dimension=0, tiled=True)
-        total = own_piece + across(far_piece, far_bit)
-        return lax.all_gather(total, "batch", axis=0, tiled=True).astype(F32)
-
-    g_w_out = reduce_pair(*[dot_tn(yg2[i], scaled_up).astype(BF16) for i in range(2)])
-    g_w_z = reduce_pair(*[dot_tn(normed, back[i][0]).astype(BF16) for i in range(2)])
-    g_w_x = reduce_pair(*[dot_tn(normed, back[i][1]).astype(BF16) for i in range(2)])
-    g_small = dot_tn(d_small, normed)
-    g_w_bc = lax.psum(g_small[: 2 * STATE].astype(BF16), ("batch", "head")).astype(F32).T
-    g_bc_total = lax.psum(g_bc, ("batch", "head"))
+    g_small = small_grads(d_small, normed, (part_z, total_out, branch_got))
 
     def pack(i):
-        gp = back[i][3]
+        gp = back[i][2]
         heads = head_grads[:, i * heads_here : (i + 1) * heads_here].reshape(-1)
         heads = jnp.pad(heads, (0, channels - heads.shape[0]))[None]
         start = 2 * STATE + i * heads_here
         return jnp.concatenate(
-            [gp[:5], heads, gp[6:7], jnp.zeros((1, channels), F32), g_small[start : start + heads_here].reshape(-1, channels)],
-            axis=0,
+            [gp[:5], heads, gates[i][2][:1], gp[7:], g_small[start : start + heads_here].reshape(-1, channels)], axis=0
         )
 
-    packed = lax.psum(pack(0) + across(pack(1), far_bit), "batch")
+    def spread(v):
+        v = jnp.pad(v.astype(BF16), ((0, -v.shape[0] % (16 * batches)), (0, 0)))
+        return v.reshape(batches, -1, channels)
+
+    far_z = send_far(part_z, g_small)
+    norm_sums = []
+
+    def normed_rows(first, count):
+        part, total = rows_back(
+            [*d_gate2, back[0][0], back[1][0], d_small],
+            [*w_z2, *w_x2, w_small],
+            first,
+            count,
+            normed,
+            (norm_sums[0], far_z) if norm_sums else (g_small,),
+        )
+        norm_sums.append(total)
+        return part
+
+    _, d_normed_got, d_normed_in = scatter_rows(normed_rows)
+    d_normed_in = d_normed_in()
+    bc_rows, few_rows = 2 * STATE * width_in // channels, 8 * 2 * STATE // channels
+    shared = spread(jnp.concatenate([g_small[: 2 * STATE].reshape(-1, channels), g_bc.reshape(-1, channels), sum(norm_sums)[:1].reshape(-1, channels)], axis=0))
+    private = spread(pack(0) + across(pack(1), far_bit))
+    own_cut = grad_pieces(normed, back[0][0], jnp.concatenate([shared, private], axis=1), batches, bits)
+    own_part = lax.psum_scatter(own_cut.reshape(-1, channels), "batch", scatter_dimension=0, tiled=True)
+    seen = []
+    total_z = added(part_z[0], far_z, (own_cut,))
+    total_out = delayed(total_out, (total_z, d_normed_got))
+    halves_here, halves_there = gather_both([total_out, total_z], seen)
+    own_part = delayed(own_part, halves_here)
+
+    cut = 2 * (width_in // batches // 2)
+    far_sent = across(delayed(far_piece, seen[0]), far_bit)
+    bc_piece = own_part[cut : cut + shared.shape[1]]
+    bit = 1
+    while bit < stacks:
+        bc_piece = add(bc_piece, across(bc_piece, bit))
+        bit *= 2
+    own_total = jnp.concatenate(
+        [add(own_part[:cut], far_sent), bc_piece, own_part[cut + shared.shape[1] :]], axis=0
+    )
+    everything = lax.all_gather(own_total, "batch", axis=0, tiled=True).reshape(batches, -1, channels)
+    g_w_out, g_w_z = [place_halves(v, got, core) for v, got in zip(halves_here, halves_there)]
+    common = everything[:, cut : cut + shared.shape[1]].reshape(-1, channels).astype(F32)
+    packed = everything[:, cut + shared.shape[1] :].reshape(-1, channels).astype(F32)
+    g_w_bc = common[:bc_rows].reshape(2 * STATE, width_in).T
+    g_bc_total = common[bc_rows : bc_rows + few_rows].reshape(8, -1)
     heads_total = packed[5]
-    g_w_dt = packed[8:].reshape(heads_here, width_in).T
+    g_w_dt = packed[8 : 8 + heads_here * width_in // channels].reshape(heads_here, width_in).T
+    g_norm = common[bc_rows + few_rows : bc_rows + few_rows + width_in // channels].reshape(-1) / norm_gain
 
     residual = hidden_in.astype(F32)
-    inverse = inverse_all[:rows]
+    inverse = lax.rsqrt(jnp.mean(residual * residual, axis=-1, keepdims=True) + EPSILON)
     unit_rows = residual * inverse
-    g_norm = lax.psum(jnp.sum(d_normed_in * unit_rows, axis=0), ("batch", "head"))
     d_unit = d_normed_in * norm_gain
     d_residual = inverse * (d_unit - unit_rows * jnp.mean(d_unit * unit_rows, axis=-1, keepdims=True))
     in_grad = (out_grad.astype(F32) + d_residual).astype(BF16)
+    g_w_x = place_pieces(everything, cut // 2, bits, (g_w_out, g_w_z, in_grad))
     return (
         mixed,
         in_grad,

time: 1010 us -> 737 us (0.73)
  waiting for transfers between devices: 502 us -> 213 us
  matrix products: 187 us -> 0.24 us
  Pallas kernels: 128 us -> 310 us
  local copies, waits for them, and re-layouts: 58.4 us -> 115 us
  blocking collectives: 39.4 us -> 0 us
    pallas_call x0 -> x33, Pallas kernels: none -> 200 us  [the longest x4 34.3 us: grad_half(): pl.pallas_call(ignore(kernel, 1 + len(operands), len(later)), grid_spec=p...]
    dot_general x21 -> x0, matrix products: 186 us -> none  [the longest x7 68.2 us: dot_nt(): lax.dot_general(a, b, (((1,), (1,)), ((), ())), preferred_element_type=F32)]
    psum x2 -> x0, waiting for transfers between devices: 142 us -> none  [the longest x1 133 us: body(): lax.psum(g_small[:2 * STATE].astype(BF16), ('batch', 'head')).astype(F32)]
    reduce_scatter x6 -> x4, waiting for transfers between devices: 141 us -> 0.03 us  [the longest x2 0.02 us: scatter_offloaded(): lax.psum_scatter(flat, 'batch', scatter_dimension=0, tiled=True, axis_ind...]
    ppermute x0 -> x8, waiting for transfers between devices: none -> 40.3 us  [planar(): return lax.ppermute(v, 'batch', [(i, i ^ bit) for i in range(batches)])]
    psum x1 -> x0, blocking collectives: 39.4 us -> none  [body(): lax.psum(jnp.sum(d_normed_in * unit_rows, axis=0), ('batch', 'head'))]
    all_gather x6 -> x3, waiting for transfers between devices: 47.7 us -> 14 us  [the longest x1 13.9 us: body(): lax.all_gather(own_total, 'batch', axis=0, tiled=True)]
    unnamed x124 -> x180, local copies, waits for them, and re-layouts: 30.5 us -> 62.7 us
  transfers between devices with their start and end apart: 28 -> 30, of which waited for: 15 -> 13; matrix products, arithmetic and copies ran while one was open for 24% -> 11% of each run, Pallas kernels for 9% -> 38%
where the time goes in v2:
time: 737 us; the launch traced here: 724 us
  Pallas kernels  310 us (42%)
  waiting for transfers between devices  213 us (29%)
  local copies, waits for them, and re-layouts  115 us (16%)
  other arithmetic  36.4 us (5%)
  starting transfers between devices  30.1 us (4%)
  between operations  19 us (3%)
    ppermute x15, waiting for transfers between devices, across(): return lax.ppermute(v, 'head', [(i, i ^ bit) for i in range(stacks)])  159 us
    pallas_call x6, Pallas kernels, call(): pl.pallas_call(kernel, grid_spec=pltpu.PrefetchScalarGridSpec(num_scalar_...  110 us
    unnamed x180, local copies, waits for them, and re-layouts  62.7 us
    ppermute x8, waiting for transfers between devices, planar(): return lax.ppermute(v, 'batch', [(i, i ^ bit) for i in range(batches)])  40.3 us
    pallas_call x4, Pallas kernels, grad_half(): pl.pallas_call(ignore(kernel, 1 + len(operands), len(later)), grid_spec=p...  34.3 us
    pallas_call x4, Pallas kernels, project(): pl.pallas_call(ignore(kernel, 2, len(later)), grid=(columns // wide,), in...  32.2 us
    pallas_call x2, Pallas kernels, rows_back(): pl.pallas_call(ignore(kernel, 2 * count + 1, len(later)), grid=(columns /...  28.8 us
    ppermute x15, starting transfers between devices, across(): return lax.ppermute(v, 'head', [(i, i ^ bit) for i in range(stacks)])  23.4 us
  transfers between devices with their start and end apart: 30, of which 13 were waited for; matrix products, arithmetic and copies ran while one was open for 11% of the time, Pallas kernels for 38%

profile of v2, /device:TPU:0, one launch (start us, length us, event | category | flops | bytes accessed | tf_op | source)
XLA Modules:
  0.0 724.3 jit_solution(16252547499784668066)
XLA Ops:
  19.0 70.5 %collective-permute-done.2 = bf16[16,2048]{0,1:T(8,128)(2,1)S(1)} collective-permute-done((bf16[16,2048]{0,1:T(8,128)(2,1)S(1)}, bf16[16,2048]{0,1:T(8,128)(2,1)S(1)}, u32[]{:S(2)}, u32[]{:S(2)}) %collective-permute-start.2) | collective-permute-done | bytes 65568 | tf_op jit(solution)/shard_map/ppermute | solution.py:989
  132.5 8.4 %shard_map.302.refs_2_.refs_1_ = bf16[1024,1024]{1,0:T(8,128)(2,1)S(1)} custom-call(bf16[1024,2048]{1,0:T(8,128)(2,1)} %shard_map.298.x.refs_0_.refs_1_.a.refs_10_, bf16[2048,1024]{1,0:T(8,128)(2,1)} %refs_5_.3, bf16[1024,1024]{1,0:T(8,128)(2,1)S(1)} %shard_map.301.refs_2_.refs_1_), custom_call_target="tpu_custom_call" | custom-call | flops 60000000 | bytes 1000 | tf_op jit(solution)/shard_map/pallas_call | solution.py:437
  143.1 12.3 %collective-permute-done.4.refs_7_ = bf16[512,2048]{1,0:T(8,128)(2,1)} collective-permute-done((bf16[512,2048]{1,0:T(8,128)(2,1)}, bf16[512,2048]{1,0:T(8,128)(2,1)}, u32[]{:S(2)}, u32[]{:S(2)}) %collective-permute-start.4) | collective-permute-done | bytes 2097184 | tf_op jit(solution)/shard_map/ppermute | solution.py:989
  155.4 19.1 %shard_map.303 = (bf16[1024,1024]{1,0:T(8,128)(2,1)S(1)}, bf16[1024,1024]{1,0:T(8,128)(2,1)}, bf16[1024,1024]{1,0:T(8,128)(2,1)}, bf16[512,1024]{1,0:T(8,128)(2,1)S(1)}, f32[1024,128]{1,0:T(8,128)S(1)}) custom-call(s32[5]{0:T(128)S(1)} %pad_add_fusion.info.refs_0_, bf16[1024,1024]{1,0:T(8,128)(2,1)} %copy-done.10, bf16[1024,1024]{1,0:T(8,128)(2,1)} %copy-done.26, ...), custom_call_target="tpu_custom_call" | custom-call | flops 200000000 | bytes 1000 | tf_op jit(solution)/shard_map/pallas_call | solution.py:406
  184.7 8.2 %shard_map.306 = (bf16[1024,1024]{1,0:T(8,128)(2,1)S(1)}, f32[1024,128]{1,0:T(8,128)S(1)}) custom-call(bf16[1024,2048]{1,0:T(8,128)(2,1)} %copy-done.68, bf16[1024,2048]{1,0:T(8,128)(2,1)} %refs_2_.3, bf16[1024,1024]{1,0:T(8,128)(2,1)S(1)} %copy-done.2), custom_call_target="tpu_custom_call" | custom-call | flops 80000000 | bytes 1000 | tf_op jit(solution)/shard_map/pallas_call | solution.py:495
  204.3 8.5 %shard_map.308.gate.refs_1_ = bf16[1024,1024]{1,0:T(8,128)(2,1)S(1)} custom-call(bf16[1024,2048]{1,0:T(8,128)(2,1)} %shard_map.298.x.refs_0_.refs_1_.a.refs_10_, bf16[8,2,256,1024]{3,2,1,0:T(8,128)(2,1)} %bitcast.107, bf16[1024,1024]{1,0:T(8,128)(2,1)S(1)} %shard_map.307.refs_2_.inner.refs_1_), custom_call_target="tpu_custom_call" | custom-call | flops 60000000 | bytes 1000 | tf_op jit(solution)/shard_map/pallas_call | solution.py:437
  214.1 19.2 %shard_map.309 = (bf16[1024,1024]{1,0:T(8,128)(2,1)S(1)}, bf16[1024,1024]{1,0:T(8,128)(2,1)}, bf16[1024,1024]{1,0:T(8,128)(2,1)}, bf16[512,1024]{1,0:T(8,128)(2,1)S(1)}, f32[1024,128]{1,0:T(8,128)S(1)}) custom-call(s32[5]{0:T(128)S(1)} %pad_add_fusion.info.refs_0_, bf16[1024,1024]{1,0:T(8,128)(2,1)} %copy-done.12, bf16[1024,1024]{1,0:T(8,128)(2,1)} %copy-done.27, ...), custom_call_target="tpu_custom_call" | custom-call | flops 200000000 | bytes 1000 | tf_op jit(solution)/shard_map/pallas_call | solution.py:406
  237.5 7.9 %shard_map.311 = (bf16[1024,1024]{1,0:T(8,128)(2,1)S(1)}, f32[1024,128]{1,0:T(8,128)S(1)}) custom-call(bf16[1024,2048]{1,0:T(8,128)(2,1)} %copy-done.68, bf16[1024,2048]{1,0:T(8,128)(2,1)} %all-gather.6.cloned.1.call-done.b.refs_3_, bf16[1024,1024]{1,0:T(8,128)(2,1)S(1)} %copy-done.3), custom_call_target="tpu_custom_call" | custom-call | flops 80000000 | bytes 1000 | tf_op jit(solution)/shard_map/pallas_call | solution.py:495
  258.5 8.8 %shard_map.313.refs_5_ = bf16[4,2,128,2048]{3,2,1,0:T(8,128)(2,1)} custom-call(s32[1]{0:T(128)} %bitcast.20.refs_0_, bf16[1024,1024]{1,0:T(8,128)(2,1)S(1)} %copy-done.2, bf16[1024,1024]{1,0:T(8,128)(2,1)S(1)} %copy-done.4, bf16[1024,2048]{1,0:T(8,128)(2,1)} %copy-done.68, f32[8,1024]{1,0:T(8,128)S(1)} %maximum_maximum_fusion.refs_4_.refs_3_.refs_5_, ...), custom_call_target="tpu_custom_call" | custom-call | flops 70000000 | bytes 1000 | tf_op jit(solution)/shard_map/pallas_call | solution.py:760
  278.5 9.6 %shard_map.316.refs_4_ = bf16[4,2,128,2048]{3,2,1,0:T(8,128)(2,1)} custom-call(s32[1]{0:T(128)} %bitcast.24.refs_0_.info, bf16[1024,1024]{1,0:T(8,128)(2,1)S(1)} %copy-done.2, bf16[1024,1024]{1,0:T(8,128)(2,1)S(1)} %copy-done.5, bf16[1024,2048]{1,0:T(8,128)(2,1)} %copy-done.68, bf16[4,2,128,2048]{3,2,1,0:T(8,128)(2,1)} %copy-done.70, ...), custom_call_target="tpu_custom_call" | custom-call | flops 70000000 | bytes 1000 | tf_op jit(solution)/shard_map/pallas_call | solution.py:760
  313.5 8.2 %shard_map.319.refs_9_ = bf16[4,2,256,1024]{3,2,1,0:T(8,128)(2,1)} custom-call(s32[1]{0:T(128)} %bitcast.24.refs_0_.info, bf16[1024,2048]{1,0:T(8,128)(2,1)} %shard_map.298.x.refs_0_.refs_1_.a.refs_10_, bf16[1024,1024]{1,0:T(8,128)(2,1)S(1)} %copy-done.7, bf16[1024,1024]{1,0:T(8,128)(2,1)S(1)} %get-tuple-element.66.refs_3_.refs_1_, ...), custom_call_target="tpu_custom_call" | custom-call | flops 70000000 | bytes 1000 | tf_op jit(solution)/shard_map/pallas_call | solution.py:760
  323.9 33.0 %shard_map.320 = (bf16[1024,1024]{1,0:T(8,128)(2,1)S(1)}, f32[1024,256]{1,0:T(8,128)S(1)}, f32[8,1024]{1,0:T(8,128)S(1)}, f32[64,1024]{1,0:T(8,128)S(1)}) custom-call(s32[5]{0:T(128)S(1)} %pad_add_fusion.info.refs_0_, bf16[1024,1024]{1,0:T(8,128)(2,1)} %copy-done.12, bf16[1024,1024]{1,0:T(8,128)(2,1)} %copy-done.45, bf16[1024,1024]{1,0:T(8,128)(2,1)} %copy-done.47, ...), custom_call_target="tpu_custom_call" | custom-call | flops 360000000 | bytes 1000 | tf_op jit(solution)/shard_map/pallas_call | solution.py:406
  356.9 10.4 %shard_map.321.refs_9_ = bf16[8,256,1024]{2,1,0:T(8,128)(2,1)} custom-call(bf16[1024,2048]{1,0:T(8,128)(2,1)} %shard_map.298.x.refs_0_.refs_1_.a.refs_10_, bf16[1024,1024]{1,0:T(8,128)(2,1)S(1)} %get-tuple-element.72.b.refs_3_), custom_call_target="tpu_custom_call" | custom-call | flops 100000000 | bytes 1000 | tf_op jit(solution)/shard_map/pallas_call | solution.py:804
  378.2 33.0 %shard_map.322 = (bf16[1024,1024]{1,0:T(8,128)(2,1)S(1)}, f32[1024,256]{1,0:T(8,128)S(1)}, f32[8,1024]{1,0:T(8,128)S(1)}, f32[64,1024]{1,0:T(8,128)S(1)}) custom-call(s32[5]{0:T(128)S(1)} %pad_add_fusion.info.refs_0_, bf16[1024,1024]{1,0:T(8,128)(2,1)} %copy-done.10, bf16[1024,1024]{1,0:T(8,128)(2,1)} %copy-done.35, bf16[1024,1024]{1,0:T(8,128)(2,1)} %copy-done.46, ...), custom_call_target="tpu_custom_call" | custom-call | flops 360000000 | bytes 1000 | tf_op jit(solution)/shard_map/pallas_call | solution.py:406
  433.1 12.9 %collective-permute-done.10.refs_1_ = bf16[128,2048]{1,0:T(8,128)(2,1)} collective-permute-done((bf16[128,2048]{1,0:T(8,128)(2,1)}, bf16[128,2048]{1,0:T(8,128)(2,1)}, u32[]{:S(2)}, u32[]{:S(2)}) %collective-permute-start.10) | collective-permute-done | bytes 524320 | tf_op jit(solution)/shard_map/ppermute | solution.py:989
  476.8 14.4 %shard_map.326 = (bf16[512,2048]{1,0:T(8,128)(2,1)S(1)}, f32[8,2048]{1,0:T(8,128)S(1)}) custom-call(bf16[1024,1024]{1,0:T(8,128)(2,1)} %copy-done.6, bf16[1024,1024]{1,0:T(8,128)(2,1)} %copy-done.11, bf16[1024,1024]{1,0:T(8,128)(2,1)} %copy-done.13, bf16[1024,1024]{1,0:T(8,128)(2,1)} %copy-done.28, bf16[1024,288]{1,0:T(8,128)(2,1)S(1)} %pad_maximum_fusion.3.refs_0_.refs_4_, ...), custom_call_target="tpu_custom_call" | custom-call | flops 150000000 | bytes 1000 | tf_op jit(solution)/shard_map/pallas_call | solution.py:921
  494.2 14.4 %shard_map.327 = (bf16[512,2048]{1,0:T(8,128)(2,1)S(1)}, f32[8,2048]{1,0:T(8,128)S(1)}) custom-call(bf16[1024,1024]{1,0:T(8,128)(2,1)} %copy-done.6, bf16[1024,1024]{1,0:T(8,128)(2,1)} %copy-done.11, bf16[1024,1024]{1,0:T(8,128)(2,1)} %copy-done.13, bf16[1024,1024]{1,0:T(8,128)(2,1)} %copy-done.28, bf16[1024,288]{1,0:T(8,128)(2,1)S(1)} %pad_maximum_fusion.3.refs_0_.refs_4_, ...), custom_call_target="tpu_custom_call" | custom-call | flops 150000000 | bytes 1000 | tf_op jit(solution)/shard_map/pallas_call | solution.py:921
  513.0 10.6 %shard_map.328.refs_2_ = bf16[8,352,1024]{2,1,0:T(8,128)(2,1)} custom-call(bf16[1024,2048]{1,0:T(8,128)(2,1)} %shard_map.298.x.refs_0_.refs_1_.a.refs_10_, bf16[1024,1024]{1,0:T(8,128)(2,1)S(1)} %copy-done.15, bf16[8,96,1024]{2,1,0:T(8,128)(2,1)S(1)} %pad_maximum_fusion.1.refs_0_), custom_call_target="tpu_custom_call" | custom-call | flops 100000000 | bytes 1000 | tf_op jit(solution)/shard_map/pallas_call | solution.py:804
  527.6 43.4 %collective-permute-done.12.refs_2_ = bf16[512,2048]{1,0:T(8,128)(2,1)S(1)} collective-permute-done((bf16[512,2048]{1,0:T(8,128)(2,1)}, bf16[512,2048]{1,0:T(8,128)(2,1)S(1)}, u32[]{:S(2)}, u32[]{:S(2)}) %collective-permute-start.12) | collective-permute-done | bytes 2097184 | tf_op jit(solution)/shard_map/ppermute | solution.py:989
  577.5 16.3 %collective-permute-done.14 = bf16[128,2048]{1,0:T(8,128)(2,1)} collective-permute-done((bf16[128,2048]{1,0:T(8,128)(2,1)}, bf16[128,2048]{1,0:T(8,128)(2,1)}, u32[]{:S(2)}, u32[]{:S(2)}) %collective-permute-start.14) | collective-permute-done | bytes 524320 | tf_op jit(solution)/shard_map/ppermute | solution.py:1011
  598.3 17.0 %collective-permute-done.17 = bf16[512,1024]{1,0:T(8,128)(2,1)S(1)} collective-permute-done((bf16[512,1024]{1,0:T(8,128)(2,1)S(1)}, bf16[512,1024]{1,0:T(8,128)(2,1)S(1)}, u32[]{:S(2)}, u32[]{:S(2)}) %collective-permute-start.17) | collective-permute-done | bytes 1048608 | tf_op jit(solution)/shard_map/ppermute | solution.py:1011
  632.5 9.9 %collective-permute-done.19 = bf16[80,1024]{1,0:T(8,128)(2,1)S(1)} collective-permute-done((bf16[80,1024]{1,0:T(8,128)(2,1)S(1)}, bf16[80,1024]{1,0:T(8,128)(2,1)S(1)}, u32[]{:S(2)}, u32[]{:S(2)}) %collective-permute-start.19) | collective-permute-done | bytes 163872 | tf_op jit(solution)/shard_map/ppermute | solution.py:989
  655.8 7.9 %shard_map.318 = bf16[512,2048]{1,0:T(8,128)(2,1)S(1)} custom-call(bf16[1024,1024]{1,0:T(8,128)(2,1)S(1)} %copy-done.2, bf16[1024,1024]{1,0:T(8,128)(2,1)} %get-tuple-element.56.y.refs_1_.refs_2_, bf16[1024,2048]{1,0:T(8,128)(2,1)} %refs_2_.3, bf16[1024,2048]{1,0:T(8,128)(2,1)} %all-gather.6.cloned.1.call-done.b.refs_3_, ...), custom_call_target="tpu_custom_call" | custom-call | flops 50000000 | bytes 1000 | tf_op jit(solution)/shard_map/pallas_call | solution.py:523
  682.6 13.9 %all-gather.8.cloned.1.call-done = bf16[2816,1024]{1,0:T(8,128)(2,1)} async-done(((bf16[352,1024]{1,0:T(8,128)(2,1)}), bf16[2816,1024]{1,0:T(8,128)(2,1)}) %all-gather.8.cloned.1.call-update) | async-done | bytes 5767184 | tf_op jit(solution)/shard_map/all_gather | solution.py:1241
  (386 shorter events, 287.4 us)
Async XLA Ops:
  7.2 187.8 %all-gather.4.cloned.1.call-start = ((), (), s32[]{:S(2)}) async-start(), calls=%async_computation.4 | async-start | bytes 9437184 | tf_op jit(solution)/shard_map/all_gather | solution.py:1056
  7.2 83.4 %collective-permute-start = (bf16[512,2048]{1,0:T(8,128)(2,1)}, bf16[512,2048]{1,0:T(8,128)(2,1)}, u32[]{:S(2)}, u32[]{:S(2)}) collective-permute-start(bf16[512,2048]{1,0:T(8,128)(2,1)} %refs_0_.3), channel_id=1, source_target_pairs={{0,1},{1,0},{2,3},{3,2},{4,5},{5,4},{6,7},{7,6},{8,9},{9,8},{10,11... | collective-permute-start | bytes 6291464 | tf_op jit(solution)/shard_map/ppermute | solution.py:989
  12.8 77.1 %collective-permute-start.1 = (bf16[512,1024]{1,0:T(8,128)(2,1)}, bf16[512,1024]{1,0:T(8,128)(2,1)S(1)}, u32[]{:S(2)}, u32[]{:S(2)}) collective-permute-start(bf16[512,1024]{1,0:T(8,128)(2,1)} %pad_maximum_fusion.2), channel_id=1, source_target_pairs={{0,2},{1,3},{2,0},{3,1},{4,6},{5,7},{6,4},{7,5},{8,10},{9,11},{10,... | collective-permute-start | bytes 3145736 | tf_op jit(solution)/shard_map/ppermute | solution.py:989
  15.7 73.8 %collective-permute-start.2 = (bf16[16,2048]{0,1:T(8,128)(2,1)S(1)}, bf16[16,2048]{0,1:T(8,128)(2,1)S(1)}, u32[]{:S(2)}, u32[]{:S(2)}) collective-permute-start(bf16[16,2048]{0,1:T(8,128)(2,1)S(1)} %bitcast.121), channel_id=1, source_target_pairs={{0,2},{1,3},{2,0},{3,1},{4,6},{5,7},{6,4},{7,5},{8,10},{9,11},{10,... | collective-permute-start | bytes 196616 | tf_op jit(solution)/shard_map/ppermute | solution.py:989
  16.4 73.5 %collective-permute-start.3 = (f32[8,1024]{1,0:T(8,128)S(1)}, f32[8,1024]{1,0:T(8,128)S(1)}, u32[]{:S(2)}, u32[]{:S(2)}) collective-permute-start(f32[8,1024]{1,0:T(8,128)S(1)} %concatenate.104), channel_id=1, source_target_pairs={{0,2},{1,3},{2,0},{3,1},{4,6},{5,7},{6,4},{7,5},{8,10},{9,11},{10,... | collective-permute-start | bytes 98312 | tf_op jit(solution)/shard_map/ppermute | solution.py:989
  91.9 143.9 %all-gather.6.cloned.1.call-start = ((), (), s32[]{:S(2)}) async-start(), calls=%async_computation.5 | async-start | bytes 4718592 | tf_op jit(solution)/shard_map/all_gather | solution.py:1095
  96.3 59.0 %collective-permute-start.4 = (bf16[512,2048]{1,0:T(8,128)(2,1)}, bf16[512,2048]{1,0:T(8,128)(2,1)}, u32[]{:S(2)}, u32[]{:S(2)}) collective-permute-start(bf16[512,2048]{1,0:T(8,128)(2,1)} %shard_map.297.refs_6_), channel_id=1, source_target_pairs={{0,1},{1,0},{2,3},{3,2},{4,5},{5,4},{6,7},{7,6},{8,9},{9,8},{10,11... | collective-permute-start | bytes 6291464 | tf_op jit(solution)/shard_map/ppermute | solution.py:989
  113.6 62.8 %collective-permute-start.5 = (bf16[128,2048]{1,0:T(8,128)(2,1)}, bf16[128,2048]{1,0:T(8,128)(2,1)}, u32[]{:S(2)}, u32[]{:S(2)}) collective-permute-start(bf16[128,2048]{1,0:T(8,128)(2,1)} %constant_dynamic-slice_fusion), channel_id=1, source_target_pairs={{0,2},{1,3},{2,0},{3,1},{4,6},{5,7},{6,4},{7,5},{8,10},{9,11},{10,... | collective-permute-start | bytes 1572872 | tf_op jit(solution)/shard_map/ppermute | solution.py:989
  178.6 239.3 %reduce-scatter.7.cloned.1.call-start = ((), (), s32[]{:S(2)}) async-start(), calls=%async_computation.7 | async-start | bytes 5242880 | tf_op jit(solution)/shard_map/reduce_scatter | solution.py:1140
  288.1 159.1 %reduce-scatter.5.cloned.1.call-start = ((), (), s32[]{:S(2)}) async-start(), calls=%async_computation.6 | async-start | bytes 5242880 | tf_op jit(solution)/shard_map/reduce_scatter | solution.py:1140
  321.6 296.0 %reduce-scatter.11.cloned.1.call-start = ((), (), s32[]{:S(2)}) async-start(), calls=%async_computation.9 | async-start | bytes 4718592 | tf_op jit(solution)/shard_map/reduce_scatter | solution.py:1172
  367.4 259.2 %reduce-scatter.9.cloned.1.call-start = ((), (), s32[]{:S(2)}) async-start(), calls=%async_computation.8 | async-start | bytes 6488064 | tf_op jit(solution)/shard_map/reduce_scatter | solution.py:1224
  367.4 79.8 %collective-permute-start.8 = (bf16[512,2048]{1,0:T(8,128)(2,1)}, bf16[512,2048]{1,0:T(8,128)(2,1)}, u32[]{:S(2)}, u32[]{:S(2)}) collective-permute-start(bf16[512,2048]{1,0:T(8,128)(2,1)} %copy-done.39), channel_id=1, source_target_pairs={{0,1},{1,0},{2,3},{3,2},{4,5},{5,4},{6,7},{7,6},{8,9},{9,8},{10,11... | collective-permute-start | bytes 6291464 | tf_op jit(solution)/shard_map/ppermute | solution.py:989
  419.8 26.2 %collective-permute-start.10 = (bf16[128,2048]{1,0:T(8,128)(2,1)}, bf16[128,2048]{1,0:T(8,128)(2,1)}, u32[]{:S(2)}, u32[]{:S(2)}) collective-permute-start(bf16[128,2048]{1,0:T(8,128)(2,1)} %dynamic-slice_bitcast_fusion.1), channel_id=1, source_target_pairs={{0,2},{1,3},{2,0},{3,1},{4,6},{5,7},{6,4},{7,5},{8,10},{9,11},{10,... | collective-permute-start | bytes 1572872 | tf_op jit(solution)/shard_map/ppermute | solution.py:989
  457.4 36.8 %collective-permute-start.11 = (bf16[256,1024]{1,0:T(8,128)(2,1)}, bf16[256,1024]{1,0:T(8,128)(2,1)}, u32[]{:S(2)}, u32[]{:S(2)}) collective-permute-start(bf16[256,1024]{1,0:T(8,128)(2,1)} %dynamic-slice_bitcast_fusion), channel_id=1, source_target_pairs={{0,2},{1,3},{2,0},{3,1},{4,6},{5,7},{6,4},{7,5},{8,10},{9,11},{10,... | collective-permute-start | bytes 1572872 | tf_op jit(solution)/shard_map/ppermute | solution.py:989
  462.9 29.7 %collective-permute-start.13 = (f32[40,1024]{1,0:T(8,128)}, f32[40,1024]{1,0:T(8,128)}, u32[]{:S(2)}, u32[]{:S(2)}) collective-permute-start(f32[40,1024]{1,0:T(8,128)} %concatenate.122), channel_id=1, source_target_pairs={{0,2},{1,3},{2,0},{3,1},{4,6},{5,7},{6,4},{7,5},{8,10},{9,11},{10,... | collective-permute-start | bytes 491528 | tf_op jit(solution)/shard_map/ppermute | solution.py:989
  523.7 172.9 %all-gather.8.cloned.1.call-start = ((), (), s32[]{:S(2)}) async-start(), calls=%async_computation.10 | async-start | bytes 6488064 | tf_op jit(solution)/shard_map/all_gather | solution.py:1241
  523.7 47.3 %collective-permute-start.12 = (bf16[512,2048]{1,0:T(8,128)(2,1)}, bf16[512,2048]{1,0:T(8,128)(2,1)S(1)}, u32[]{:S(2)}, u32[]{:S(2)}) collective-permute-start(bf16[512,2048]{1,0:T(8,128)(2,1)} %copy-done.67), channel_id=1, source_target_pairs={{0,1},{1,0},{2,3},{3,2},{4,5},{5,4},{6,7},{7,6},{8,9},{9,8},{10,11... | collective-permute-start | bytes 6291464 | tf_op jit(solution)/shard_map/ppermute | solution.py:989
  526.1 48.8 %collective-permute-start.16 = (bf16[256,1024]{1,0:T(8,128)(2,1)S(1)}, bf16[256,1024]{1,0:T(8,128)(2,1)}, u32[]{:S(2)}, u32[]{:S(2)}) collective-permute-start(bf16[256,1024]{1,0:T(8,128)(2,1)S(1)} %shard_map.329.refs_1_), channel_id=1, source_target_pairs={{0,16},{4,20},{8,24},{12,28},{16,0},{20,4},{24,8},{28,12},{1,17},{... | collective-permute-start | bytes 1572872 | tf_op jit(solution)/shard_map/ppermute | solution.py:1011
  573.4 20.4 %collective-permute-start.14 = (bf16[128,2048]{1,0:T(8,128)(2,1)}, bf16[128,2048]{1,0:T(8,128)(2,1)}, u32[]{:S(2)}, u32[]{:S(2)}) collective-permute-start(bf16[128,2048]{1,0:T(8,128)(2,1)} %shard_map.330), channel_id=1, source_target_pairs={{0,8},{4,12},{8,0},{12,4},{16,24},{20,28},{24,16},{28,20},{1,9},{5... | collective-permute-start | bytes 1572872 | tf_op jit(solution)/shard_map/ppermute | solution.py:1011
  576.8 38.4 %collective-permute-start.17 = (bf16[512,1024]{1,0:T(8,128)(2,1)S(1)}, bf16[512,1024]{1,0:T(8,128)(2,1)S(1)}, u32[]{:S(2)}, u32[]{:S(2)}) collective-permute-start(bf16[512,1024]{1,0:T(8,128)(2,1)S(1)} %maximum_select_fusion.3.refs_2_), channel_id=1, source_target_pairs={{0,8},{4,12},{8,0},{12,4},{16,24},{20,28},{24,16},{28,20},{1,9},{5... | collective-permute-start | bytes 3145736 | tf_op jit(solution)/shard_map/ppermute | solution.py:1011
  596.8 25.2 %collective-permute-start.15 = (bf16[256,2048]{1,0:T(8,128)(2,1)}, bf16[256,2048]{1,0:T(8,128)(2,1)}, u32[]{:S(2)}, u32[]{:S(2)}) collective-permute-start(bf16[256,2048]{1,0:T(8,128)(2,1)} %maximum_select_fusion.2.refs_1_), channel_id=1, source_target_pairs={{0,16},{4,20},{8,24},{12,28},{16,0},{20,4},{24,8},{28,12},{1,17},{... | collective-permute-start | bytes 3145736 | tf_op jit(solution)/shard_map/ppermute | solution.py:1011
  619.5 30.3 %collective-permute-start.18 = (bf16[256,1024]{1,0:T(8,128)(2,1)}, bf16[256,1024]{1,0:T(8,128)(2,1)S(1)}, u32[]{:S(2)}, u32[]{:S(2)}) collective-permute-start(bf16[256,1024]{1,0:T(8,128)(2,1)} %shard_map.332), channel_id=1, source_target_pairs={{0,2},{1,3},{2,0},{3,1},{4,6},{5,7},{6,4},{7,5},{8,10},{9,11},{10,... | collective-permute-start | bytes 1572872 | tf_op jit(solution)/shard_map/ppermute | solution.py:989
  653.2 25.9 %collective-permute-start.22 = (bf16[512,2048]{1,0:T(8,128)(2,1)}, bf16[512,2048]{1,0:T(8,128)(2,1)S(1)}, u32[]{:S(2)}, u32[]{:S(2)}) collective-permute-start(bf16[512,2048]{1,0:T(8,128)(2,1)} %maximum_select_fusion.refs_1_.a), channel_id=1, source_target_pairs={{0,4},{4,0},{8,12},{12,8},{16,20},{20,16},{24,28},{28,24},{1,5},{5... | collective-permute-start | bytes 6291464 | tf_op jit(solution)/shard_map/ppermute | solution.py:1011
  (95 other events, 579.5 us)
Sparse Core Ops, SparseCore 0:
  92.0 55.8 all-gather.3
  178.7 37.1 all-gather.5
  288.3 53.7 reduce-scatter.6
  345.1 52.7 reduce-scatter.4
  401.1 51.2 reduce-scatter.10
  523.8 65.4 reduce-scatter.8
  653.2 43.3 all-gather.7

commit v3 on v2

--- a/solution.py
+++ b/solution.py
@@ -775,7 +775,7 @@
     )(half[None], *operands, *later)
 
 
-def grad_pieces(left, right, shared, batches, bits):
+def grad_pieces(left, right, shared, batches, bits, later=()):
     t, width = left.shape
     columns = right.shape[1]
     chips = batches // 2
@@ -802,18 +802,19 @@
                 out[:, 2 * tall :, :] = refs[0][...]
 
     return pl.pallas_call(
-        kernel,
+        ignore(kernel, 3 if extra else 2, len(later)),
         grid=(width // high,),
         in_specs=[
             pl.BlockSpec((t, high), lambda i: (0, i)),
             pl.BlockSpec((t, columns), lambda i: (0, 0)),
         ]
-        + ([pl.BlockSpec(shared.shape, lambda i: (0, 0, 0))] if extra else []),
+        + ([pl.BlockSpec(shared.shape, lambda i: (0, 0, 0))] if extra else [])
+        + unread(later),
         out_specs=pl.BlockSpec((batches, 2 * tall + extra, columns), lambda i: (0, 0, 0)),
         out_shape=shape((batches, 2 * tall + extra, columns), BF16),
         compiler_params=pltpu.CompilerParams(vmem_limit_bytes=VMEM_LIMIT),
         cost_estimate=lasting(10),
-    )(left, right, *([shared] if extra else []))
+    )(left, right, *([shared] if extra else []), *later)
 
 
 def place_pieces(v, tall, bits, later):
@@ -1210,7 +1211,7 @@
             first,
             count,
             normed,
-            (norm_sums[0], far_z) if norm_sums else (g_small,),
+            (norm_sums[0],) if norm_sums else (g_small,),
         )
         norm_sums.append(total)
         return part
@@ -1219,12 +1220,12 @@
     d_normed_in = d_normed_in()
     bc_rows, few_rows = 2 * STATE * width_in // channels, 8 * 2 * STATE // channels
     shared = spread(jnp.concatenate([g_small[: 2 * STATE].reshape(-1, channels), g_bc.reshape(-1, channels), sum(norm_sums)[:1].reshape(-1, channels)], axis=0))
-    private = spread(pack(0) + across(pack(1), far_bit))
-    own_cut = grad_pieces(normed, back[0][0], jnp.concatenate([shared, private], axis=1), batches, bits)
+    private = spread(pack(0) + delayed(across(pack(1), far_bit), (norm_sums[-1],)))
+    own_cut = grad_pieces(normed, back[0][0], jnp.concatenate([shared, private], axis=1), batches, bits, (d_normed_got,))
     own_part = lax.psum_scatter(own_cut.reshape(-1, channels), "batch", scatter_dimension=0, tiled=True)
     seen = []
-    total_z = added(part_z[0], far_z, (own_cut,))
-    total_out = delayed(total_out, (total_z, d_normed_got))
+    total_z = added(part_z[0], far_z, (norm_sums[-1],))
+    total_out = delayed(total_out, (total_z,))
     halves_here, halves_there = gather_both([total_out, total_z], seen)
     own_part = delayed(own_part, halves_here)
 

time: 737 us -> 730 us (level)
  waiting for transfers between devices: 213 us -> 196 us
    ppermute x15, waiting for transfers between devices: 159 us -> 131 us  [across(): return lax.ppermute(v, 'head', [(i, i ^ bit) for i in range(stacks)])]
    ppermute x8, waiting for transfers between devices: 40.3 us -> 49.9 us  [planar(): return lax.ppermute(v, 'batch', [(i, i ^ bit) for i in range(batches)])]
    unnamed x180 -> x212, local copies, waits for them, and re-layouts: 62.7 us -> 60.3 us
  transfers between devices with their start and end apart: 30 -> 30, of which waited for: 13 -> 14; matrix products, arithmetic and copies ran while one was open for 11% -> 12% of each run, Pallas kernels for 38% -> 38%
where the time goes in v3:
time: 730 us; the launch traced here: 718 us
  Pallas kernels  308 us (42%)
  waiting for transfers between devices  196 us (27%)
  local copies, waits for them, and re-layouts  118 us (16%)
  other arithmetic  40.8 us (6%)
  starting transfers between devices  35.1 us (5%)
  between operations  19.1 us (3%)
    ppermute x15, waiting for transfers between devices, across(): return lax.ppermute(v, 'head', [(i, i ^ bit) for i in range(stacks)])  131 us
    pallas_call x6, Pallas kernels, call(): pl.pallas_call(kernel, grid_spec=pltpu.PrefetchScalarGridSpec(num_scalar_...  110 us
    unnamed x212, local copies, waits for them, and re-layouts  60.3 us
    ppermute x8, waiting for transfers between devices, planar(): return lax.ppermute(v, 'batch', [(i, i ^ bit) for i in range(batches)])  49.9 us
    pallas_call x4, Pallas kernels, grad_half(): pl.pallas_call(ignore(kernel, 1 + len(operands), len(later)), grid_spec=p...  34.3 us
    pallas_call x4, Pallas kernels, project(): pl.pallas_call(ignore(kernel, 2, len(later)), grid=(columns // wide,), in...  32.2 us
    pallas_call x2, Pallas kernels, rows_back(): pl.pallas_call(ignore(kernel, 2 * count + 1, len(later)), grid=(columns /...  29.6 us
    ppermute x15, starting transfers between devices, across(): return lax.ppermute(v, 'head', [(i, i ^ bit) for i in range(stacks)])  28.1 us
  transfers between devices with their start and end apart: 30, of which 14 were waited for; matrix products, arithmetic and copies ran while one was open for 12% of the time, Pallas kernels for 38%

profile of v3, /device:TPU:0, one launch (start us, length us, event | category | flops | bytes accessed | tf_op | source)
XLA Modules:
  0.0 717.8 jit_solution(15221510959944872535)
XLA Ops:
  19.0 70.5 %collective-permute-done.2 = bf16[16,2048]{0,1:T(8,128)(2,1)S(1)} collective-permute-done((bf16[16,2048]{0,1:T(8,128)(2,1)S(1)}, bf16[16,2048]{0,1:T(8,128)(2,1)S(1)}, u32[]{:S(2)}, u32[]{:S(2)}) %collective-permute-start.2) | collective-permute-done | bytes 65568 | tf_op jit(solution)/shard_map/ppermute | solution.py:990
  132.5 8.4 %shard_map.302.refs_2_.refs_1_ = bf16[1024,1024]{1,0:T(8,128)(2,1)S(1)} custom-call(bf16[1024,2048]{1,0:T(8,128)(2,1)} %shard_map.298.x.refs_0_.refs_1_.a.refs_10_, bf16[2048,1024]{1,0:T(8,128)(2,1)} %refs_5_.3, bf16[1024,1024]{1,0:T(8,128)(2,1)S(1)} %shard_map.301.refs_2_.refs_1_), custom_call_target="tpu_custom_call" | custom-call | flops 60000000 | bytes 1000 | tf_op jit(solution)/shard_map/pallas_call | solution.py:437
  143.0 12.4 %collective-permute-done.4.refs_7_ = bf16[512,2048]{1,0:T(8,128)(2,1)} collective-permute-done((bf16[512,2048]{1,0:T(8,128)(2,1)}, bf16[512,2048]{1,0:T(8,128)(2,1)}, u32[]{:S(2)}, u32[]{:S(2)}) %collective-permute-start.4) | collective-permute-done | bytes 2097184 | tf_op jit(solution)/shard_map/ppermute | solution.py:990
  155.4 19.1 %shard_map.303 = (bf16[1024,1024]{1,0:T(8,128)(2,1)S(1)}, bf16[1024,1024]{1,0:T(8,128)(2,1)}, bf16[1024,1024]{1,0:T(8,128)(2,1)}, bf16[512,1024]{1,0:T(8,128)(2,1)S(1)}, f32[1024,128]{1,0:T(8,128)S(1)}) custom-call(s32[5]{0:T(128)S(1)} %pad_add_fusion.info.refs_0_, bf16[1024,1024]{1,0:T(8,128)(2,1)} %copy-done.10, bf16[1024,1024]{1,0:T(8,128)(2,1)} %copy-done.25, ...), custom_call_target="tpu_custom_call" | custom-call | flops 200000000 | bytes 1000 | tf_op jit(solution)/shard_map/pallas_call | solution.py:406
  184.7 8.2 %shard_map.306 = (bf16[1024,1024]{1,0:T(8,128)(2,1)S(1)}, f32[1024,128]{1,0:T(8,128)S(1)}) custom-call(bf16[1024,2048]{1,0:T(8,128)(2,1)} %copy-done.72, bf16[1024,2048]{1,0:T(8,128)(2,1)} %refs_2_.3, bf16[1024,1024]{1,0:T(8,128)(2,1)S(1)} %copy-done.2), custom_call_target="tpu_custom_call" | custom-call | flops 80000000 | bytes 1000 | tf_op jit(solution)/shard_map/pallas_call | solution.py:495
  204.3 8.5 %shard_map.308.gate.refs_1_ = bf16[1024,1024]{1,0:T(8,128)(2,1)S(1)} custom-call(bf16[1024,2048]{1,0:T(8,128)(2,1)} %shard_map.298.x.refs_0_.refs_1_.a.refs_10_, bf16[8,2,256,1024]{3,2,1,0:T(8,128)(2,1)} %bitcast.107, bf16[1024,1024]{1,0:T(8,128)(2,1)S(1)} %shard_map.307.refs_2_.inner.refs_1_), custom_call_target="tpu_custom_call" | custom-call | flops 60000000 | bytes 1000 | tf_op jit(solution)/shard_map/pallas_call | solution.py:437
  214.2 19.2 %shard_map.309 = (bf16[1024,1024]{1,0:T(8,128)(2,1)S(1)}, bf16[1024,1024]{1,0:T(8,128)(2,1)}, bf16[1024,1024]{1,0:T(8,128)(2,1)}, bf16[512,1024]{1,0:T(8,128)(2,1)S(1)}, f32[1024,128]{1,0:T(8,128)S(1)}) custom-call(s32[5]{0:T(128)S(1)} %pad_add_fusion.info.refs_0_, bf16[1024,1024]{1,0:T(8,128)(2,1)} %copy-done.15, bf16[1024,1024]{1,0:T(8,128)(2,1)} %copy-done.26, ...), custom_call_target="tpu_custom_call" | custom-call | flops 200000000 | bytes 1000 | tf_op jit(solution)/shard_map/pallas_call | solution.py:406
  237.5 7.9 %shard_map.311 = (bf16[1024,1024]{1,0:T(8,128)(2,1)S(1)}, f32[1024,128]{1,0:T(8,128)S(1)}) custom-call(bf16[1024,2048]{1,0:T(8,128)(2,1)} %copy-done.72, bf16[1024,2048]{1,0:T(8,128)(2,1)} %all-gather.6.cloned.1.call-done.b.refs_3_, bf16[1024,1024]{1,0:T(8,128)(2,1)S(1)} %copy-done.3), custom_call_target="tpu_custom_call" | custom-call | flops 80000000 | bytes 1000 | tf_op jit(solution)/shard_map/pallas_call | solution.py:495
  259.1 8.8 %shard_map.313.refs_5_ = bf16[4,2,128,2048]{3,2,1,0:T(8,128)(2,1)} custom-call(s32[1]{0:T(128)} %bitcast.20.refs_0_, bf16[1024,1024]{1,0:T(8,128)(2,1)S(1)} %copy-done.2, bf16[1024,1024]{1,0:T(8,128)(2,1)S(1)} %copy-done.4, bf16[1024,2048]{1,0:T(8,128)(2,1)} %copy-done.72, f32[8,1024]{1,0:T(8,128)S(1)} %maximum_maximum_fusion.refs_4_.refs_3_.refs_5_, ...), custom_call_target="tpu_custom_call" | custom-call | flops 70000000 | bytes 1000 | tf_op jit(solution)/shard_map/pallas_call | solution.py:760
  279.2 9.6 %shard_map.316.refs_4_ = bf16[4,2,128,2048]{3,2,1,0:T(8,128)(2,1)} custom-call(s32[1]{0:T(128)} %bitcast.24.refs_0_.info, bf16[1024,1024]{1,0:T(8,128)(2,1)S(1)} %copy-done.2, bf16[1024,1024]{1,0:T(8,128)(2,1)S(1)} %copy-done.5, bf16[1024,2048]{1,0:T(8,128)(2,1)} %copy-done.72, bf16[4,2,128,2048]{3,2,1,0:T(8,128)(2,1)} %copy-done.75, ...), custom_call_target="tpu_custom_call" | custom-call | flops 70000000 | bytes 1000 | tf_op jit(solution)/shard_map/pallas_call | solution.py:760
  296.9 7.8 %shard_map.317.refs_4_.refs_5_ = bf16[4,2,256,1024]{3,2,1,0:T(8,128)(2,1)} custom-call(s32[1]{0:T(128)} %bitcast.20.refs_0_, bf16[1024,2048]{1,0:T(8,128)(2,1)} %shard_map.298.x.refs_0_.refs_1_.a.refs_10_, bf16[1024,1024]{1,0:T(8,128)(2,1)S(1)} %copy-done.7, bf16[1024,1024]{1,0:T(8,128)(2,1)S(1)} %get-tuple-element.66.refs_3_.refs_1_, ...), custom_call_target="tpu_custom_call" | custom-call | flops 70000000 | bytes 1000 | tf_op jit(solution)/shard_map/pallas_call | solution.py:760
  314.2 8.2 %shard_map.319.refs_9_ = bf16[4,2,256,1024]{3,2,1,0:T(8,128)(2,1)} custom-call(s32[1]{0:T(128)} %bitcast.24.refs_0_.info, bf16[1024,2048]{1,0:T(8,128)(2,1)} %shard_map.298.x.refs_0_.refs_1_.a.refs_10_, bf16[1024,1024]{1,0:T(8,128)(2,1)S(1)} %copy-done.7, bf16[1024,1024]{1,0:T(8,128)(2,1)S(1)} %get-tuple-element.66.refs_3_.refs_1_, ...), custom_call_target="tpu_custom_call" | custom-call | flops 70000000 | bytes 1000 | tf_op jit(solution)/shard_map/pallas_call | solution.py:760
  325.2 33.0 %shard_map.320 = (bf16[1024,1024]{1,0:T(8,128)(2,1)S(1)}, f32[1024,256]{1,0:T(8,128)S(1)}, f32[8,1024]{1,0:T(8,128)S(1)}, f32[64,1024]{1,0:T(8,128)S(1)}) custom-call(s32[5]{0:T(128)S(1)} %copy-done.67, bf16[1024,1024]{1,0:T(8,128)(2,1)} %copy-done.15, bf16[1024,1024]{1,0:T(8,128)(2,1)} %copy-done.43, bf16[1024,1024]{1,0:T(8,128)(2,1)} %copy-done.45, ...), custom_call_target="tpu_custom_call" | custom-call | flops 360000000 | bytes 1000 | tf_op jit(solution)/shard_map/pallas_call | solution.py:406
  358.2 10.5 %shard_map.321.refs_9_ = bf16[8,256,1024]{2,1,0:T(8,128)(2,1)} custom-call(bf16[1024,2048]{1,0:T(8,128)(2,1)} %shard_map.298.x.refs_0_.refs_1_.a.refs_10_, bf16[1024,1024]{1,0:T(8,128)(2,1)S(1)} %get-tuple-element.72.b.refs_3_), custom_call_target="tpu_custom_call" | custom-call | flops 100000000 | bytes 1000 | tf_op jit(solution)/shard_map/pallas_call | solution.py:804
  378.7 33.0 %shard_map.322 = (bf16[1024,1024]{1,0:T(8,128)(2,1)S(1)}, f32[1024,256]{1,0:T(8,128)S(1)}, f32[8,1024]{1,0:T(8,128)S(1)}, f32[64,1024]{1,0:T(8,128)S(1)}) custom-call(s32[5]{0:T(128)S(1)} %copy-done.67, bf16[1024,1024]{1,0:T(8,128)(2,1)} %copy-done.10, bf16[1024,1024]{1,0:T(8,128)(2,1)} %copy-done.34, bf16[1024,1024]{1,0:T(8,128)(2,1)} %copy-done.44, ...), custom_call_target="tpu_custom_call" | custom-call | flops 360000000 | bytes 1000 | tf_op jit(solution)/shard_map/pallas_call | solution.py:406
  429.7 15.8 %collective-permute-done.10.refs_1_ = bf16[128,2048]{1,0:T(8,128)(2,1)} collective-permute-done((bf16[128,2048]{1,0:T(8,128)(2,1)}, bf16[128,2048]{1,0:T(8,128)(2,1)}, u32[]{:S(2)}, u32[]{:S(2)}) %collective-permute-start.10) | collective-permute-done | bytes 524320 | tf_op jit(solution)/shard_map/ppermute | solution.py:990
  453.3 15.2 %shard_map.326 = (bf16[512,2048]{1,0:T(8,128)(2,1)}, f32[8,2048]{1,0:T(8,128)S(1)}) custom-call(bf16[1024,1024]{1,0:T(8,128)(2,1)} %copy-done.6, bf16[1024,1024]{1,0:T(8,128)(2,1)} %copy-done.11, bf16[1024,1024]{1,0:T(8,128)(2,1)} %copy-done.12, bf16[1024,1024]{1,0:T(8,128)(2,1)} %copy-done.27, bf16[1024,288]{1,0:T(8,128)(2,1)S(1)} %pad_maximum_fusion.3.refs_0_.refs_4_, ...), custom_call_target="tpu_custom_call" | custom-call | flops 150000000 | bytes 1000 | tf_op jit(solution)/shard_map/pallas_call | solution.py:922
  498.6 14.4 %shard_map.327 = (bf16[512,2048]{1,0:T(8,128)(2,1)S(1)}, f32[8,2048]{1,0:T(8,128)S(1)}) custom-call(bf16[1024,1024]{1,0:T(8,128)(2,1)} %copy-done.6, bf16[1024,1024]{1,0:T(8,128)(2,1)} %copy-done.11, bf16[1024,1024]{1,0:T(8,128)(2,1)} %copy-done.12, bf16[1024,1024]{1,0:T(8,128)(2,1)} %copy-done.27, bf16[1024,288]{1,0:T(8,128)(2,1)S(1)} %pad_maximum_fusion.3.refs_0_.refs_4_, ...), custom_call_target="tpu_custom_call" | custom-call | flops 150000000 | bytes 1000 | tf_op jit(solution)/shard_map/pallas_call | solution.py:922
  519.8 10.6 %shard_map.329 = bf16[8,352,1024]{2,1,0:T(8,128)(2,1)} custom-call(bf16[1024,2048]{1,0:T(8,128)(2,1)} %shard_map.298.x.refs_0_.refs_1_.a.refs_10_, bf16[1024,1024]{1,0:T(8,128)(2,1)S(1)} %copy-done.14, bf16[8,96,1024]{2,1,0:T(8,128)(2,1)S(1)} %pad_maximum_fusion.1.refs_2_, bf16[512,2048]{1,0:T(8,128)(2,1)} %collective-permute-done.11.refs_3_), custom_call_target="tpu_custom_call" | custom-call | flops 100000000 | bytes 1000 | tf_op jit(solution)/shard_map/pallas_call | solution.py:804
  537.0 21.8 %collective-permute-done.13.refs_1_ = bf16[256,1024]{1,0:T(8,128)(2,1)S(1)} collective-permute-done((bf16[256,1024]{1,0:T(8,128)(2,1)S(1)}, bf16[256,1024]{1,0:T(8,128)(2,1)S(1)}, u32[]{:S(2)}, u32[]{:S(2)}) %collective-permute-start.13) | collective-permute-done | bytes 524320 | tf_op jit(solution)/shard_map/ppermute | solution.py:990
  563.5 19.9 %collective-permute-done.14 = bf16[128,2048]{1,0:T(8,128)(2,1)} collective-permute-done((bf16[128,2048]{1,0:T(8,128)(2,1)S(1)}, bf16[128,2048]{1,0:T(8,128)(2,1)}, u32[]{:S(2)}, u32[]{:S(2)}) %collective-permute-start.14) | collective-permute-done | bytes 524320 | tf_op jit(solution)/shard_map/ppermute | solution.py:1012
  594.8 22.8 %collective-permute-done.15 = bf16[256,2048]{1,0:T(8,128)(2,1)} collective-permute-done((bf16[256,2048]{1,0:T(8,128)(2,1)S(1)}, bf16[256,2048]{1,0:T(8,128)(2,1)}, u32[]{:S(2)}, u32[]{:S(2)}) %collective-permute-start.15) | collective-permute-done | bytes 1048608 | tf_op jit(solution)/shard_map/ppermute | solution.py:1012
  649.1 7.7 %shard_map.318 = bf16[512,2048]{1,0:T(8,128)(2,1)S(1)} custom-call(bf16[1024,1024]{1,0:T(8,128)(2,1)S(1)} %copy-done.2, bf16[1024,1024]{1,0:T(8,128)(2,1)} %get-tuple-element.56.y.refs_1_.refs_2_, bf16[1024,2048]{1,0:T(8,128)(2,1)} %refs_2_.3, bf16[1024,2048]{1,0:T(8,128)(2,1)} %all-gather.6.cloned.1.call-done.b.refs_3_, ...), custom_call_target="tpu_custom_call" | custom-call | flops 50000000 | bytes 1000 | tf_op jit(solution)/shard_map/pallas_call | solution.py:523
  674.8 15.3 %all-gather.8.cloned.1.call-done = bf16[2816,1024]{1,0:T(8,128)(2,1)} async-done(((bf16[352,1024]{1,0:T(8,128)(2,1)}), bf16[2816,1024]{1,0:T(8,128)(2,1)}) %all-gather.8.cloned.1.call-update) | async-done | bytes 5767184 | tf_op jit(solution)/shard_map/all_gather | solution.py:1242
  (419 shorter events, 290.2 us)
Async XLA Ops:
  7.2 187.9 %all-gather.4.cloned.1.call-start = ((), (), s32[]{:S(2)}) async-start(), calls=%async_computation.4 | async-start | bytes 9437184 | tf_op jit(solution)/shard_map/all_gather | solution.py:1057
  7.2 83.4 %collective-permute-start = (bf16[512,2048]{1,0:T(8,128)(2,1)}, bf16[512,2048]{1,0:T(8,128)(2,1)}, u32[]{:S(2)}, u32[]{:S(2)}) collective-permute-start(bf16[512,2048]{1,0:T(8,128)(2,1)} %refs_0_.3), channel_id=1, source_target_pairs={{0,1},{1,0},{2,3},{3,2},{4,5},{5,4},{6,7},{7,6},{8,9},{9,8},{10,11... | collective-permute-start | bytes 6291464 | tf_op jit(solution)/shard_map/ppermute | solution.py:990
  12.8 77.1 %collective-permute-start.1 = (bf16[512,1024]{1,0:T(8,128)(2,1)}, bf16[512,1024]{1,0:T(8,128)(2,1)S(1)}, u32[]{:S(2)}, u32[]{:S(2)}) collective-permute-start(bf16[512,1024]{1,0:T(8,128)(2,1)} %pad_maximum_fusion.2), channel_id=1, source_target_pairs={{0,2},{1,3},{2,0},{3,1},{4,6},{5,7},{6,4},{7,5},{8,10},{9,11},{10,... | collective-permute-start | bytes 3145736 | tf_op jit(solution)/shard_map/ppermute | solution.py:990
  15.7 73.8 %collective-permute-start.2 = (bf16[16,2048]{0,1:T(8,128)(2,1)S(1)}, bf16[16,2048]{0,1:T(8,128)(2,1)S(1)}, u32[]{:S(2)}, u32[]{:S(2)}) collective-permute-start(bf16[16,2048]{0,1:T(8,128)(2,1)S(1)} %bitcast.121), channel_id=1, source_target_pairs={{0,2},{1,3},{2,0},{3,1},{4,6},{5,7},{6,4},{7,5},{8,10},{9,11},{10,... | collective-permute-start | bytes 196616 | tf_op jit(solution)/shard_map/ppermute | solution.py:990
  16.4 73.5 %collective-permute-start.3 = (f32[8,1024]{1,0:T(8,128)S(1)}, f32[8,1024]{1,0:T(8,128)S(1)}, u32[]{:S(2)}, u32[]{:S(2)}) collective-permute-start(f32[8,1024]{1,0:T(8,128)S(1)} %concatenate.104), channel_id=1, source_target_pairs={{0,2},{1,3},{2,0},{3,1},{4,6},{5,7},{6,4},{7,5},{8,10},{9,11},{10,... | collective-permute-start | bytes 98312 | tf_op jit(solution)/shard_map/ppermute | solution.py:990
  91.9 144.0 %all-gather.6.cloned.1.call-start = ((), (), s32[]{:S(2)}) async-start(), calls=%async_computation.5 | async-start | bytes 4718592 | tf_op jit(solution)/shard_map/all_gather | solution.py:1096
  96.3 59.0 %collective-permute-start.4 = (bf16[512,2048]{1,0:T(8,128)(2,1)}, bf16[512,2048]{1,0:T(8,128)(2,1)}, u32[]{:S(2)}, u32[]{:S(2)}) collective-permute-start(bf16[512,2048]{1,0:T(8,128)(2,1)} %shard_map.297.refs_6_), channel_id=1, source_target_pairs={{0,1},{1,0},{2,3},{3,2},{4,5},{5,4},{6,7},{7,6},{8,9},{9,8},{10,11... | collective-permute-start | bytes 6291464 | tf_op jit(solution)/shard_map/ppermute | solution.py:990
  113.6 62.7 %collective-permute-start.5 = (bf16[128,2048]{1,0:T(8,128)(2,1)}, bf16[128,2048]{1,0:T(8,128)(2,1)}, u32[]{:S(2)}, u32[]{:S(2)}) collective-permute-start(bf16[128,2048]{1,0:T(8,128)(2,1)} %constant_dynamic-slice_fusion), channel_id=1, source_target_pairs={{0,2},{1,3},{2,0},{3,1},{4,6},{5,7},{6,4},{7,5},{8,10},{9,11},{10,... | collective-permute-start | bytes 1572872 | tf_op jit(solution)/shard_map/ppermute | solution.py:990
  178.6 238.7 %reduce-scatter.7.cloned.1.call-start = ((), (), s32[]{:S(2)}) async-start(), calls=%async_computation.7 | async-start | bytes 5242880 | tf_op jit(solution)/shard_map/reduce_scatter | solution.py:1141
  288.8 157.8 %reduce-scatter.5.cloned.1.call-start = ((), (), s32[]{:S(2)}) async-start(), calls=%async_computation.6 | async-start | bytes 5242880 | tf_op jit(solution)/shard_map/reduce_scatter | solution.py:1141
  322.4 268.1 %reduce-scatter.11.cloned.1.call-start = ((), (), s32[]{:S(2)}) async-start(), calls=%async_computation.9 | async-start | bytes 4718592 | tf_op jit(solution)/shard_map/reduce_scatter | solution.py:1173
  368.8 257.5 %reduce-scatter.9.cloned.1.call-start = ((), (), s32[]{:S(2)}) async-start(), calls=%async_computation.8 | async-start | bytes 6488064 | tf_op jit(solution)/shard_map/reduce_scatter | solution.py:1225
  368.8 77.8 %collective-permute-start.8 = (bf16[512,2048]{1,0:T(8,128)(2,1)}, bf16[512,2048]{1,0:T(8,128)(2,1)}, u32[]{:S(2)}, u32[]{:S(2)}) collective-permute-start(bf16[512,2048]{1,0:T(8,128)(2,1)} %copy-done.38), channel_id=1, source_target_pairs={{0,1},{1,0},{2,3},{3,2},{4,5},{5,4},{6,7},{7,6},{8,9},{9,8},{10,11... | collective-permute-start | bytes 6291464 | tf_op jit(solution)/shard_map/ppermute | solution.py:990
  419.1 26.3 %collective-permute-start.10 = (bf16[128,2048]{1,0:T(8,128)(2,1)}, bf16[128,2048]{1,0:T(8,128)(2,1)}, u32[]{:S(2)}, u32[]{:S(2)}) collective-permute-start(bf16[128,2048]{1,0:T(8,128)(2,1)} %dynamic-slice_bitcast_fusion.1), channel_id=1, source_target_pairs={{0,2},{1,3},{2,0},{3,1},{4,6},{5,7},{6,4},{7,5},{8,10},{9,11},{10,... | collective-permute-start | bytes 1572872 | tf_op jit(solution)/shard_map/ppermute | solution.py:990
  468.5 51.3 %collective-permute-start.11 = (bf16[512,2048]{1,0:T(8,128)(2,1)}, bf16[512,2048]{1,0:T(8,128)(2,1)}, u32[]{:S(2)}, u32[]{:S(2)}) collective-permute-start(bf16[512,2048]{1,0:T(8,128)(2,1)} %get-tuple-element.81), channel_id=1, source_target_pairs={{0,1},{1,0},{2,3},{3,2},{4,5},{5,4},{6,7},{7,6},{8,9},{9,8},{10,11... | collective-permute-start | bytes 6291464 | tf_op jit(solution)/shard_map/ppermute | solution.py:990
  493.3 24.8 %collective-permute-start.12 = (f32[40,1024]{1,0:T(8,128)}, f32[40,1024]{1,0:T(8,128)}, u32[]{:S(2)}, u32[]{:S(2)}) collective-permute-start(f32[40,1024]{1,0:T(8,128)} %concatenate.122), channel_id=1, source_target_pairs={{0,2},{1,3},{2,0},{3,1},{4,6},{5,7},{6,4},{7,5},{8,10},{9,11},{10,... | collective-permute-start | bytes 491528 | tf_op jit(solution)/shard_map/ppermute | solution.py:990
  530.4 159.7 %all-gather.8.cloned.1.call-start = ((), (), s32[]{:S(2)}) async-start(), calls=%async_computation.10 | async-start | bytes 6488064 | tf_op jit(solution)/shard_map/all_gather | solution.py:1242
  533.4 25.4 %collective-permute-start.13 = (bf16[256,1024]{1,0:T(8,128)(2,1)S(1)}, bf16[256,1024]{1,0:T(8,128)(2,1)S(1)}, u32[]{:S(2)}, u32[]{:S(2)}) collective-permute-start(bf16[256,1024]{1,0:T(8,128)(2,1)S(1)} %dynamic-slice_bitcast_fusion), channel_id=1, source_target_pairs={{0,2},{1,3},{2,0},{3,1},{4,6},{5,7},{6,4},{7,5},{8,10},{9,11},{10,... | collective-permute-start | bytes 1572872 | tf_op jit(solution)/shard_map/ppermute | solution.py:990
  560.1 23.3 %collective-permute-start.14 = (bf16[128,2048]{1,0:T(8,128)(2,1)S(1)}, bf16[128,2048]{1,0:T(8,128)(2,1)}, u32[]{:S(2)}, u32[]{:S(2)}) collective-permute-start(bf16[128,2048]{1,0:T(8,128)(2,1)S(1)} %shard_map.331), channel_id=1, source_target_pairs={{0,8},{4,12},{8,0},{12,4},{16,24},{20,28},{24,16},{28,20},{1,9},{5... | collective-permute-start | bytes 1572872 | tf_op jit(solution)/shard_map/ppermute | solution.py:1012
  561.8 25.0 %collective-permute-start.16 = (bf16[256,1024]{1,0:T(8,128)(2,1)}, bf16[256,1024]{1,0:T(8,128)(2,1)}, u32[]{:S(2)}, u32[]{:S(2)}) collective-permute-start(bf16[256,1024]{1,0:T(8,128)(2,1)} %shard_map.330.refs_1_), channel_id=1, source_target_pairs={{0,16},{4,20},{8,24},{12,28},{16,0},{20,4},{24,8},{28,12},{1,17},{... | collective-permute-start | bytes 1572872 | tf_op jit(solution)/shard_map/ppermute | solution.py:1012
  585.3 32.3 %collective-permute-start.15 = (bf16[256,2048]{1,0:T(8,128)(2,1)S(1)}, bf16[256,2048]{1,0:T(8,128)(2,1)}, u32[]{:S(2)}, u32[]{:S(2)}) collective-permute-start(bf16[256,2048]{1,0:T(8,128)(2,1)S(1)} %maximum_select_fusion.2.refs_1_), channel_id=1, source_target_pairs={{0,16},{4,20},{8,24},{12,28},{16,0},{20,4},{24,8},{28,12},{1,17},{... | collective-permute-start | bytes 3145736 | tf_op jit(solution)/shard_map/ppermute | solution.py:1012
  590.0 31.7 %collective-permute-start.17 = (bf16[512,1024]{1,0:T(8,128)(2,1)}, bf16[512,1024]{1,0:T(8,128)(2,1)}, u32[]{:S(2)}, u32[]{:S(2)}) collective-permute-start(bf16[512,1024]{1,0:T(8,128)(2,1)} %maximum_select_fusion.3.refs_2_), channel_id=1, source_target_pairs={{0,8},{4,12},{8,0},{12,4},{16,24},{20,28},{24,16},{28,20},{1,9},{5... | collective-permute-start | bytes 3145736 | tf_op jit(solution)/shard_map/ppermute | solution.py:1012
  592.4 46.3 %collective-permute-start.18 = (bf16[256,1024]{1,0:T(8,128)(2,1)}, bf16[256,1024]{1,0:T(8,128)(2,1)}, u32[]{:S(2)}, u32[]{:S(2)}) collective-permute-start(bf16[256,1024]{1,0:T(8,128)(2,1)} %shard_map.333), channel_id=1, source_target_pairs={{0,2},{1,3},{2,0},{3,1},{4,6},{5,7},{6,4},{7,5},{8,10},{9,11},{10,... | collective-permute-start | bytes 1572872 | tf_op jit(solution)/shard_map/ppermute | solution.py:990
  646.5 24.7 %collective-permute-start.22 = (bf16[512,2048]{1,0:T(8,128)(2,1)}, bf16[512,2048]{1,0:T(8,128)(2,1)S(1)}, u32[]{:S(2)}, u32[]{:S(2)}) collective-permute-start(bf16[512,2048]{1,0:T(8,128)(2,1)} %maximum_select_fusion.refs_1_.a), channel_id=1, source_target_pairs={{0,4},{4,0},{8,12},{12,8},{16,20},{20,16},{24,28},{28,24},{1,5},{5... | collective-permute-start | bytes 6291464 | tf_op jit(solution)/shard_map/ppermute | solution.py:1012
  (111 other events, 763.6 us)
Sparse Core Ops, SparseCore 0:
  92.0 55.8 all-gather.3
  178.7 37.1 all-gather.5
  289.0 53.7 reduce-scatter.6
  345.8 52.6 reduce-scatter.4
  401.7 51.3 reduce-scatter.10
  530.6 77.6 reduce-scatter.8
  646.5 43.5 all-gather.7

commit v4 on v3

--- a/solution.py
+++ b/solution.py
@@ -1173,7 +1173,6 @@
     far_piece = lax.psum_scatter(far_cut.reshape(-1, channels), "batch", scatter_dimension=0, tiled=True)
     far_out = send_far(part_out, back[1][0])
     back[0] = scan_back(0, (far_cut,))
-    total_out = added(part_out[0], far_out, (back[0][0],))
     d_pairs, g_bc = pair_backward(per_block, info, pairs, back[0][1], back[1][1], par_bc)
     heads_out = [b[3].reshape(-1, 16, SEQ_LEN) for b in back]
     d_step = jnp.concatenate([h[:, :GROUP].reshape(-1, SEQ_LEN) for h in heads_out], axis=0)
@@ -1186,7 +1185,7 @@
     d_rates = d_rates_pre.astype(BF16)
     d_small = jnp.concatenate([d_pairs, d_rates.T], axis=1)
 
-    g_small = small_grads(d_small, normed, (part_z, total_out, branch_got))
+    g_small = small_grads(d_small, normed, (part_z, branch_got))
 
     def pack(i):
         gp = back[i][2]
@@ -1221,10 +1220,11 @@
     bc_rows, few_rows = 2 * STATE * width_in // channels, 8 * 2 * STATE // channels
     shared = spread(jnp.concatenate([g_small[: 2 * STATE].reshape(-1, channels), g_bc.reshape(-1, channels), sum(norm_sums)[:1].reshape(-1, channels)], axis=0))
     private = spread(pack(0) + delayed(across(pack(1), far_bit), (norm_sums[-1],)))
-    own_cut = grad_pieces(normed, back[0][0], jnp.concatenate([shared, private], axis=1), batches, bits, (d_normed_got,))
+    own_cut = grad_pieces(normed, back[0][0], jnp.concatenate([shared, private], axis=1), batches, bits, (d_normed_got, far_z, far_out))
     own_part = lax.psum_scatter(own_cut.reshape(-1, channels), "batch", scatter_dimension=0, tiled=True)
     seen = []
     total_z = added(part_z[0], far_z, (norm_sums[-1],))
+    total_out = added(part_out[0], far_out, (norm_sums[-1],))
     total_out = delayed(total_out, (total_z,))
     halves_here, halves_there = gather_both([total_out, total_z], seen)
     own_part = delayed(own_part, halves_here)

time: 730 us -> 710 us (0.973)
  local copies, waits for them, and re-layouts: 118 us -> 107 us
    ppermute x15, waiting for transfers between devices: 131 us -> 119 us  [across(): return lax.ppermute(v, 'head', [(i, i ^ bit) for i in range(stacks)])]
    reduce_scatter x1, waiting for transfers between devices: 0.01 us -> 7.34 us  [body(): lax.psum_scatter(own_cut.reshape(-1, channels), 'batch', scatter_dimensio...]
    unnamed x212 -> x188, local copies, waits for them, and re-layouts: 60.3 us -> 59.8 us
  transfers between devices with their start and end apart: 30 -> 30, of which waited for: 14 -> 15; matrix products, arithmetic and copies ran while one was open for 12% -> 11% of each run, Pallas kernels for 38% -> 37%
where the time goes in v4:
time: 710 us; the launch traced here: 697 us
  Pallas kernels  308 us (43%)
  waiting for transfers between devices  189 us (27%)
  local copies, waits for them, and re-layouts  107 us (15%)
  other arithmetic  39.1 us (6%)
  starting transfers between devices  34.9 us (5%)
  between operations  19.1 us (3%)
    ppermute x15, waiting for transfers between devices, across(): return lax.ppermute(v, 'head', [(i, i ^ bit) for i in range(stacks)])  119 us
    pallas_call x6, Pallas kernels, call(): pl.pallas_call(kernel, grid_spec=pltpu.PrefetchScalarGridSpec(num_scalar_...  110 us
    unnamed x188, local copies, waits for them, and re-layouts  59.8 us
    ppermute x8, waiting for transfers between devices, planar(): return lax.ppermute(v, 'batch', [(i, i ^ bit) for i in range(batches)])  46.8 us
    pallas_call x4, Pallas kernels, grad_half(): pl.pallas_call(ignore(kernel, 1 + len(operands), len(later)), grid_spec=p...  34.1 us
    pallas_call x4, Pallas kernels, project(): pl.pallas_call(ignore(kernel, 2, len(later)), grid=(columns // wide,), in...  32.2 us
    pallas_call x2, Pallas kernels, rows_back(): pl.pallas_call(ignore(kernel, 2 * count + 1, len(later)), grid=(columns /...  29.7 us
    ppermute x15, starting transfers between devices, across(): return lax.ppermute(v, 'head', [(i, i ^ bit) for i in range(stacks)])  27.2 us
  transfers between devices with their start and end apart: 30, of which 15 were waited for; matrix products, arithmetic and copies ran while one was open for 11% of the time, Pallas kernels for 37%

profile of v4, /device:TPU:0, one launch (start us, length us, event | category | flops | bytes accessed | tf_op | source)
XLA Modules:
  0.0 697.4 jit_solution(4849584006963308891)
XLA Ops:
  19.0 70.5 %collective-permute-done.2 = bf16[16,2048]{0,1:T(8,128)(2,1)S(1)} collective-permute-done((bf16[16,2048]{0,1:T(8,128)(2,1)S(1)}, bf16[16,2048]{0,1:T(8,128)(2,1)S(1)}, u32[]{:S(2)}, u32[]{:S(2)}) %collective-permute-start.2) | collective-permute-done | bytes 65568 | tf_op jit(solution)/shard_map/ppermute | solution.py:990
  132.5 8.4 %shard_map.302.refs_2_.refs_1_ = bf16[1024,1024]{1,0:T(8,128)(2,1)S(1)} custom-call(bf16[1024,2048]{1,0:T(8,128)(2,1)} %shard_map.298.x.refs_0_.refs_1_.a.refs_10_, bf16[2048,1024]{1,0:T(8,128)(2,1)} %refs_5_.3, bf16[1024,1024]{1,0:T(8,128)(2,1)S(1)} %shard_map.301.refs_2_.refs_1_), custom_call_target="tpu_custom_call" | custom-call | flops 60000000 | bytes 1000 | tf_op jit(solution)/shard_map/pallas_call | solution.py:437
  143.1 12.4 %collective-permute-done.4.refs_7_ = bf16[512,2048]{1,0:T(8,128)(2,1)} collective-permute-done((bf16[512,2048]{1,0:T(8,128)(2,1)}, bf16[512,2048]{1,0:T(8,128)(2,1)}, u32[]{:S(2)}, u32[]{:S(2)}) %collective-permute-start.4) | collective-permute-done | bytes 2097184 | tf_op jit(solution)/shard_map/ppermute | solution.py:990
  155.4 19.1 %shard_map.303 = (bf16[1024,1024]{1,0:T(8,128)(2,1)S(1)}, bf16[1024,1024]{1,0:T(8,128)(2,1)}, bf16[1024,1024]{1,0:T(8,128)(2,1)}, bf16[512,1024]{1,0:T(8,128)(2,1)S(1)}, f32[1024,128]{1,0:T(8,128)S(1)}) custom-call(s32[5]{0:T(128)S(1)} %pad_add_fusion.info.refs_0_, bf16[1024,1024]{1,0:T(8,128)(2,1)} %copy-done.10, bf16[1024,1024]{1,0:T(8,128)(2,1)} %copy-done.22, ...), custom_call_target="tpu_custom_call" | custom-call | flops 200000000 | bytes 1000 | tf_op jit(solution)/shard_map/pallas_call | solution.py:406
  184.7 8.2 %shard_map.306 = (bf16[1024,1024]{1,0:T(8,128)(2,1)S(1)}, f32[1024,128]{1,0:T(8,128)S(1)}) custom-call(bf16[1024,2048]{1,0:T(8,128)(2,1)} %copy-done.70, bf16[1024,2048]{1,0:T(8,128)(2,1)} %refs_2_.3, bf16[1024,1024]{1,0:T(8,128)(2,1)S(1)} %copy-done.2), custom_call_target="tpu_custom_call" | custom-call | flops 80000000 | bytes 1000 | tf_op jit(solution)/shard_map/pallas_call | solution.py:495
  196.6 7.7 %shard_map.307.refs_2_.inner.refs_1_ = bf16[1024,1024]{1,0:T(8,128)(2,1)S(1)} custom-call(bf16[1024,2048]{1,0:T(8,128)(2,1)} %shard_map.298.x.refs_0_.refs_1_.a.refs_10_, bf16[8,2,256,1024]{3,2,1,0:T(8,128)(2,1)} %bitcast.106, bf16[1024,1024]{1,0:T(8,128)(2,1)S(1)} %copy-done.35), custom_call_target="tpu_custom_call" | custom-call | flops 60000000 | bytes 1000 | tf_op jit(solution)/shard_map/pallas_call | solution.py:437
  204.3 8.5 %shard_map.308.gate.refs_1_ = bf16[1024,1024]{1,0:T(8,128)(2,1)S(1)} custom-call(bf16[1024,2048]{1,0:T(8,128)(2,1)} %shard_map.298.x.refs_0_.refs_1_.a.refs_10_, bf16[8,2,256,1024]{3,2,1,0:T(8,128)(2,1)} %bitcast.107, bf16[1024,1024]{1,0:T(8,128)(2,1)S(1)} %shard_map.307.refs_2_.inner.refs_1_), custom_call_target="tpu_custom_call" | custom-call | flops 60000000 | bytes 1000 | tf_op jit(solution)/shard_map/pallas_call | solution.py:437
  214.2 19.2 %shard_map.309 = (bf16[1024,1024]{1,0:T(8,128)(2,1)S(1)}, bf16[1024,1024]{1,0:T(8,128)(2,1)}, bf16[1024,1024]{1,0:T(8,128)(2,1)}, bf16[512,1024]{1,0:T(8,128)(2,1)S(1)}, f32[1024,128]{1,0:T(8,128)S(1)}) custom-call(s32[5]{0:T(128)S(1)} %pad_add_fusion.info.refs_0_, bf16[1024,1024]{1,0:T(8,128)(2,1)} %copy-done.12, bf16[1024,1024]{1,0:T(8,128)(2,1)} %copy-done.23, ...), custom_call_target="tpu_custom_call" | custom-call | flops 200000000 | bytes 1000 | tf_op jit(solution)/shard_map/pallas_call | solution.py:406
  237.6 7.9 %shard_map.311 = (bf16[1024,1024]{1,0:T(8,128)(2,1)S(1)}, f32[1024,128]{1,0:T(8,128)S(1)}) custom-call(bf16[1024,2048]{1,0:T(8,128)(2,1)} %copy-done.70, bf16[1024,2048]{1,0:T(8,128)(2,1)} %all-gather.6.cloned.1.call-done.b.refs_3_, bf16[1024,1024]{1,0:T(8,128)(2,1)S(1)} %copy-done.3), custom_call_target="tpu_custom_call" | custom-call | flops 80000000 | bytes 1000 | tf_op jit(solution)/shard_map/pallas_call | solution.py:495
  258.7 8.8 %shard_map.313.refs_5_ = bf16[4,2,128,2048]{3,2,1,0:T(8,128)(2,1)} custom-call(s32[1]{0:T(128)} %bitcast.20.refs_0_, bf16[1024,1024]{1,0:T(8,128)(2,1)S(1)} %copy-done.2, bf16[1024,1024]{1,0:T(8,128)(2,1)S(1)} %copy-done.4, bf16[1024,2048]{1,0:T(8,128)(2,1)} %copy-done.70, f32[8,1024]{1,0:T(8,128)S(1)} %maximum_maximum_fusion.refs_4_.refs_3_.refs_5_, ...), custom_call_target="tpu_custom_call" | custom-call | flops 70000000 | bytes 1000 | tf_op jit(solution)/shard_map/pallas_call | solution.py:760
  287.3 9.8 %shard_map.316.refs_4_ = bf16[4,2,128,2048]{3,2,1,0:T(8,128)(2,1)} custom-call(s32[1]{0:T(128)} %bitcast.24.refs_0_.info, bf16[1024,1024]{1,0:T(8,128)(2,1)S(1)} %copy-done.2, bf16[1024,1024]{1,0:T(8,128)(2,1)S(1)} %copy-done.5, bf16[1024,2048]{1,0:T(8,128)(2,1)} %copy-done.70, bf16[4,2,128,2048]{3,2,1,0:T(8,128)(2,1)} %copy-done.73, ...), custom_call_target="tpu_custom_call" | custom-call | flops 70000000 | bytes 1000 | tf_op jit(solution)/shard_map/pallas_call | solution.py:760
  313.9 8.1 %shard_map.319.refs_9_ = bf16[4,2,256,1024]{3,2,1,0:T(8,128)(2,1)} custom-call(s32[1]{0:T(128)} %bitcast.24.refs_0_.info, bf16[1024,2048]{1,0:T(8,128)(2,1)} %shard_map.298.x.refs_0_.refs_1_.a.refs_10_, bf16[1024,1024]{1,0:T(8,128)(2,1)S(1)} %copy-done.7, bf16[1024,1024]{1,0:T(8,128)(2,1)S(1)} %get-tuple-element.66.refs_3_.refs_1_, ...), custom_call_target="tpu_custom_call" | custom-call | flops 70000000 | bytes 1000 | tf_op jit(solution)/shard_map/pallas_call | solution.py:760
  324.8 33.0 %shard_map.320 = (bf16[1024,1024]{1,0:T(8,128)(2,1)S(1)}, f32[1024,256]{1,0:T(8,128)S(1)}, f32[8,1024]{1,0:T(8,128)S(1)}, f32[64,1024]{1,0:T(8,128)S(1)}) custom-call(s32[5]{0:T(128)S(1)} %pad_add_fusion.info.refs_0_, bf16[1024,1024]{1,0:T(8,128)(2,1)} %copy-done.12, bf16[1024,1024]{1,0:T(8,128)(2,1)} %copy-done.43, bf16[1024,1024]{1,0:T(8,128)(2,1)} %copy-done.45, ...), custom_call_target="tpu_custom_call" | custom-call | flops 360000000 | bytes 1000 | tf_op jit(solution)/shard_map/pallas_call | solution.py:406
  357.9 10.5 %shard_map.321.refs_9_ = bf16[8,256,1024]{2,1,0:T(8,128)(2,1)} custom-call(bf16[1024,2048]{1,0:T(8,128)(2,1)} %shard_map.298.x.refs_0_.refs_1_.a.refs_10_, bf16[1024,1024]{1,0:T(8,128)(2,1)S(1)} %get-tuple-element.72.b.refs_3_), custom_call_target="tpu_custom_call" | custom-call | flops 100000000 | bytes 1000 | tf_op jit(solution)/shard_map/pallas_call | solution.py:804
  376.5 33.0 %shard_map.322 = (bf16[1024,1024]{1,0:T(8,128)(2,1)S(1)}, f32[1024,256]{1,0:T(8,128)S(1)}, f32[8,1024]{1,0:T(8,128)S(1)}, f32[64,1024]{1,0:T(8,128)S(1)}) custom-call(s32[5]{0:T(128)S(1)} %pad_add_fusion.info.refs_0_, bf16[1024,1024]{1,0:T(8,128)(2,1)} %copy-done.10, bf16[1024,1024]{1,0:T(8,128)(2,1)} %copy-done.33, bf16[1024,1024]{1,0:T(8,128)(2,1)} %copy-done.44, ...), custom_call_target="tpu_custom_call" | custom-call | flops 360000000 | bytes 1000 | tf_op jit(solution)/shard_map/pallas_call | solution.py:406
  430.7 15.2 %shard_map.325 = (bf16[512,2048]{1,0:T(8,128)(2,1)}, f32[8,2048]{1,0:T(8,128)S(1)}) custom-call(bf16[1024,1024]{1,0:T(8,128)(2,1)} %copy-done.6, bf16[1024,1024]{1,0:T(8,128)(2,1)} %copy-done.11, bf16[1024,1024]{1,0:T(8,128)(2,1)} %copy-done.25, bf16[1024,1024]{1,0:T(8,128)(2,1)} %copy-done.24, bf16[1024,288]{1,0:T(8,128)(2,1)S(1)} %pad_maximum_fusion.3.refs_0_.refs_4_, ...), custom_call_target="tpu_custom_call" | custom-call | flops 150000000 | bytes 1000 | tf_op jit(solution)/shard_map/pallas_call | solution.py:922
  474.0 14.5 %shard_map.326 = (bf16[512,2048]{1,0:T(8,128)(2,1)S(1)}, f32[8,2048]{1,0:T(8,128)S(1)}) custom-call(bf16[1024,1024]{1,0:T(8,128)(2,1)} %copy-done.6, bf16[1024,1024]{1,0:T(8,128)(2,1)} %copy-done.11, bf16[1024,1024]{1,0:T(8,128)(2,1)} %copy-done.25, bf16[1024,1024]{1,0:T(8,128)(2,1)} %copy-done.24, bf16[1024,288]{1,0:T(8,128)(2,1)S(1)} %pad_maximum_fusion.3.refs_0_.refs_4_, ...), custom_call_target="tpu_custom_call" | custom-call | flops 150000000 | bytes 1000 | tf_op jit(solution)/shard_map/pallas_call | solution.py:922
  493.6 13.4 %collective-permute-done.11.refs_0_ = f32[40,1024]{1,0:T(8,128)} collective-permute-done((f32[40,1024]{1,0:T(8,128)}, f32[40,1024]{1,0:T(8,128)}, u32[]{:S(2)}, u32[]{:S(2)}) %collective-permute-start.11) | collective-permute-done | bytes 163872 | tf_op jit(solution)/shard_map/ppermute | solution.py:990
  508.1 9.5 %collective-permute-done.12.refs_4_.refs_1_ = bf16[256,1024]{1,0:T(8,128)(2,1)} collective-permute-done((bf16[256,1024]{1,0:T(8,128)(2,1)}, bf16[256,1024]{1,0:T(8,128)(2,1)}, u32[]{:S(2)}, u32[]{:S(2)}) %collective-permute-start.12) | collective-permute-done | bytes 524320 | tf_op jit(solution)/shard_map/ppermute | solution.py:990
  519.8 10.6 %shard_map.328 = bf16[8,352,1024]{2,1,0:T(8,128)(2,1)} custom-call(bf16[1024,2048]{1,0:T(8,128)(2,1)} %shard_map.298.x.refs_0_.refs_1_.a.refs_10_, bf16[1024,1024]{1,0:T(8,128)(2,1)S(1)} %copy-done.26, bf16[8,96,1024]{2,1,0:T(8,128)(2,1)S(1)} %pad_maximum_fusion.1.refs_2_, bf16[512,2048]{1,0:T(8,128)(2,1)} %collective-permute-done.10.refs_3_, ...), custom_call_target="tpu_custom_call" | custom-call | flops 100000000 | bytes 1000 | tf_op jit(solution)/shard_map/pallas_call | solution.py:804
  537.4 10.1 %collective-permute-done.14 = bf16[128,2048]{1,0:T(8,128)(2,1)} collective-permute-done((bf16[128,2048]{1,0:T(8,128)(2,1)S(1)}, bf16[128,2048]{1,0:T(8,128)(2,1)}, u32[]{:S(2)}, u32[]{:S(2)}) %collective-permute-start.14) | collective-permute-done | bytes 524320 | tf_op jit(solution)/shard_map/ppermute | solution.py:1012
  559.3 29.2 %collective-permute-done.15 = bf16[256,2048]{1,0:T(8,128)(2,1)} collective-permute-done((bf16[256,2048]{1,0:T(8,128)(2,1)S(1)}, bf16[256,2048]{1,0:T(8,128)(2,1)}, u32[]{:S(2)}, u32[]{:S(2)}) %collective-permute-start.15) | collective-permute-done | bytes 1048608 | tf_op jit(solution)/shard_map/ppermute | solution.py:1012
  629.0 7.7 %shard_map.318 = bf16[512,2048]{1,0:T(8,128)(2,1)S(1)} custom-call(bf16[1024,1024]{1,0:T(8,128)(2,1)S(1)} %copy-done.2, bf16[1024,1024]{1,0:T(8,128)(2,1)} %get-tuple-element.56.y.refs_1_.refs_2_, bf16[1024,2048]{1,0:T(8,128)(2,1)} %refs_2_.3, bf16[1024,2048]{1,0:T(8,128)(2,1)} %all-gather.6.cloned.1.call-done.b.refs_3_, ...), custom_call_target="tpu_custom_call" | custom-call | flops 50000000 | bytes 1000 | tf_op jit(solution)/shard_map/pallas_call | solution.py:523
  654.6 15.1 %all-gather.8.cloned.1.call-done = bf16[2816,1024]{1,0:T(8,128)(2,1)} async-done(((bf16[352,1024]{1,0:T(8,128)(2,1)}), bf16[2816,1024]{1,0:T(8,128)(2,1)}) %all-gather.8.cloned.1.call-update) | async-done | bytes 5767184 | tf_op jit(solution)/shard_map/all_gather | solution.py:1242
  (395 shorter events, 288.1 us)
Async XLA Ops:
  7.2 187.8 %all-gather.4.cloned.1.call-start = ((), (), s32[]{:S(2)}) async-start(), calls=%async_computation.4 | async-start | bytes 9437184 | tf_op jit(solution)/shard_map/all_gather | solution.py:1057
  7.2 83.4 %collective-permute-start = (bf16[512,2048]{1,0:T(8,128)(2,1)}, bf16[512,2048]{1,0:T(8,128)(2,1)}, u32[]{:S(2)}, u32[]{:S(2)}) collective-permute-start(bf16[512,2048]{1,0:T(8,128)(2,1)} %refs_0_.3), channel_id=1, source_target_pairs={{0,1},{1,0},{2,3},{3,2},{4,5},{5,4},{6,7},{7,6},{8,9},{9,8},{10,11... | collective-permute-start | bytes 6291464 | tf_op jit(solution)/shard_map/ppermute | solution.py:990
  12.8 77.1 %collective-permute-start.1 = (bf16[512,1024]{1,0:T(8,128)(2,1)}, bf16[512,1024]{1,0:T(8,128)(2,1)S(1)}, u32[]{:S(2)}, u32[]{:S(2)}) collective-permute-start(bf16[512,1024]{1,0:T(8,128)(2,1)} %pad_maximum_fusion.2), channel_id=1, source_target_pairs={{0,2},{1,3},{2,0},{3,1},{4,6},{5,7},{6,4},{7,5},{8,10},{9,11},{10,... | collective-permute-start | bytes 3145736 | tf_op jit(solution)/shard_map/ppermute | solution.py:990
  15.7 73.8 %collective-permute-start.2 = (bf16[16,2048]{0,1:T(8,128)(2,1)S(1)}, bf16[16,2048]{0,1:T(8,128)(2,1)S(1)}, u32[]{:S(2)}, u32[]{:S(2)}) collective-permute-start(bf16[16,2048]{0,1:T(8,128)(2,1)S(1)} %bitcast.121), channel_id=1, source_target_pairs={{0,2},{1,3},{2,0},{3,1},{4,6},{5,7},{6,4},{7,5},{8,10},{9,11},{10,... | collective-permute-start | bytes 196616 | tf_op jit(solution)/shard_map/ppermute | solution.py:990
  16.4 73.5 %collective-permute-start.3 = (f32[8,1024]{1,0:T(8,128)S(1)}, f32[8,1024]{1,0:T(8,128)S(1)}, u32[]{:S(2)}, u32[]{:S(2)}) collective-permute-start(f32[8,1024]{1,0:T(8,128)S(1)} %concatenate.104), channel_id=1, source_target_pairs={{0,2},{1,3},{2,0},{3,1},{4,6},{5,7},{6,4},{7,5},{8,10},{9,11},{10,... | collective-permute-start | bytes 98312 | tf_op jit(solution)/shard_map/ppermute | solution.py:990
  92.0 144.1 %all-gather.6.cloned.1.call-start = ((), (), s32[]{:S(2)}) async-start(), calls=%async_computation.5 | async-start | bytes 4718592 | tf_op jit(solution)/shard_map/all_gather | solution.py:1096
  96.4 59.0 %collective-permute-start.4 = (bf16[512,2048]{1,0:T(8,128)(2,1)}, bf16[512,2048]{1,0:T(8,128)(2,1)}, u32[]{:S(2)}, u32[]{:S(2)}) collective-permute-start(bf16[512,2048]{1,0:T(8,128)(2,1)} %shard_map.297.refs_6_), channel_id=1, source_target_pairs={{0,1},{1,0},{2,3},{3,2},{4,5},{5,4},{6,7},{7,6},{8,9},{9,8},{10,11... | collective-permute-start | bytes 6291464 | tf_op jit(solution)/shard_map/ppermute | solution.py:990
  113.6 62.8 %collective-permute-start.5 = (bf16[128,2048]{1,0:T(8,128)(2,1)}, bf16[128,2048]{1,0:T(8,128)(2,1)}, u32[]{:S(2)}, u32[]{:S(2)}) collective-permute-start(bf16[128,2048]{1,0:T(8,128)(2,1)} %constant_dynamic-slice_fusion), channel_id=1, source_target_pairs={{0,2},{1,3},{2,0},{3,1},{4,6},{5,7},{6,4},{7,5},{8,10},{9,11},{10,... | collective-permute-start | bytes 1572872 | tf_op jit(solution)/shard_map/ppermute | solution.py:990
  178.6 245.5 %reduce-scatter.5.cloned.1.call-start = ((), (), s32[]{:S(2)}) async-start(), calls=%async_computation.6 | async-start | bytes 5242880 | tf_op jit(solution)/shard_map/reduce_scatter | solution.py:1141
  267.5 17.8 %collective-permute-start.7 = (bf16[4,2,128,2048]{3,2,1,0:T(8,128)(2,1)}, bf16[4,2,128,2048]{3,2,1,0:T(8,128)(2,1)S(1)}, u32[]{:S(2)}, u32[]{:S(2)}) collective-permute-start(bf16[4,2,128,2048]{3,2,1,0:T(8,128)(2,1)} %shard_map.313.refs_5_), channel_id=1, source_target_pairs={{0,4},{4,0},{8,12},{12,8},{16,20},{20,16},{24,28},{28,24},{1,5},{5... | collective-permute-start | bytes 12582920 | tf_op jit(solution)/shard_map/ppermute | solution.py:1012
  322.0 127.8 %reduce-scatter.7.cloned.1.call-start = ((), (), s32[]{:S(2)}) async-start(), calls=%async_computation.7 | async-start | bytes 5242880 | tf_op jit(solution)/shard_map/reduce_scatter | solution.py:1141
  322.6 233.0 %reduce-scatter.11.cloned.1.call-start = ((), (), s32[]{:S(2)}) async-start(), calls=%async_computation.9 | async-start | bytes 4718592 | tf_op jit(solution)/shard_map/reduce_scatter | solution.py:1173
  368.4 236.9 %reduce-scatter.9.cloned.1.call-start = ((), (), s32[]{:S(2)}) async-start(), calls=%async_computation.8 | async-start | bytes 6488064 | tf_op jit(solution)/shard_map/reduce_scatter | solution.py:1224
  368.4 55.6 %collective-permute-start.8 = (bf16[512,2048]{1,0:T(8,128)(2,1)}, bf16[512,2048]{1,0:T(8,128)(2,1)}, u32[]{:S(2)}, u32[]{:S(2)}) collective-permute-start(bf16[512,2048]{1,0:T(8,128)(2,1)} %copy-done.37), channel_id=1, source_target_pairs={{0,1},{1,0},{2,3},{3,2},{4,5},{5,4},{6,7},{7,6},{8,9},{9,8},{10,11... | collective-permute-start | bytes 6291464 | tf_op jit(solution)/shard_map/ppermute | solution.py:990
  445.9 73.9 %collective-permute-start.10 = (bf16[512,2048]{1,0:T(8,128)(2,1)}, bf16[512,2048]{1,0:T(8,128)(2,1)}, u32[]{:S(2)}, u32[]{:S(2)}) collective-permute-start(bf16[512,2048]{1,0:T(8,128)(2,1)} %get-tuple-element.81), channel_id=1, source_target_pairs={{0,1},{1,0},{2,3},{3,2},{4,5},{5,4},{6,7},{7,6},{8,9},{9,8},{10,11... | collective-permute-start | bytes 6291464 | tf_op jit(solution)/shard_map/ppermute | solution.py:990
  451.8 56.3 %collective-permute-start.13 = (bf16[128,2048]{1,0:T(8,128)(2,1)}, bf16[128,2048]{1,0:T(8,128)(2,1)S(1)}, u32[]{:S(2)}, u32[]{:S(2)}) collective-permute-start(bf16[128,2048]{1,0:T(8,128)(2,1)} %dynamic-slice_bitcast_fusion), channel_id=1, source_target_pairs={{0,2},{1,3},{2,0},{3,1},{4,6},{5,7},{6,4},{7,5},{8,10},{9,11},{10,... | collective-permute-start | bytes 1572872 | tf_op jit(solution)/shard_map/ppermute | solution.py:990
  466.9 40.0 %collective-permute-start.11 = (f32[40,1024]{1,0:T(8,128)}, f32[40,1024]{1,0:T(8,128)}, u32[]{:S(2)}, u32[]{:S(2)}) collective-permute-start(f32[40,1024]{1,0:T(8,128)} %concatenate.122), channel_id=1, source_target_pairs={{0,2},{1,3},{2,0},{3,1},{4,6},{5,7},{6,4},{7,5},{8,10},{9,11},{10,... | collective-permute-start | bytes 491528 | tf_op jit(solution)/shard_map/ppermute | solution.py:990
  468.8 48.8 %collective-permute-start.12 = (bf16[256,1024]{1,0:T(8,128)(2,1)}, bf16[256,1024]{1,0:T(8,128)(2,1)}, u32[]{:S(2)}, u32[]{:S(2)}) collective-permute-start(bf16[256,1024]{1,0:T(8,128)(2,1)} %dynamic-slice_bitcast_fusion.1), channel_id=1, source_target_pairs={{0,2},{1,3},{2,0},{3,1},{4,6},{5,7},{6,4},{7,5},{8,10},{9,11},{10,... | collective-permute-start | bytes 1572872 | tf_op jit(solution)/shard_map/ppermute | solution.py:990
  530.4 139.3 %all-gather.8.cloned.1.call-start = ((), (), s32[]{:S(2)}) async-start(), calls=%async_computation.10 | async-start | bytes 6488064 | tf_op jit(solution)/shard_map/all_gather | solution.py:1242
  549.4 39.0 %collective-permute-start.15 = (bf16[256,2048]{1,0:T(8,128)(2,1)S(1)}, bf16[256,2048]{1,0:T(8,128)(2,1)}, u32[]{:S(2)}, u32[]{:S(2)}) collective-permute-start(bf16[256,2048]{1,0:T(8,128)(2,1)S(1)} %maximum_select_fusion.2.refs_1_), channel_id=1, source_target_pairs={{0,16},{4,20},{8,24},{12,28},{16,0},{20,4},{24,8},{28,12},{1,17},{... | collective-permute-start | bytes 3145736 | tf_op jit(solution)/shard_map/ppermute | solution.py:1012
  553.9 38.9 %collective-permute-start.17 = (bf16[512,1024]{1,0:T(8,128)(2,1)}, bf16[512,1024]{1,0:T(8,128)(2,1)}, u32[]{:S(2)}, u32[]{:S(2)}) collective-permute-start(bf16[512,1024]{1,0:T(8,128)(2,1)} %maximum_select_fusion.3.refs_2_), channel_id=1, source_target_pairs={{0,8},{4,12},{8,0},{12,4},{16,24},{20,28},{24,16},{28,20},{1,9},{5... | collective-permute-start | bytes 3145736 | tf_op jit(solution)/shard_map/ppermute | solution.py:1012
  557.4 60.8 %collective-permute-start.18 = (bf16[256,1024]{1,0:T(8,128)(2,1)}, bf16[256,1024]{1,0:T(8,128)(2,1)}, u32[]{:S(2)}, u32[]{:S(2)}) collective-permute-start(bf16[256,1024]{1,0:T(8,128)(2,1)} %shard_map.333), channel_id=1, source_target_pairs={{0,2},{1,3},{2,0},{3,1},{4,6},{5,7},{6,4},{7,5},{8,10},{9,11},{10,... | collective-permute-start | bytes 1572872 | tf_op jit(solution)/shard_map/ppermute | solution.py:990
  626.3 20.2 %collective-permute-start.21 = (bf16[1024,1024]{1,0:T(8,128)(2,1)}, bf16[1024,1024]{1,0:T(8,128)(2,1)S(1)}, u32[]{:S(2)}, u32[]{:S(2)}) collective-permute-start(bf16[1024,1024]{1,0:T(8,128)(2,1)} %maximum_select_fusion.1.refs_2_.a), channel_id=1, source_target_pairs={{0,4},{4,0},{8,12},{12,8},{16,20},{20,16},{24,28},{28,24},{1,5},{5... | collective-permute-start | bytes 6291464 | tf_op jit(solution)/shard_map/ppermute | solution.py:1012
  626.4 24.7 %collective-permute-start.22 = (bf16[512,2048]{1,0:T(8,128)(2,1)}, bf16[512,2048]{1,0:T(8,128)(2,1)S(1)}, u32[]{:S(2)}, u32[]{:S(2)}) collective-permute-start(bf16[512,2048]{1,0:T(8,128)(2,1)} %maximum_select_fusion.refs_1_.a), channel_id=1, source_target_pairs={{0,4},{4,0},{8,12},{12,8},{16,20},{20,16},{24,28},{28,24},{1,5},{5... | collective-permute-start | bytes 6291464 | tf_op jit(solution)/shard_map/ppermute | solution.py:1012
  (99 other events, 593.3 us)
Sparse Core Ops, SparseCore 0:
  92.1 55.8 all-gather.3
  178.7 37.1 all-gather.5
  322.2 53.6 reduce-scatter.4
  379.0 52.6 reduce-scatter.6
  434.8 51.3 reduce-scatter.10
  530.5 74.7 reduce-scatter.8
  626.4 43.2 all-gather.7

commit v5 on v4

--- a/solution.py
+++ b/solution.py
@@ -1055,10 +1055,6 @@
     far_parts = delayed(far_parts, (hidden_got, w_dt_far, par_far))
     far_parts = delayed(far_parts, (hidden_got, w_dt_far, par_far))
     far_both = lax.all_gather(far_parts, "batch", axis=0, tiled=True).reshape(batches, 2, piece, channels)
-    out_piece = channels // batches
-    w_out_part = across(
-        lax.dynamic_slice_in_dim(w_out, lot * out_piece + nothing(normed), out_piece, 0), far_bit
-    )
     up_got = others(up_sent)
     upstream = jnp.concatenate([out_grad, up_got], axis=0)
     active = (jnp.arange(channels) // HEAD_DIM < width * heads_here // (heads_here * stacks)).astype(F32)
@@ -1090,6 +1086,10 @@
 
     inner_own = project(normed, w_x, BF16, (bc,))
     gate_own = project(normed, w_z, BF16, (inner_own,))
+    out_piece = channels // batches
+    w_out_part = across(
+        lax.dynamic_slice_in_dim(w_out, lot * out_piece + nothing(gate_own), out_piece, 0), far_bit
+    )
     forward_own = scan_forward(per_block, info, inner_own, gate_own, bc, bct, hs2[0], par2[0], (up_got,))
     dn_own = project_back(upstream, w_out, forward_own[2], ())
     w_x_far, w_z_far = (far_both, 0), (far_both, 1)

time: 710 us -> 704 us (level)
    ppermute x15, waiting for transfers between devices: 119 us -> 111 us  [across(): return lax.ppermute(v, 'head', [(i, i ^ bit) for i in range(stacks)])]
  transfers between devices with their start and end apart: 30 -> 30, of which waited for: 15 -> 15; matrix products, arithmetic and copies ran while one was open for 11% -> 11% of each run, Pallas kernels for 37% -> 38%
where the time goes in v5:
time: 704 us; the launch traced here: 692 us
  Pallas kernels  308 us (44%)
  waiting for transfers between devices  183 us (26%)
  local copies, waits for them, and re-layouts  105 us (15%)
  other arithmetic  39 us (6%)
  starting transfers between devices  37.4 us (5%)
  between operations  19.1 us (3%)
    ppermute x15, waiting for transfers between devices, across(): return lax.ppermute(v, 'head', [(i, i ^ bit) for i in range(stacks)])  111 us
    pallas_call x6, Pallas kernels, call(): pl.pallas_call(kernel, grid_spec=pltpu.PrefetchScalarGridSpec(num_scalar_...  110 us
    unnamed x188, local copies, waits for them, and re-layouts  58.1 us
    ppermute x8, waiting for transfers between devices, planar(): return lax.ppermute(v, 'batch', [(i, i ^ bit) for i in range(batches)])  46.2 us
    pallas_call x4, Pallas kernels, grad_half(): pl.pallas_call(ignore(kernel, 1 + len(operands), len(later)), grid_spec=p...  34.1 us
    pallas_call x4, Pallas kernels, project(): pl.pallas_call(ignore(kernel, 2, len(later)), grid=(columns // wide,), in...  32.2 us
    ppermute x15, starting transfers between devices, across(): return lax.ppermute(v, 'head', [(i, i ^ bit) for i in range(stacks)])  29.8 us
    pallas_call x2, Pallas kernels, rows_back(): pl.pallas_call(ignore(kernel, 2 * count + 1, len(later)), grid=(columns /...  29.7 us
  transfers between devices with their start and end apart: 30, of which 15 were waited for; matrix products, arithmetic and copies ran while one was open for 11% of the time, Pallas kernels for 38%

profile of v5, /device:TPU:0, one launch (start us, length us, event | category | flops | bytes accessed | tf_op | source)
XLA Modules:
  0.0 691.8 jit_solution(18259846965388190241)
XLA Ops:
  19.0 70.4 %collective-permute-done.2 = bf16[16,2048]{0,1:T(8,128)(2,1)S(1)} collective-permute-done((bf16[16,2048]{0,1:T(8,128)(2,1)S(1)}, bf16[16,2048]{0,1:T(8,128)(2,1)S(1)}, u32[]{:S(2)}, u32[]{:S(2)}) %collective-permute-start.2) | collective-permute-done | bytes 65568 | tf_op jit(solution)/shard_map/ppermute | solution.py:990
  126.2 8.4 %shard_map.302.refs_2_.refs_1_ = bf16[1024,1024]{1,0:T(8,128)(2,1)S(1)} custom-call(bf16[1024,2048]{1,0:T(8,128)(2,1)} %shard_map.298.x.refs_0_.refs_1_.a.refs_10_, bf16[2048,1024]{1,0:T(8,128)(2,1)} %refs_5_.3, bf16[1024,1024]{1,0:T(8,128)(2,1)S(1)} %shard_map.301.refs_2_.refs_1_), custom_call_target="tpu_custom_call" | custom-call | flops 60000000 | bytes 1000 | tf_op jit(solution)/shard_map/pallas_call | solution.py:437
  148.4 19.1 %shard_map.303 = (bf16[1024,1024]{1,0:T(8,128)(2,1)S(1)}, bf16[1024,1024]{1,0:T(8,128)(2,1)}, bf16[1024,1024]{1,0:T(8,128)(2,1)}, bf16[512,1024]{1,0:T(8,128)(2,1)S(1)}, f32[1024,128]{1,0:T(8,128)S(1)}) custom-call(s32[5]{0:T(128)S(1)} %pad_add_fusion.info.refs_0_, bf16[1024,1024]{1,0:T(8,128)(2,1)} %copy-done.10, bf16[1024,1024]{1,0:T(8,128)(2,1)} %copy-done.22, ...), custom_call_target="tpu_custom_call" | custom-call | flops 200000000 | bytes 1000 | tf_op jit(solution)/shard_map/pallas_call | solution.py:406
  177.7 8.0 %shard_map.306 = (bf16[1024,1024]{1,0:T(8,128)(2,1)S(1)}, f32[1024,128]{1,0:T(8,128)S(1)}) custom-call(bf16[1024,2048]{1,0:T(8,128)(2,1)} %copy-done.70, bf16[1024,2048]{1,0:T(8,128)(2,1)} %refs_2_.3, bf16[1024,1024]{1,0:T(8,128)(2,1)S(1)} %copy-done.2), custom_call_target="tpu_custom_call" | custom-call | flops 80000000 | bytes 1000 | tf_op jit(solution)/shard_map/pallas_call | solution.py:495
  189.4 7.7 %shard_map.307.refs_2_.inner.refs_1_ = bf16[1024,1024]{1,0:T(8,128)(2,1)S(1)} custom-call(bf16[1024,2048]{1,0:T(8,128)(2,1)} %shard_map.298.x.refs_0_.refs_1_.a.refs_10_, bf16[8,2,256,1024]{3,2,1,0:T(8,128)(2,1)} %bitcast.106, bf16[1024,1024]{1,0:T(8,128)(2,1)S(1)} %copy-done.35), custom_call_target="tpu_custom_call" | custom-call | flops 60000000 | bytes 1000 | tf_op jit(solution)/shard_map/pallas_call | solution.py:437
  197.1 8.5 %shard_map.308.gate.refs_1_ = bf16[1024,1024]{1,0:T(8,128)(2,1)S(1)} custom-call(bf16[1024,2048]{1,0:T(8,128)(2,1)} %shard_map.298.x.refs_0_.refs_1_.a.refs_10_, bf16[8,2,256,1024]{3,2,1,0:T(8,128)(2,1)} %bitcast.107, bf16[1024,1024]{1,0:T(8,128)(2,1)S(1)} %shard_map.307.refs_2_.inner.refs_1_), custom_call_target="tpu_custom_call" | custom-call | flops 60000000 | bytes 1000 | tf_op jit(solution)/shard_map/pallas_call | solution.py:437
  206.9 19.3 %shard_map.309 = (bf16[1024,1024]{1,0:T(8,128)(2,1)S(1)}, bf16[1024,1024]{1,0:T(8,128)(2,1)}, bf16[1024,1024]{1,0:T(8,128)(2,1)}, bf16[512,1024]{1,0:T(8,128)(2,1)S(1)}, f32[1024,128]{1,0:T(8,128)S(1)}) custom-call(s32[5]{0:T(128)S(1)} %pad_add_fusion.info.refs_0_, bf16[1024,1024]{1,0:T(8,128)(2,1)} %copy-done.12, bf16[1024,1024]{1,0:T(8,128)(2,1)} %copy-done.23, ...), custom_call_target="tpu_custom_call" | custom-call | flops 200000000 | bytes 1000 | tf_op jit(solution)/shard_map/pallas_call | solution.py:406
  230.4 7.9 %shard_map.311 = (bf16[1024,1024]{1,0:T(8,128)(2,1)S(1)}, f32[1024,128]{1,0:T(8,128)S(1)}) custom-call(bf16[1024,2048]{1,0:T(8,128)(2,1)} %copy-done.70, bf16[1024,2048]{1,0:T(8,128)(2,1)} %all-gather.6.cloned.1.call-done.b.refs_3_, bf16[1024,1024]{1,0:T(8,128)(2,1)S(1)} %copy-done.3), custom_call_target="tpu_custom_call" | custom-call | flops 80000000 | bytes 1000 | tf_op jit(solution)/shard_map/pallas_call | solution.py:495
  251.4 8.8 %shard_map.313.refs_5_ = bf16[4,2,128,2048]{3,2,1,0:T(8,128)(2,1)} custom-call(s32[1]{0:T(128)} %bitcast.20.refs_0_, bf16[1024,1024]{1,0:T(8,128)(2,1)S(1)} %copy-done.2, bf16[1024,1024]{1,0:T(8,128)(2,1)S(1)} %copy-done.4, bf16[1024,2048]{1,0:T(8,128)(2,1)} %copy-done.70, f32[8,1024]{1,0:T(8,128)S(1)} %maximum_maximum_fusion.refs_4_.refs_3_.refs_5_, ...), custom_call_target="tpu_custom_call" | custom-call | flops 70000000 | bytes 1000 | tf_op jit(solution)/shard_map/pallas_call | solution.py:760
  280.0 9.8 %shard_map.316.refs_4_ = bf16[4,2,128,2048]{3,2,1,0:T(8,128)(2,1)} custom-call(s32[1]{0:T(128)} %bitcast.24.refs_0_.info, bf16[1024,1024]{1,0:T(8,128)(2,1)S(1)} %copy-done.2, bf16[1024,1024]{1,0:T(8,128)(2,1)S(1)} %copy-done.5, bf16[1024,2048]{1,0:T(8,128)(2,1)} %copy-done.70, bf16[4,2,128,2048]{3,2,1,0:T(8,128)(2,1)} %copy-done.73, ...), custom_call_target="tpu_custom_call" | custom-call | flops 70000000 | bytes 1000 | tf_op jit(solution)/shard_map/pallas_call | solution.py:760
  306.7 8.1 %shard_map.319.refs_9_ = bf16[4,2,256,1024]{3,2,1,0:T(8,128)(2,1)} custom-call(s32[1]{0:T(128)} %bitcast.24.refs_0_.info, bf16[1024,2048]{1,0:T(8,128)(2,1)} %shard_map.298.x.refs_0_.refs_1_.a.refs_10_, bf16[1024,1024]{1,0:T(8,128)(2,1)S(1)} %copy-done.7, bf16[1024,1024]{1,0:T(8,128)(2,1)S(1)} %get-tuple-element.66.refs_3_.refs_1_, ...), custom_call_target="tpu_custom_call" | custom-call | flops 70000000 | bytes 1000 | tf_op jit(solution)/shard_map/pallas_call | solution.py:760
  317.6 33.0 %shard_map.320 = (bf16[1024,1024]{1,0:T(8,128)(2,1)S(1)}, f32[1024,256]{1,0:T(8,128)S(1)}, f32[8,1024]{1,0:T(8,128)S(1)}, f32[64,1024]{1,0:T(8,128)S(1)}) custom-call(s32[5]{0:T(128)S(1)} %pad_add_fusion.info.refs_0_, bf16[1024,1024]{1,0:T(8,128)(2,1)} %copy-done.12, bf16[1024,1024]{1,0:T(8,128)(2,1)} %copy-done.43, bf16[1024,1024]{1,0:T(8,128)(2,1)} %copy-done.45, ...), custom_call_target="tpu_custom_call" | custom-call | flops 360000000 | bytes 1000 | tf_op jit(solution)/shard_map/pallas_call | solution.py:406
  350.6 10.4 %shard_map.321.refs_9_ = bf16[8,256,1024]{2,1,0:T(8,128)(2,1)} custom-call(bf16[1024,2048]{1,0:T(8,128)(2,1)} %shard_map.298.x.refs_0_.refs_1_.a.refs_10_, bf16[1024,1024]{1,0:T(8,128)(2,1)S(1)} %get-tuple-element.72.b.refs_3_), custom_call_target="tpu_custom_call" | custom-call | flops 100000000 | bytes 1000 | tf_op jit(solution)/shard_map/pallas_call | solution.py:804
  369.2 33.0 %shard_map.322 = (bf16[1024,1024]{1,0:T(8,128)(2,1)S(1)}, f32[1024,256]{1,0:T(8,128)S(1)}, f32[8,1024]{1,0:T(8,128)S(1)}, f32[64,1024]{1,0:T(8,128)S(1)}) custom-call(s32[5]{0:T(128)S(1)} %pad_add_fusion.info.refs_0_, bf16[1024,1024]{1,0:T(8,128)(2,1)} %copy-done.10, bf16[1024,1024]{1,0:T(8,128)(2,1)} %copy-done.33, bf16[1024,1024]{1,0:T(8,128)(2,1)} %copy-done.44, ...), custom_call_target="tpu_custom_call" | custom-call | flops 360000000 | bytes 1000 | tf_op jit(solution)/shard_map/pallas_call | solution.py:406
  423.3 15.2 %shard_map.325 = (bf16[512,2048]{1,0:T(8,128)(2,1)}, f32[8,2048]{1,0:T(8,128)S(1)}) custom-call(bf16[1024,1024]{1,0:T(8,128)(2,1)} %copy-done.6, bf16[1024,1024]{1,0:T(8,128)(2,1)} %copy-done.11, bf16[1024,1024]{1,0:T(8,128)(2,1)} %copy-done.25, bf16[1024,1024]{1,0:T(8,128)(2,1)} %copy-done.24, bf16[1024,288]{1,0:T(8,128)(2,1)S(1)} %pad_maximum_fusion.3.refs_0_.refs_4_, ...), custom_call_target="tpu_custom_call" | custom-call | flops 150000000 | bytes 1000 | tf_op jit(solution)/shard_map/pallas_call | solution.py:922
  468.4 14.5 %shard_map.326 = (bf16[512,2048]{1,0:T(8,128)(2,1)S(1)}, f32[8,2048]{1,0:T(8,128)S(1)}) custom-call(bf16[1024,1024]{1,0:T(8,128)(2,1)} %copy-done.6, bf16[1024,1024]{1,0:T(8,128)(2,1)} %copy-done.11, bf16[1024,1024]{1,0:T(8,128)(2,1)} %copy-done.25, bf16[1024,1024]{1,0:T(8,128)(2,1)} %copy-done.24, bf16[1024,288]{1,0:T(8,128)(2,1)S(1)} %pad_maximum_fusion.3.refs_0_.refs_4_, ...), custom_call_target="tpu_custom_call" | custom-call | flops 150000000 | bytes 1000 | tf_op jit(solution)/shard_map/pallas_call | solution.py:922
  487.9 11.6 %collective-permute-done.11.refs_0_ = f32[40,1024]{1,0:T(8,128)} collective-permute-done((f32[40,1024]{1,0:T(8,128)}, f32[40,1024]{1,0:T(8,128)}, u32[]{:S(2)}, u32[]{:S(2)}) %collective-permute-start.11) | collective-permute-done | bytes 163872 | tf_op jit(solution)/shard_map/ppermute | solution.py:990
  500.7 9.4 %collective-permute-done.12.refs_4_.refs_1_ = bf16[256,1024]{1,0:T(8,128)(2,1)} collective-permute-done((bf16[256,1024]{1,0:T(8,128)(2,1)}, bf16[256,1024]{1,0:T(8,128)(2,1)}, u32[]{:S(2)}, u32[]{:S(2)}) %collective-permute-start.12) | collective-permute-done | bytes 524320 | tf_op jit(solution)/shard_map/ppermute | solution.py:990
  512.2 10.6 %shard_map.328 = bf16[8,352,1024]{2,1,0:T(8,128)(2,1)} custom-call(bf16[1024,2048]{1,0:T(8,128)(2,1)} %shard_map.298.x.refs_0_.refs_1_.a.refs_10_, bf16[1024,1024]{1,0:T(8,128)(2,1)S(1)} %copy-done.26, bf16[8,96,1024]{2,1,0:T(8,128)(2,1)S(1)} %pad_maximum_fusion.1.refs_2_, bf16[512,2048]{1,0:T(8,128)(2,1)} %collective-permute-done.10.refs_3_, ...), custom_call_target="tpu_custom_call" | custom-call | flops 100000000 | bytes 1000 | tf_op jit(solution)/shard_map/pallas_call | solution.py:804
  529.7 10.1 %collective-permute-done.14 = bf16[128,2048]{1,0:T(8,128)(2,1)} collective-permute-done((bf16[128,2048]{1,0:T(8,128)(2,1)S(1)}, bf16[128,2048]{1,0:T(8,128)(2,1)}, u32[]{:S(2)}, u32[]{:S(2)}) %collective-permute-start.14) | collective-permute-done | bytes 524320 | tf_op jit(solution)/shard_map/ppermute | solution.py:1012
  552.6 28.4 %collective-permute-done.15 = bf16[256,2048]{1,0:T(8,128)(2,1)} collective-permute-done((bf16[256,2048]{1,0:T(8,128)(2,1)S(1)}, bf16[256,2048]{1,0:T(8,128)(2,1)}, u32[]{:S(2)}, u32[]{:S(2)}) %collective-permute-start.15) | collective-permute-done | bytes 1048608 | tf_op jit(solution)/shard_map/ppermute | solution.py:1012
  590.3 9.4 %reduce-scatter.9.cloned.1.call-done.refs_0_ = bf16[352,1024]{1,0:T(8,128)(2,1)} async-done(((bf16[2816,1024]{1,0:T(8,128)(2,1)}), bf16[352,1024]{1,0:T(8,128)(2,1)}) %reduce-scatter.9.cloned.1.call-update) | async-done | bytes 720912 | tf_op jit(solution)/shard_map/reduce_scatter | solution.py:1224
  623.4 7.6 %shard_map.318 = bf16[512,2048]{1,0:T(8,128)(2,1)S(1)} custom-call(bf16[1024,1024]{1,0:T(8,128)(2,1)S(1)} %copy-done.2, bf16[1024,1024]{1,0:T(8,128)(2,1)} %get-tuple-element.56.y.refs_1_.refs_2_, bf16[1024,2048]{1,0:T(8,128)(2,1)} %refs_2_.3, bf16[1024,2048]{1,0:T(8,128)(2,1)} %all-gather.6.cloned.1.call-done.b.refs_3_, ...), custom_call_target="tpu_custom_call" | custom-call | flops 50000000 | bytes 1000 | tf_op jit(solution)/shard_map/pallas_call | solution.py:523
  649.0 15.1 %all-gather.8.cloned.1.call-done = bf16[2816,1024]{1,0:T(8,128)(2,1)} async-done(((bf16[352,1024]{1,0:T(8,128)(2,1)}), bf16[2816,1024]{1,0:T(8,128)(2,1)}) %all-gather.8.cloned.1.call-update) | async-done | bytes 5767184 | tf_op jit(solution)/shard_map/all_gather | solution.py:1242
  (395 shorter events, 288.3 us)
Async XLA Ops:
  7.2 180.6 %all-gather.4.cloned.1.call-start = ((), (), s32[]{:S(2)}) async-start(), calls=%async_computation.4 | async-start | bytes 9437184 | tf_op jit(solution)/shard_map/all_gather | solution.py:1057
  7.2 83.4 %collective-permute-start = (bf16[512,2048]{1,0:T(8,128)(2,1)}, bf16[512,2048]{1,0:T(8,128)(2,1)}, u32[]{:S(2)}, u32[]{:S(2)}) collective-permute-start(bf16[512,2048]{1,0:T(8,128)(2,1)} %refs_0_.3), channel_id=1, source_target_pairs={{0,1},{1,0},{2,3},{3,2},{4,5},{5,4},{6,7},{7,6},{8,9},{9,8},{10,11... | collective-permute-start | bytes 6291464 | tf_op jit(solution)/shard_map/ppermute | solution.py:990
  12.8 77.1 %collective-permute-start.1 = (bf16[512,1024]{1,0:T(8,128)(2,1)}, bf16[512,1024]{1,0:T(8,128)(2,1)S(1)}, u32[]{:S(2)}, u32[]{:S(2)}) collective-permute-start(bf16[512,1024]{1,0:T(8,128)(2,1)} %pad_maximum_fusion.2), channel_id=1, source_target_pairs={{0,2},{1,3},{2,0},{3,1},{4,6},{5,7},{6,4},{7,5},{8,10},{9,11},{10,... | collective-permute-start | bytes 3145736 | tf_op jit(solution)/shard_map/ppermute | solution.py:990
  15.7 73.8 %collective-permute-start.2 = (bf16[16,2048]{0,1:T(8,128)(2,1)S(1)}, bf16[16,2048]{0,1:T(8,128)(2,1)S(1)}, u32[]{:S(2)}, u32[]{:S(2)}) collective-permute-start(bf16[16,2048]{0,1:T(8,128)(2,1)S(1)} %bitcast.121), channel_id=1, source_target_pairs={{0,2},{1,3},{2,0},{3,1},{4,6},{5,7},{6,4},{7,5},{8,10},{9,11},{10,... | collective-permute-start | bytes 196616 | tf_op jit(solution)/shard_map/ppermute | solution.py:990
  16.4 73.4 %collective-permute-start.3 = (f32[8,1024]{1,0:T(8,128)S(1)}, f32[8,1024]{1,0:T(8,128)S(1)}, u32[]{:S(2)}, u32[]{:S(2)}) collective-permute-start(f32[8,1024]{1,0:T(8,128)S(1)} %concatenate.104), channel_id=1, source_target_pairs={{0,2},{1,3},{2,0},{3,1},{4,6},{5,7},{6,4},{7,5},{8,10},{9,11},{10,... | collective-permute-start | bytes 98312 | tf_op jit(solution)/shard_map/ppermute | solution.py:990
  92.0 136.8 %all-gather.6.cloned.1.call-start = ((), (), s32[]{:S(2)}) async-start(), calls=%async_computation.5 | async-start | bytes 4718592 | tf_op jit(solution)/shard_map/all_gather | solution.py:1096
  96.4 52.1 %collective-permute-start.4 = (bf16[512,2048]{1,0:T(8,128)(2,1)}, bf16[512,2048]{1,0:T(8,128)(2,1)}, u32[]{:S(2)}, u32[]{:S(2)}) collective-permute-start(bf16[512,2048]{1,0:T(8,128)(2,1)} %shard_map.297.refs_6_), channel_id=1, source_target_pairs={{0,1},{1,0},{2,3},{3,2},{4,5},{5,4},{6,7},{7,6},{8,9},{9,8},{10,11... | collective-permute-start | bytes 6291464 | tf_op jit(solution)/shard_map/ppermute | solution.py:990
  138.6 30.7 %collective-permute-start.5 = (bf16[128,2048]{1,0:T(8,128)(2,1)}, bf16[128,2048]{1,0:T(8,128)(2,1)}, u32[]{:S(2)}, u32[]{:S(2)}) collective-permute-start(bf16[128,2048]{1,0:T(8,128)(2,1)} %constant_dynamic-slice_fusion), channel_id=1, source_target_pairs={{0,2},{1,3},{2,0},{3,1},{4,6},{5,7},{6,4},{7,5},{8,10},{9,11},{10,... | collective-permute-start | bytes 1572872 | tf_op jit(solution)/shard_map/ppermute | solution.py:990
  171.6 245.1 %reduce-scatter.5.cloned.1.call-start = ((), (), s32[]{:S(2)}) async-start(), calls=%async_computation.6 | async-start | bytes 5242880 | tf_op jit(solution)/shard_map/reduce_scatter | solution.py:1141
  260.2 17.8 %collective-permute-start.7 = (bf16[4,2,128,2048]{3,2,1,0:T(8,128)(2,1)}, bf16[4,2,128,2048]{3,2,1,0:T(8,128)(2,1)S(1)}, u32[]{:S(2)}, u32[]{:S(2)}) collective-permute-start(bf16[4,2,128,2048]{3,2,1,0:T(8,128)(2,1)} %shard_map.313.refs_5_), channel_id=1, source_target_pairs={{0,4},{4,0},{8,12},{12,8},{16,20},{20,16},{24,28},{28,24},{1,5},{5... | collective-permute-start | bytes 12582920 | tf_op jit(solution)/shard_map/ppermute | solution.py:1012
  314.8 127.6 %reduce-scatter.7.cloned.1.call-start = ((), (), s32[]{:S(2)}) async-start(), calls=%async_computation.7 | async-start | bytes 5242880 | tf_op jit(solution)/shard_map/reduce_scatter | solution.py:1141
  315.4 232.5 %reduce-scatter.11.cloned.1.call-start = ((), (), s32[]{:S(2)}) async-start(), calls=%async_computation.9 | async-start | bytes 4718592 | tf_op jit(solution)/shard_map/reduce_scatter | solution.py:1173
  361.1 238.6 %reduce-scatter.9.cloned.1.call-start = ((), (), s32[]{:S(2)}) async-start(), calls=%async_computation.8 | async-start | bytes 6488064 | tf_op jit(solution)/shard_map/reduce_scatter | solution.py:1224
  361.2 55.5 %collective-permute-start.8 = (bf16[512,2048]{1,0:T(8,128)(2,1)}, bf16[512,2048]{1,0:T(8,128)(2,1)}, u32[]{:S(2)}, u32[]{:S(2)}) collective-permute-start(bf16[512,2048]{1,0:T(8,128)(2,1)} %copy-done.37), channel_id=1, source_target_pairs={{0,1},{1,0},{2,3},{3,2},{4,5},{5,4},{6,7},{7,6},{8,9},{9,8},{10,11... | collective-permute-start | bytes 6291464 | tf_op jit(solution)/shard_map/ppermute | solution.py:990
  438.5 73.7 %collective-permute-start.10 = (bf16[512,2048]{1,0:T(8,128)(2,1)}, bf16[512,2048]{1,0:T(8,128)(2,1)}, u32[]{:S(2)}, u32[]{:S(2)}) collective-permute-start(bf16[512,2048]{1,0:T(8,128)(2,1)} %get-tuple-element.81), channel_id=1, source_target_pairs={{0,1},{1,0},{2,3},{3,2},{4,5},{5,4},{6,7},{7,6},{8,9},{9,8},{10,11... | collective-permute-start | bytes 6291464 | tf_op jit(solution)/shard_map/ppermute | solution.py:990
  444.4 56.3 %collective-permute-start.13 = (bf16[128,2048]{1,0:T(8,128)(2,1)}, bf16[128,2048]{1,0:T(8,128)(2,1)S(1)}, u32[]{:S(2)}, u32[]{:S(2)}) collective-permute-start(bf16[128,2048]{1,0:T(8,128)(2,1)} %dynamic-slice_bitcast_fusion), channel_id=1, source_target_pairs={{0,2},{1,3},{2,0},{3,1},{4,6},{5,7},{6,4},{7,5},{8,10},{9,11},{10,... | collective-permute-start | bytes 1572872 | tf_op jit(solution)/shard_map/ppermute | solution.py:990
  461.3 38.2 %collective-permute-start.11 = (f32[40,1024]{1,0:T(8,128)}, f32[40,1024]{1,0:T(8,128)}, u32[]{:S(2)}, u32[]{:S(2)}) collective-permute-start(f32[40,1024]{1,0:T(8,128)} %concatenate.122), channel_id=1, source_target_pairs={{0,2},{1,3},{2,0},{3,1},{4,6},{5,7},{6,4},{7,5},{8,10},{9,11},{10,... | collective-permute-start | bytes 491528 | tf_op jit(solution)/shard_map/ppermute | solution.py:990
  463.2 46.9 %collective-permute-start.12 = (bf16[256,1024]{1,0:T(8,128)(2,1)}, bf16[256,1024]{1,0:T(8,128)(2,1)}, u32[]{:S(2)}, u32[]{:S(2)}) collective-permute-start(bf16[256,1024]{1,0:T(8,128)(2,1)} %dynamic-slice_bitcast_fusion.1), channel_id=1, source_target_pairs={{0,2},{1,3},{2,0},{3,1},{4,6},{5,7},{6,4},{7,5},{8,10},{9,11},{10,... | collective-permute-start | bytes 1572872 | tf_op jit(solution)/shard_map/ppermute | solution.py:990
  522.9 141.2 %all-gather.8.cloned.1.call-start = ((), (), s32[]{:S(2)}) async-start(), calls=%async_computation.10 | async-start | bytes 6488064 | tf_op jit(solution)/shard_map/all_gather | solution.py:1242
  541.8 39.1 %collective-permute-start.15 = (bf16[256,2048]{1,0:T(8,128)(2,1)S(1)}, bf16[256,2048]{1,0:T(8,128)(2,1)}, u32[]{:S(2)}, u32[]{:S(2)}) collective-permute-start(bf16[256,2048]{1,0:T(8,128)(2,1)S(1)} %maximum_select_fusion.2.refs_1_), channel_id=1, source_target_pairs={{0,16},{4,20},{8,24},{12,28},{16,0},{20,4},{24,8},{28,12},{1,17},{... | collective-permute-start | bytes 3145736 | tf_op jit(solution)/shard_map/ppermute | solution.py:1012
  546.5 39.1 %collective-permute-start.17 = (bf16[512,1024]{1,0:T(8,128)(2,1)}, bf16[512,1024]{1,0:T(8,128)(2,1)}, u32[]{:S(2)}, u32[]{:S(2)}) collective-permute-start(bf16[512,1024]{1,0:T(8,128)(2,1)} %maximum_select_fusion.3.refs_2_), channel_id=1, source_target_pairs={{0,8},{4,12},{8,0},{12,4},{16,24},{20,28},{24,16},{28,20},{1,9},{5... | collective-permute-start | bytes 3145736 | tf_op jit(solution)/shard_map/ppermute | solution.py:1012
  549.9 62.7 %collective-permute-start.18 = (bf16[256,1024]{1,0:T(8,128)(2,1)}, bf16[256,1024]{1,0:T(8,128)(2,1)}, u32[]{:S(2)}, u32[]{:S(2)}) collective-permute-start(bf16[256,1024]{1,0:T(8,128)(2,1)} %shard_map.333), channel_id=1, source_target_pairs={{0,2},{1,3},{2,0},{3,1},{4,6},{5,7},{6,4},{7,5},{8,10},{9,11},{10,... | collective-permute-start | bytes 1572872 | tf_op jit(solution)/shard_map/ppermute | solution.py:990
  620.7 20.2 %collective-permute-start.21 = (bf16[1024,1024]{1,0:T(8,128)(2,1)}, bf16[1024,1024]{1,0:T(8,128)(2,1)S(1)}, u32[]{:S(2)}, u32[]{:S(2)}) collective-permute-start(bf16[1024,1024]{1,0:T(8,128)(2,1)} %maximum_select_fusion.1.refs_2_.a), channel_id=1, source_target_pairs={{0,4},{4,0},{8,12},{12,8},{16,20},{20,16},{24,28},{28,24},{1,5},{5... | collective-permute-start | bytes 6291464 | tf_op jit(solution)/shard_map/ppermute | solution.py:1012
  620.7 24.6 %collective-permute-start.22 = (bf16[512,2048]{1,0:T(8,128)(2,1)}, bf16[512,2048]{1,0:T(8,128)(2,1)S(1)}, u32[]{:S(2)}, u32[]{:S(2)}) collective-permute-start(bf16[512,2048]{1,0:T(8,128)(2,1)} %maximum_select_fusion.refs_1_.a), channel_id=1, source_target_pairs={{0,4},{4,0},{8,12},{12,8},{16,20},{20,16},{24,28},{28,24},{1,5},{5... | collective-permute-start | bytes 6291464 | tf_op jit(solution)/shard_map/ppermute | solution.py:1012
  (99 other events, 666.7 us)
Sparse Core Ops, SparseCore 0:
  92.1 55.8 all-gather.3
  171.7 38.4 all-gather.5
  314.9 55.2 reduce-scatter.4
  373.3 52.6 reduce-scatter.6
  429.2 51.3 reduce-scatter.10
  523.0 76.6 reduce-scatter.8
  620.8 43.2 all-gather.7
